TPU v7x, 256 devices: a whole 4x4x8 slice. The times are simulated.
256 devices in a mesh: freq: 32 (over z_lo, y, x), tile: 8 (over z_hi, core).
Axes of the slice: x: 4, y: 4, z: 8 (z_hi: 4, z_lo: 2; z = z_hi * 2 + z_lo), core: 2. Of those that a mesh axis runs over, the one named last changes fastest.
Arguments:
- response: bfloat16 [2, 128, 2048, 2048], P(None, 'freq', 'tile'), may hold values from -0.09375 to 0.09375
- direct: float32 [2, 128, 8, 2048], P(None, 'freq', None, 'tile'), may hold values from -6 to 6
- onset: int32 [8, 2048], P(None, 'tile'), may hold values from 32 to 223
Outputs:
- minus_spectrum: float32 [2, 128, 8, 2048], P(None, 'freq', None, 'tile')
- plus_spectrum: float32 [2, 128, 8, 2048], P(None, 'freq', None, 'tile')
Inputs may be any that keep to these rules, and one draw needn't show every extreme that they name: onset sample of the direct arrival for each focal point and position.
All inputs are finite; a program needn't handle non-finite values.
Results may differ from a plain program's by a relative error of at most 0.0029.
Values may be sent and summed in bfloat16 or wider, within the bound.
No kernel may reach another device: no remote copies, remote signals or barrier semaphores. Data moves between devices by JAX's collectives and lax.ppermute only.
A program may use at most 64 MiB of HBM per device.

v0:
```python
import math

import jax
import jax.numpy as jnp
from jax import lax
from jax.sharding import PartitionSpec as P

NT = 512
ITERS = 2
FIRST_BIN = 16


def tables(bins, times):
    phase = bins[:, None] * times[None, :] % NT
    angle = 2.0 * math.pi / NT * phase.astype(jnp.float32)
    return (jnp.cos(angle), jnp.sin(angle))


def window_mask(onset, times):
    shifted = jnp.where(times >= NT // 2, times - NT, times)
    keep = (shifted[None, :, None] > -onset[:, None, :]) & (
        shifted[None, :, None] < onset[:, None, :]
    )
    return keep.astype(jnp.float32)


def roundtrip(spectrum, onset):
    scale = math.sqrt(2.0 / NT)
    highest = lax.Precision.HIGHEST
    fpd = spectrum.shape[1]
    groups = lax.axis_size("freq")
    own = lax.axis_index("freq")
    span = NT // groups
    own_times = own * span + jnp.arange(span, dtype=jnp.int32)
    own_bins = FIRST_BIN + own * fpd + jnp.arange(fpd, dtype=jnp.int32)
    piece = lax.all_gather(spectrum, "freq", axis=1, tiled=True)
    bins = jnp.int32(0) + FIRST_BIN + jnp.arange(piece.shape[1], dtype=jnp.int32)
    cosine, sine = tables(bins, own_times)
    term = jnp.einsum("jt,jpn->ptn", cosine, piece[0], precision=highest) - jnp.einsum(
        "jt,jpn->ptn", sine, piece[1], precision=highest
    )
    signal = scale * term
    signal = signal * window_mask(onset, own_times)
    piece = lax.all_gather(signal, "freq", axis=1, tiled=True)
    times = jnp.arange(piece.shape[1], dtype=jnp.int32)
    cosine, sine = tables(own_bins, times)
    real = jnp.einsum("jt,ptn->jpn", cosine, piece, precision=highest)
    imag = jnp.einsum("jt,ptn->jpn", sine, piece, precision=highest)
    return scale * jnp.stack([real, -imag])


def on_device(response, direct, onset):
    focal = direct.shape[2]
    plus = direct
    minus = direct
    for step in range(ITERS):
        columns = lax.all_gather(plus.astype(jnp.bfloat16), "tile", axis=3, tiled=True)
        stacked = jnp.concatenate([columns[0], columns[1]], axis=1)
        first = jnp.einsum("fqn,frn->fqr", stacked, response[0], preferred_element_type=jnp.float32)
        second = jnp.einsum(
            "fqn,frn->fqr", stacked, response[1], preferred_element_type=jnp.float32
        )
        upgoing = jnp.stack(
            [first[:, :focal] - second[:, focal:], first[:, focal:] + second[:, :focal]]
        )
        minus = roundtrip(upgoing, onset)
        rounded = minus.astype(jnp.bfloat16)
        stacked = jnp.concatenate([rounded[0], rounded[1]], axis=1)
        first = jnp.einsum("fqr,frs->fqs", stacked, response[0], preferred_element_type=jnp.float32)
        second = jnp.einsum(
            "fqr,frs->fqs", stacked, response[1], preferred_element_type=jnp.float32
        )
        partial_sources = jnp.stack(
            [first[:, :focal] + second[:, focal:], first[:, focal:] - second[:, :focal]]
        )
        sources = lax.psum_scatter(partial_sources, "tile", scatter_dimension=3, tiled=True)
        plus = direct + roundtrip(sources, onset)
    return (minus, plus)


def solution(mesh):
    return jax.shard_map(
        on_device,
        mesh=mesh,
        in_specs=(P(None, "freq", "tile", None), P(None, "freq", None, "tile"), P(None, "tile")),
        out_specs=(P(None, "freq", None, "tile"), P(None, "freq", None, "tile")),
        check_vma=False,
    )
```

profile of v0, /device:TPU:1, one launch (start us, length us, event | category | flops | bytes accessed | tf_op | source)
XLA Modules:
  0.0 1440.5 jit_solution(1283074996597032080)
XLA Ops:
  8.1 19.6 %all_gather.30 = bf16[2,4,8,2048]{3,2,1,0:T(8,128)(2,1)S(1)} all-gather(bf16[2,4,8,256]{3,2,1,0:T(8,128)(2,1)S(1)} %convert_element_type.13), channel_id=1, replica_groups=mesh['freq'=32,'tile'=8] {'tile'}, dimensions={3}, use_global_device_ids=true | all-gather | bytes 294912 | tf_op jit(solution)/shard_map/all_gather | solution.py:57
  27.7 3.4 fusion.6
  31.1 3.4 fusion.14
  35.2 134.1 %all-gather.9.cloned.1.call-done = f32[2,128,8,256]{3,2,1,0:T(8,128)} async-done(((f32[2,4,8,256]{3,2,1,0:T(8,128)}), f32[2,128,8,256]{3,2,1,0:T(8,128)}) %all-gather.9.cloned.1.call-update) | async-done | bytes 2097168 | tf_op jit(solution)/shard_map/all_gather | solution.py:36
  173.7 160.8 %all-gather.11.cloned.1.call-done = f32[8,512,256]{2,1,0:T(8,128)} async-done(((f32[8,16,256]{2,1,0:T(8,128)}), f32[8,512,256]{2,1,0:T(8,128)}) %all-gather.11.cloned.1.call-update) | async-done | bytes 4194320 | tf_op jit(solution)/shard_map/all_gather | solution.py:44
  334.5 4.5 fusion.39
  341.3 2.8 fusion.4
  344.2 2.8 fusion.12
  348.0 55.8 %reduce-scatter.3.cloned.1.call-done = f32[2,4,8,256]{3,2,1,0:T(8,128)} async-done(((f32[2,4,8,2048]{3,2,1,0:T(8,128)}), f32[2,4,8,256]{3,2,1,0:T(8,128)}) %reduce-scatter.3.cloned.1.call-update) | async-done | bytes 65552 | tf_op jit(solution)/shard_map/reduce_scatter | solution.py:76
  404.1 136.5 %all-gather.13.cloned.1.call-done = f32[2,128,8,256]{3,2,1,0:T(8,128)} async-done(((f32[2,4,8,256]{3,2,1,0:T(8,128)}), f32[2,128,8,256]{3,2,1,0:T(8,128)}) %all-gather.13.cloned.1.call-update) | async-done | bytes 2097168 | tf_op jit(solution)/shard_map/all_gather | solution.py:36
  545.0 160.8 %all-gather.15.cloned.1.call-done = f32[8,512,256]{2,1,0:T(8,128)} async-done(((f32[8,16,256]{2,1,0:T(8,128)}), f32[8,512,256]{2,1,0:T(8,128)}) %all-gather.15.cloned.1.call-update) | async-done | bytes 4194320 | tf_op jit(solution)/shard_map/all_gather | solution.py:44
  705.8 4.5 fusion.38
  712.6 37.6 %all_gather.35 = bf16[2,4,8,2048]{3,1,2,0:T(4,128)(2,1)S(1)} all-gather(bf16[2,4,8,256]{3,1,2,0:T(4,128)(2,1)S(1)} %fusion.60), channel_id=1, replica_groups=mesh['freq'=32,'tile'=8] {'tile'}, dimensions={3}, use_global_device_ids=true | all-gather | bytes 294912 | tf_op jit(solution)/shard_map/all_gather | solution.py:57
  750.4 3.4 fusion.2
  753.8 3.4 fusion.10
  758.0 131.8 %all-gather.17.cloned.1.call-done = f32[2,128,8,256]{3,2,1,0:T(8,128)} async-done(((f32[2,4,8,256]{3,2,1,0:T(8,128)}), f32[2,128,8,256]{3,2,1,0:T(8,128)}) %all-gather.17.cloned.1.call-update) | async-done | bytes 2097168 | tf_op jit(solution)/shard_map/all_gather | solution.py:36
  894.4 160.6 %all-gather.19.cloned.1.call-done = f32[8,512,256]{2,1,0:T(8,128)} async-done(((f32[8,16,256]{2,1,0:T(8,128)}), f32[8,512,256]{2,1,0:T(8,128)}) %all-gather.19.cloned.1.call-update) | async-done | bytes 4194320 | tf_op jit(solution)/shard_map/all_gather | solution.py:44
  1054.9 4.5 fusion.37
  1061.8 2.8 fusion
  1064.6 2.8 fusion.8
  1068.4 55.8 %reduce-scatter.5.cloned.1.call-done = f32[2,4,8,256]{3,2,1,0:T(8,128)} async-done(((f32[2,4,8,2048]{3,2,1,0:T(8,128)}), f32[2,4,8,256]{3,2,1,0:T(8,128)}) %reduce-scatter.5.cloned.1.call-update) | async-done | bytes 65552 | tf_op jit(solution)/shard_map/reduce_scatter | solution.py:76
  1124.6 136.5 %all-gather.21.cloned.1.call-done = f32[2,128,8,256]{3,2,1,0:T(8,128)} async-done(((f32[2,4,8,256]{3,2,1,0:T(8,128)}), f32[2,128,8,256]{3,2,1,0:T(8,128)}) %all-gather.21.cloned.1.call-update) | async-done | bytes 2097168 | tf_op jit(solution)/shard_map/all_gather | solution.py:36
  1266.0 160.2 %all-gather.23.cloned.1.call-done = f32[8,512,256]{2,1,0:T(8,128)} async-done(((f32[8,16,256]{2,1,0:T(8,128)}), f32[8,512,256]{2,1,0:T(8,128)}) %all-gather.23.cloned.1.call-update) | async-done | bytes 4194320 | tf_op jit(solution)/shard_map/all_gather | solution.py:44
  1426.2 4.5 fusion.36
  (74 shorter events, 33.0 us)
Async XLA Ops:
  7.2 162.2 %all-gather.9.cloned.1.call-start = ((), (), s32[]{:S(2)}) async-start(), calls=%async_computation.2 | async-start | bytes 2162688 | tf_op jit(solution)/shard_map/all_gather | solution.py:36
  27.7 7.5 copy-start.5
  35.1 299.4 %all-gather.11.cloned.1.call-start = ((), (), s32[]{:S(2)}) async-start(), calls=%async_computation.3 | async-start | bytes 4325376 | tf_op jit(solution)/shard_map/all_gather | solution.py:44
  173.7 230.2 %reduce-scatter.3.cloned.1.call-start = ((), (), s32[]{:S(2)}) async-start(), calls=%async_computation.4 | async-start | bytes 589824 | tf_op jit(solution)/shard_map/reduce_scatter | solution.py:76
  334.5 4.5 copy-start
  348.0 192.7 %all-gather.13.cloned.1.call-start = ((), (), s32[]{:S(2)}) async-start(), calls=%async_computation.5 | async-start | bytes 2162688 | tf_op jit(solution)/shard_map/all_gather | solution.py:36
  403.9 301.9 %all-gather.15.cloned.1.call-start = ((), (), s32[]{:S(2)}) async-start(), calls=%async_computation.6 | async-start | bytes 4325376 | tf_op jit(solution)/shard_map/all_gather | solution.py:44
  544.9 167.6 %copy-start.4 = (f32[2,4,8,256]{3,2,1,0:T(8,128)S(1)}, f32[2,4,8,256]{3,2,1,0:T(8,128)}, u32[]{:S(2)}) copy-start(f32[2,4,8,256]{3,2,1,0:T(8,128)} %param.4) | copy-start | bytes 196612
  544.9 344.9 %all-gather.17.cloned.1.call-start = ((), (), s32[]{:S(2)}) async-start(), calls=%async_computation.7 | async-start | bytes 2162688 | tf_op jit(solution)/shard_map/all_gather | solution.py:36
  705.8 4.5 copy-start.2
  757.9 297.0 %all-gather.19.cloned.1.call-start = ((), (), s32[]{:S(2)}) async-start(), calls=%async_computation.8 | async-start | bytes 4325376 | tf_op jit(solution)/shard_map/all_gather | solution.py:44
  894.1 230.2 %reduce-scatter.5.cloned.1.call-start = ((), (), s32[]{:S(2)}) async-start(), calls=%async_computation.9 | async-start | bytes 589824 | tf_op jit(solution)/shard_map/reduce_scatter | solution.py:76
  1054.9 4.5 copy-start.3
  1068.4 192.7 %all-gather.21.cloned.1.call-start = ((), (), s32[]{:S(2)}) async-start(), calls=%async_computation.10 | async-start | bytes 2162688 | tf_op jit(solution)/shard_map/all_gather | solution.py:36
  1124.3 301.9 %all-gather.23.cloned.1.call-start = ((), (), s32[]{:S(2)}) async-start(), calls=%async_computation.11 | async-start | bytes 4325376 | tf_op jit(solution)/shard_map/all_gather | solution.py:44
  1426.2 4.5 copy-start.1
Sparse Core Ops, SparseCore 0:
  35.2 134.0 all-gather.8
  173.8 160.6 all-gather.10
  348.1 55.7 reduce-scatter.2
  405.6 134.9 all-gather.12
  545.0 160.6 all-gather.14
  758.0 131.6 all-gather.16
  894.2 160.6 all-gather.18
  1068.5 55.6 reduce-scatter.4
  1126.0 134.9 all-gather.20
  1265.5 160.6 all-gather.22
where the time goes:
time: 1460 us; the launch traced here: 1440 us
  waiting for transfers between devices  1290 us (88%)
  matrix products  62.4 us (4%)
  blocking collectives  57.2 us (4%)
    all_gather x4, waiting for transfers between devices, roundtrip(): piece = lax.all_gather(signal, 'freq', axis=1, tiled=True)  642 us
    all_gather x4, waiting for transfers between devices, roundtrip(): piece = lax.all_gather(spectrum, 'freq', axis=1, tiled=True)  539 us
    reduce_scatter x2, waiting for transfers between devices, on_device(): lax.psum_scatter(partial_sources, 'tile', scatter_dimension=3, tiled=True)  112 us
    all_gather x2, blocking collectives, on_device(): lax.all_gather(plus.astype(jnp.bfloat16), 'tile', axis=3, tiled=True)  57.2 us
  transfers between devices with their start and end apart: 10, of which 10 were waited for; matrix products, arithmetic and copies ran while one was open for 0% of the time, Pallas kernels for 0%

commit v1 on v0

v1 whole, which is shorter than its diff:
```python
import functools
import math

import jax
import jax.numpy as jnp
import numpy as np
from jax import lax
from jax.experimental import pallas as pl
from jax.experimental.pallas import tpu as pltpu
from jax.sharding import PartitionSpec as P

NT = 512
ITERS = 2
FIRST_BIN = 16
NF = 128
FP = 8
LAGS = 224
LANES = 128
BF16 = jnp.bfloat16
F32 = jnp.float32
VMEM_LIMIT = 24 * 1024 * 1024


def split(table):
    high = table.astype(np.float32).astype(jnp.bfloat16)
    low = (table - high.astype(np.float64)).astype(np.float32).astype(jnp.bfloat16)
    return high, low


def tables():
    bins = FIRST_BIN + np.arange(NF)
    lags = np.arange(LAGS)
    angle = 2.0 * math.pi / NT * ((lags[:, None] * bins[None, :]) % NT)
    weight = np.where(lags == 0, 2.0 / NT, 4.0 / NT)
    inverse, forward = [], []
    for table in (np.cos(angle), np.sin(angle)):
        high, low = split(table)
        inverse.append(np.concatenate([high, high, low], axis=1))
        high, low = split((table * weight[:, None]).T)
        forward.append(np.concatenate([high, high, low], axis=1))
    return np.stack(inverse), np.stack(forward)


def pieces(value):
    high = value.astype(BF16)
    low = (value - high.astype(F32)).astype(BF16)
    return jnp.concatenate([high, low, high], axis=0)


def roundtrip_kernel(summed, copies, place, inverse, forward, onset, blocks, out):
    if summed:
        rows = NF
        spectrum = blocks[:rows, :].astype(F32)
        for tile in range(1, blocks.shape[0] // rows):
            spectrum += blocks[tile * rows : (tile + 1) * rows, :].astype(F32)
    else:
        spectrum = blocks[...]
    signal = jnp.dot(inverse[0], pieces(spectrum), preferred_element_type=F32)
    focal = lax.broadcasted_iota(jnp.int32, onset.shape, 0)
    limit = jnp.sum(jnp.where(focal == place[1], onset[...], 0), axis=0, keepdims=True)
    lag = lax.broadcasted_iota(jnp.int32, signal.shape, 0)
    signal = jnp.where(lag < limit, signal, 0.0)
    result = jnp.dot(forward[0], pieces(signal), preferred_element_type=F32)
    result = result.astype(out.dtype)
    for copy in range(copies):
        out[copy * NF : (copy + 1) * NF, :] = result


def roundtrip(place, inverse, forward, onset, blocks, summed, copies, dtype):
    rows = blocks.shape[0]
    whole = lambda i, place: (0, 0)
    part = lambda i, place: (place[0], 0, 0)
    return pl.pallas_call(
        functools.partial(roundtrip_kernel, summed, copies),
        out_shape=jax.ShapeDtypeStruct((copies * NF, LANES), dtype),
        grid_spec=pltpu.PrefetchScalarGridSpec(
            num_scalar_prefetch=1,
            grid=(1,),
            in_specs=[
                pl.BlockSpec((1,) + inverse.shape[1:], part),
                pl.BlockSpec((1,) + forward.shape[1:], part),
                pl.BlockSpec((FP, LANES), lambda i, place: (0, place[2])),
                pl.BlockSpec((rows, LANES), whole),
            ],
            out_specs=pl.BlockSpec((copies * NF, LANES), whole),
        ),
        compiler_params=pltpu.CompilerParams(vmem_limit_bytes=VMEM_LIMIT),
        name="roundtrip",
    )(place, inverse, forward, onset, blocks)


def forward_kernel(updated, *refs):
    if updated:
        direct, update, response, out, held = refs
    else:
        direct, response, out = refs
    step = pl.program_id(0)
    if updated:

        @pl.when(step == 0)
        def _():
            held[...] = update[...].astype(F32)

    tiles = direct.shape[0]
    columns = []
    for tile in range(tiles):
        for half in range(2):
            both = []
            for part in range(2):
                value = direct[tile, part, step, :, half * LANES : (half + 1) * LANES]
                if updated:
                    start = tile * NF + (half * 2 + part) * 4
                    value = value + held[pl.ds(start + step, FP, stride=16), :]
                both.append(value)
            columns.append(jnp.concatenate(both, axis=0).astype(BF16))
    stacked = jnp.concatenate(columns, axis=1)
    dims = (((1,), (1,)), ((), ()))
    first = lax.dot_general(stacked, response[0, 0], dims, preferred_element_type=F32)
    second = lax.dot_general(stacked, response[1, 0], dims, preferred_element_type=F32)
    parts = (first[:FP] - second[FP:], first[FP:] + second[:FP])
    for half in range(2):
        for part in range(2):
            start = (half * 2 + part) * 4
            out[pl.ds(start + step, FP, stride=16), :] = parts[part][:, half * LANES : (half + 1) * LANES]


def forward_product(direct, update, response):
    bins = response.shape[1]
    updated = update is not None
    in_specs = [pl.BlockSpec(direct.shape, lambda j: (0, 0, 0, 0, 0))]
    args = [direct]
    scratch = []
    if updated:
        in_specs.append(pl.BlockSpec(update.shape, lambda j: (0, 0)))
        args.append(update)
        scratch.append(pltpu.VMEM(update.shape, F32))
    in_specs.append(pl.BlockSpec((2, 1) + response.shape[2:], lambda j: (0, j, 0, 0)))
    return pl.pallas_call(
        functools.partial(forward_kernel, updated),
        out_shape=jax.ShapeDtypeStruct((NF, LANES), F32),
        grid=(bins,),
        in_specs=in_specs,
        out_specs=pl.BlockSpec((NF, LANES), lambda j: (0, 0)),
        scratch_shapes=scratch,
        compiler_params=pltpu.CompilerParams(vmem_limit_bytes=VMEM_LIMIT),
        name="forward_product",
    )(*args, response)


def adjoint_kernel(blocks, response, out, minus, held):
    step = pl.program_id(0)
    rows = []
    for part in range(2):
        halves = []
        for half in range(2):
            start = (half * 2 + part) * 4
            halves.append(blocks[pl.ds(start + step, FP, stride=16), :])
        rows.append(jnp.concatenate(halves, axis=1))
        minus[part, 0] = rows[-1]
    stacked = jnp.concatenate(rows, axis=0).astype(BF16)
    first = jnp.dot(stacked, response[0, 0], preferred_element_type=F32)
    second = jnp.dot(stacked, response[1, 0], preferred_element_type=F32)
    parts = (first[:FP] + second[FP:], first[FP:] - second[:FP])
    tiles = response.shape[3] // (2 * LANES)
    for tile in range(tiles):
        for half in range(2):
            lane = (tile * 2 + half) * LANES
            for part in range(2):
                start = tile * NF + (half * 2 + part) * 4
                held[pl.ds(start + step, FP, stride=16), :] = parts[part][:, lane : lane + LANES]

    @pl.when(step == pl.num_programs(0) - 1)
    def _():
        out[...] = held[...].astype(out.dtype)


def adjoint_product(blocks, response):
    bins, receivers, sources = response.shape[1:]
    rows = NF * sources // (2 * LANES)
    return pl.pallas_call(
        adjoint_kernel,
        out_shape=(
            jax.ShapeDtypeStruct((rows, LANES), BF16),
            jax.ShapeDtypeStruct((2, bins, FP, receivers), F32),
        ),
        grid=(bins,),
        in_specs=[
            pl.BlockSpec((NF, LANES), lambda j: (0, 0)),
            pl.BlockSpec((2, 1) + response.shape[2:], lambda j: (0, j, 0, 0)),
        ],
        out_specs=(
            pl.BlockSpec((rows, LANES), lambda j: (0, 0)),
            pl.BlockSpec((2, 1, FP, receivers), lambda j: (0, j, 0, 0)),
        ),
        scratch_shapes=[pltpu.VMEM((rows, LANES), F32)],
        compiler_params=pltpu.CompilerParams(vmem_limit_bytes=VMEM_LIMIT),
        name="adjoint_product",
    )(blocks, response)


def finish_kernel(direct, blocks, out):
    for bin_ in range(direct.shape[1]):
        for part in range(2):
            for half in range(2):
                lanes = slice(half * LANES, (half + 1) * LANES)
                value = blocks[pl.ds((half * 2 + part) * 4 + bin_, FP, stride=16), :]
                out[part, bin_, :, lanes] = direct[part, bin_, :, lanes] + value


def finish(direct, blocks):
    return pl.pallas_call(
        finish_kernel,
        out_shape=jax.ShapeDtypeStruct(direct.shape, F32),
        name="finish",
    )(direct, blocks)


def exchange(blocks, axes, count):
    shaped = blocks.reshape(count, blocks.shape[0] // count, LANES)
    return lax.all_to_all(shaped, axes, 0, 0, tiled=True).reshape(blocks.shape)


def on_device(response, direct, onset):
    groups = lax.axis_size("freq")
    tiles = lax.axis_size("tile")
    everyone = ("tile", "freq")
    own = lax.axis_index("freq")
    place = jnp.stack([own % 2, own // 4, own // 2 % 2]).astype(jnp.int32)
    inverse, forward = (jnp.asarray(table) for table in tables())
    trip = functools.partial(roundtrip, place, inverse, forward, onset)
    gathered = lax.all_gather(direct, "tile", axis=0)
    update = None
    for step in range(ITERS):
        upgoing = forward_product(gathered, update, response)
        blocks = trip(exchange(upgoing, "freq", groups), False, 1, F32)
        blocks = exchange(blocks, "freq", groups)
        partial, minus = adjoint_product(blocks, response)
        partial = exchange(partial, everyone, groups * tiles)
        if step + 1 < ITERS:
            update = exchange(trip(partial, True, tiles, BF16), everyone, groups * tiles)
        else:
            plus = finish(direct, exchange(trip(partial, True, 1, F32), "freq", groups))
    return (minus, plus)


def solution(mesh):
    return jax.shard_map(
        on_device,
        mesh=mesh,
        in_specs=(P(None, "freq", "tile", None), P(None, "freq", None, "tile"), P(None, "tile")),
        out_specs=(P(None, "freq", None, "tile"), P(None, "freq", None, "tile")),
        check_vma=False,
    )
```

time: 1460 us -> 180 us (0.12); the launches traced: 1440 us -> 179 us
  waiting for transfers between devices: 1290 us -> 7.16 us
  blocking collectives: 57.2 us -> 132 us
  matrix products: 62.4 us -> 0 us
  Pallas kernels: 0 us -> 18.2 us
    all_gather x8 -> x0, waiting for transfers between devices: 1180 us -> none  [the longest x4 642 us: roundtrip(): piece = lax.all_gather(signal, 'freq', axis=1, tiled=True)]
    reduce_scatter x2 -> x0, waiting for transfers between devices: 112 us -> none  [on_device(): lax.psum_scatter(partial_sources, 'tile', scatter_dimension=3, tiled=True)]
    all_to_all x0 -> x7, blocking collectives: none -> 112 us  [exchange(): return lax.all_to_all(shaped, axes, 0, 0, tiled=True).reshape(blocks.shape)]
    dot_general x24 -> x0, matrix products: 62.4 us -> none  [the longest x4 18.2 us: roundtrip(): imag = jnp.einsum('jt,ptn->jpn', sine, piece, precision=highest)]
    all_gather x2 -> x1, blocking collectives: 57.2 us -> 20.3 us  [on_device(): gathered = lax.all_gather(direct, 'tile', axis=0)]
    pallas_call x0 -> x9, Pallas kernels: none -> 18.2 us  [the longest x2 7.08 us: forward_product(): pl.pallas_call(functools.partial(forward_kernel, updated), out_shape=jax....]
  transfers between devices with their start and end apart: 10 -> 1, of which waited for: 10 -> 1; matrix products, arithmetic and copies ran while one was open for 0% -> 0% of each run, Pallas kernels for 0% -> 0%
where the time goes in v1:
time: 180 us; the launch traced here: 179 us
  blocking collectives  132 us (73%)
  Pallas kernels  18.2 us (10%)
  local copies, waits for them, and re-layouts  13.5 us (8%)
  starting transfers between devices  7.43 us (4%)
  waiting for transfers between devices  7.16 us (4%)
    all_to_all x7, blocking collectives, exchange(): return lax.all_to_all(shaped, axes, 0, 0, tiled=True).reshape(blocks.shape)  112 us
    all_gather x1, blocking collectives, on_device(): gathered = lax.all_gather(direct, 'tile', axis=0)  20.3 us
    unnamed x14, local copies, waits for them, and re-layouts  13.5 us
    all_to_all x1, starting transfers between devices, exchange(): return lax.all_to_all(shaped, axes, 0, 0, tiled=True).reshape(blocks.shape)  7.43 us
    all_to_all x1, waiting for transfers between devices, exchange(): return lax.all_to_all(shaped, axes, 0, 0, tiled=True).reshape(blocks.shape)  7.16 us
    pallas_call x2, Pallas kernels, forward_product(): pl.pallas_call(functools.partial(forward_kernel, updated), out_shape=jax....  7.08 us
    pallas_call x2, Pallas kernels, adjoint_product(): pl.pallas_call(adjoint_kernel, out_shape=(jax.ShapeDtypeStruct((rows, LAN...  5.74 us
    pallas_call x4, Pallas kernels, roundtrip(): pl.pallas_call(functools.partial(roundtrip_kernel, summed, copies), out_s...  3.84 us
  transfers between devices with their start and end apart: 1, of which 1 were waited for; matrix products, arithmetic and copies ran while one was open for 0% of the time, Pallas kernels for 0%

profile of v1, /device:TPU:1, one launch (start us, length us, event | category | flops | bytes accessed | tf_op | source)
XLA Modules:
  0.0 178.9 jit_solution(1065077350351232637)
XLA Ops:
  0.7 20.3 %all-gather = f32[16,4,8,256]{3,2,1,0:T(8,128)S(1)} all-gather(f32[2,4,8,256]{3,2,1,0:T(8,128)} %direct.1), channel_id=2, replica_groups=mesh['freq'=32,'tile'=8] {'tile'}, dimensions={0}, use_global_device_ids=true | all-gather | bytes 589824 | tf_op jit(solution)/shard_map/all_gather | solution.py:231
  21.0 3.4 %copy-done = bf16[2,4,256,2048]{3,2,1,0:T(8,128)(2,1)S(1)} copy-done((bf16[2,4,256,2048]{3,2,1,0:T(8,128)(2,1)S(1)}, bf16[2,4,256,2048]{3,2,1,0:T(8,128)(2,1)}, u32[]{:S(2)}) %copy-start) | copy-done | bytes 8388632
  24.3 3.8 %forward_product.2 = f32[128,128]{1,0:T(8,128)} custom-call(f32[8,2,4,8,256]{4,3,2,1,0:T(8,128)S(1)} %bitcast.20, bf16[2,4,256,2048]{3,2,1,0:T(8,128)(2,1)S(1)} %copy-done), custom_call_target="tpu_custom_call" | custom-call | tf_op jit(solution)/shard_map/forward_product/pallas_call | solution.py:138
  28.2 7.4 %all-to-all-start = ((f32[32,4,128]{2,1,0:T(4,128)}), f32[32,4,128]{2,1,0:T(4,128)S(1)}, u32[]{:S(2)}, u32[]{:S(2)}) async-start(f32[32,4,128]{2,1,0:T(4,128)} %bitcast.4), calls=%async_computation | async-start | bytes 131072 | tf_op jit(solution)/shard_map/all_to_all | solution.py:220
  35.7 0.1 pad_add_fusion.place
  35.7 7.2 %all-to-all-done = f32[32,4,128]{2,1,0:T(4,128)S(1)} async-done(((f32[32,4,128]{2,1,0:T(4,128)}), f32[32,4,128]{2,1,0:T(4,128)S(1)}, u32[]{:S(2)}, u32[]{:S(2)}) %all-to-all-start) | async-done | bytes 65568 | tf_op jit(solution)/shard_map/all_to_all | solution.py:220
  42.9 0.9 roundtrip.4
  43.9 10.5 %all_to_all.40 = f32[32,4,128]{2,1,0:T(4,128)S(1)} all-to-all(f32[32,4,128]{2,1,0:T(4,128)S(1)} %bitcast.30), channel_id=1, replica_groups=mesh['freq'=32,'tile'=8] {'freq'}, dimensions={0} | all-to-all | bytes 131072 | tf_op jit(solution)/shard_map/all_to_all | solution.py:220
  54.4 3.4 %copy-done.1 = bf16[2,4,256,2048]{3,2,1,0:T(8,128)(2,1)S(1)} copy-done((bf16[2,4,256,2048]{3,2,1,0:T(8,128)(2,1)S(1)}, bf16[2,4,256,2048]{3,2,1,0:T(8,128)(2,1)}, u32[]{:S(2)}) %copy-start.1) | copy-done | bytes 8388632
  57.8 2.9 %adjoint_product.2 = (bf16[1024,128]{1,0:T(8,128)(2,1)S(1)}, f32[2,4,8,256]{3,2,1,0:T(8,128)}) custom-call(f32[128,128]{1,0:T(8,128)S(1)} %bitcast.26, bf16[2,4,256,2048]{3,2,1,0:T(8,128)(2,1)S(1)} %copy-done.1), custom_call_target="tpu_custom_call" | custom-call | tf_op jit(solution)/shard_map/adjoint_product/pallas_call | solution.py:180
  60.7 24.8 %all_to_all.41 = bf16[256,4,128]{2,1,0:T(4,128)(2,1)S(1)} all-to-all(bf16[256,4,128]{2,1,0:T(4,128)(2,1)S(1)} %bitcast.33), channel_id=1, replica_groups=mesh['freq'=32,'tile'=8] {'tile','freq'}, dimensions={0} | all-to-all | bytes 524288 | tf_op jit(solution)/shard_map/all_to_all | solution.py:220
  85.4 1.0 roundtrip.5
  86.4 20.5 %all_to_all.42 = bf16[256,4,128]{2,1,0:T(4,128)(2,1)S(1)} all-to-all(bf16[256,4,128]{2,1,0:T(4,128)(2,1)S(1)} %bitcast.25), channel_id=1, replica_groups=mesh['freq'=32,'tile'=8] {'tile','freq'}, dimensions={0} | all-to-all | bytes 524288 | tf_op jit(solution)/shard_map/all_to_all | solution.py:220
  106.9 3.4 %copy-done.2 = bf16[2,4,256,2048]{3,2,1,0:T(8,128)(2,1)S(1)} copy-done((bf16[2,4,256,2048]{3,2,1,0:T(8,128)(2,1)S(1)}, bf16[2,4,256,2048]{3,2,1,0:T(8,128)(2,1)}, u32[]{:S(2)}) %copy-start.2) | copy-done | bytes 8388632
  110.3 3.2 %forward_product.3 = f32[128,128]{1,0:T(8,128)S(1)} custom-call(f32[8,2,4,8,256]{4,3,2,1,0:T(8,128)S(1)} %bitcast.21, bf16[1024,128]{1,0:T(8,128)(2,1)S(1)} %bitcast.22, bf16[2,4,256,2048]{3,2,1,0:T(8,128)(2,1)S(1)} %copy-done.2), custom_call_target="tpu_custom_call" | custom-call | tf_op jit(solution)/shard_map/forward_product/pallas_call | solution.py:138
  113.5 10.9 %all_to_all.43 = f32[32,4,128]{2,1,0:T(4,128)S(1)} all-to-all(f32[32,4,128]{2,1,0:T(4,128)S(1)} %bitcast.28), channel_id=1, replica_groups=mesh['freq'=32,'tile'=8] {'freq'}, dimensions={0} | all-to-all | bytes 131072 | tf_op jit(solution)/shard_map/all_to_all | solution.py:220
  124.4 0.9 roundtrip.6
  125.3 10.5 %all_to_all.44 = f32[32,4,128]{2,1,0:T(4,128)S(1)} all-to-all(f32[32,4,128]{2,1,0:T(4,128)S(1)} %bitcast.32), channel_id=1, replica_groups=mesh['freq'=32,'tile'=8] {'freq'}, dimensions={0} | all-to-all | bytes 131072 | tf_op jit(solution)/shard_map/all_to_all | solution.py:220
  135.9 3.4 %copy-done.3 = bf16[2,4,256,2048]{3,2,1,0:T(8,128)(2,1)S(1)} copy-done((bf16[2,4,256,2048]{3,2,1,0:T(8,128)(2,1)S(1)}, bf16[2,4,256,2048]{3,2,1,0:T(8,128)(2,1)}, u32[]{:S(2)}) %copy-start.3) | copy-done | bytes 8388632
  139.2 2.9 %adjoint_product.3 = (bf16[1024,128]{1,0:T(8,128)(2,1)S(1)}, f32[2,4,8,256]{3,2,1,0:T(8,128)}) custom-call(f32[128,128]{1,0:T(8,128)S(1)} %bitcast.27, bf16[2,4,256,2048]{3,2,1,0:T(8,128)(2,1)S(1)} %copy-done.3), custom_call_target="tpu_custom_call" | custom-call | tf_op jit(solution)/shard_map/adjoint_product/pallas_call | solution.py:180
  142.1 23.4 %all_to_all.45 = bf16[256,4,128]{2,1,0:T(4,128)(2,1)S(1)} all-to-all(bf16[256,4,128]{2,1,0:T(4,128)(2,1)S(1)} %bitcast.34), channel_id=1, replica_groups=mesh['freq'=32,'tile'=8] {'tile','freq'}, dimensions={0} | all-to-all | bytes 524288 | tf_op jit(solution)/shard_map/all_to_all | solution.py:220
  165.5 1.0 roundtrip.7
  166.5 11.0 %all_to_all.46 = f32[32,4,128]{2,1,0:T(4,128)} all-to-all(f32[32,4,128]{2,1,0:T(4,128)S(1)} %bitcast.35), channel_id=1, replica_groups=mesh['freq'=32,'tile'=8] {'freq'}, dimensions={0} | all-to-all | bytes 131072 | tf_op jit(solution)/shard_map/all_to_all | solution.py:220
  177.4 1.5 finish.1
  (10 shorter events, 0.0 us)
Async XLA Ops:
  0.6 42.3 %copy-start.4 = (bf16[2,128,672]{2,1,0:T(8,128)(2,1)S(1)}, bf16[2,128,672]{2,1,0:T(8,128)(2,1)}, u32[]{:S(2)}) copy-start(bf16[2,128,672]{2,1,0:T(8,128)(2,1)} %constant.49.clone.forward) | copy-start | bytes 1032196
  0.6 42.3 %copy-start.6 = (s32[8,256]{1,0:T(8,128)S(1)}, s32[8,256]{1,0:T(8,128)}, u32[]{:S(2)}) copy-start(s32[8,256]{1,0:T(8,128)} %onset.7) | copy-start | bytes 24580
  21.0 3.4 %copy-start = (bf16[2,4,256,2048]{3,2,1,0:T(8,128)(2,1)S(1)}, bf16[2,4,256,2048]{3,2,1,0:T(8,128)(2,1)}, u32[]{:S(2)}) copy-start(bf16[2,4,256,2048]{3,2,1,0:T(8,128)(2,1)} %response.3) | copy-start | bytes 25165828
  24.3 18.6 %copy-start.5 = (bf16[2,224,384]{2,1,0:T(8,128)(2,1)S(1)}, bf16[2,224,384]{2,1,0:T(8,128)(2,1)}, u32[]{:S(2)}) copy-start(bf16[2,224,384]{2,1,0:T(8,128)(2,1)} %constant.48.clone.inverse) | copy-start | bytes 1032196
  28.2 14.7 %all-to-all-start = ((f32[32,4,128]{2,1,0:T(4,128)}), f32[32,4,128]{2,1,0:T(4,128)S(1)}, u32[]{:S(2)}, u32[]{:S(2)}) async-start(f32[32,4,128]{2,1,0:T(4,128)} %bitcast.4), calls=%async_computation | async-start | bytes 131072 | tf_op jit(solution)/shard_map/all_to_all | solution.py:220
  54.4 3.4 %copy-start.1 = (bf16[2,4,256,2048]{3,2,1,0:T(8,128)(2,1)S(1)}, bf16[2,4,256,2048]{3,2,1,0:T(8,128)(2,1)}, u32[]{:S(2)}) copy-start(bf16[2,4,256,2048]{3,2,1,0:T(8,128)(2,1)} %response.3) | copy-start | bytes 25165828
  106.9 3.4 %copy-start.2 = (bf16[2,4,256,2048]{3,2,1,0:T(8,128)(2,1)S(1)}, bf16[2,4,256,2048]{3,2,1,0:T(8,128)(2,1)}, u32[]{:S(2)}) copy-start(bf16[2,4,256,2048]{3,2,1,0:T(8,128)(2,1)} %response.3) | copy-start | bytes 25165828
  135.9 3.4 %copy-start.3 = (bf16[2,4,256,2048]{3,2,1,0:T(8,128)(2,1)S(1)}, bf16[2,4,256,2048]{3,2,1,0:T(8,128)(2,1)}, u32[]{:S(2)}) copy-start(bf16[2,4,256,2048]{3,2,1,0:T(8,128)(2,1)} %response.3) | copy-start | bytes 25165828

commit v2 on v0

v2 whole, which is shorter than its diff:
```python
import functools
import math

import jax
import jax.numpy as jnp
import numpy as np
from jax import lax
from jax.experimental import pallas as pl
from jax.experimental.pallas import tpu as pltpu
from jax.sharding import PartitionSpec as P

NT = 512
ITERS = 2
FIRST_BIN = 16
NF = 128
FP = 8
LAGS = 224
LANES = 128
BF16 = jnp.bfloat16
F32 = jnp.float32
VMEM_LIMIT = 24 * 1024 * 1024


def split(table):
    high = table.astype(np.float32).astype(jnp.bfloat16)
    low = (table - high.astype(np.float64)).astype(np.float32).astype(jnp.bfloat16)
    return high, low


def tables():
    bins = FIRST_BIN + np.arange(NF)
    lags = np.arange(LAGS)
    angle = 2.0 * math.pi / NT * ((lags[:, None] * bins[None, :]) % NT)
    weight = np.where(lags == 0, 2.0 / NT, 4.0 / NT)
    inverse, spread, forward = [], [], []
    for table in (np.cos(angle), np.sin(angle)):
        high, low = split(table)
        inverse.append(np.concatenate([high, high, low], axis=1))
        wide = np.pad(table.reshape(LAGS, NF // 4, 4), ((0, 0), (0, 0), (0, 4))).reshape(LAGS, 2 * NF)
        high, low = split(wide)
        spread.append(np.concatenate([high, high, low], axis=1))
        high, low = split((table * weight[:, None]).T)
        forward.append(np.concatenate([high, high, low], axis=1))
    return np.stack(inverse), np.stack(spread), np.stack(forward)


def pieces(value):
    high = value.astype(BF16)
    low = (value - high.astype(F32)).astype(BF16)
    return jnp.concatenate([high, low, high], axis=0)


def in_vmem(array):
    return pltpu.with_memory_space_constraint(array, pltpu.VMEM)


VMEM = pl.BlockSpec(memory_space=pltpu.VMEM)
SMEM = pl.BlockSpec(memory_space=pltpu.SMEM)
PARAMS = pltpu.CompilerParams(vmem_limit_bytes=VMEM_LIMIT)


def hold_kernel(response, held, done):
    copy = pltpu.make_async_copy(response, held, done)
    copy.start()
    copy.wait()


def hold(response):
    return pl.pallas_call(
        hold_kernel,
        out_shape=pltpu.VMEM(response.shape, response.dtype),
        in_specs=[pl.BlockSpec(memory_space=pltpu.HBM)],
        out_specs=VMEM,
        scratch_shapes=[pltpu.SemaphoreType.DMA],
        compiler_params=PARAMS,
        name="hold",
    )(pltpu.with_memory_space_constraint(response, pltpu.HBM))


def prepare_kernel(direct, out):
    for bin_ in range(direct.shape[1]):
        value = jnp.concatenate([direct[0, bin_], direct[1, bin_]], axis=0).astype(BF16)
        for copy in range(out.shape[0]):
            out[copy, bin_] = value


def prepare(direct, copies):
    parts, bins, focal, positions = direct.shape
    return pl.pallas_call(
        prepare_kernel,
        out_shape=jax.ShapeDtypeStruct((copies, bins, parts * focal, positions), BF16),
        in_specs=[VMEM],
        out_specs=VMEM,
        compiler_params=PARAMS,
        name="prepare",
    )(direct)


def forward_dots(stacked, response, bin_):
    dims = (((1,), (1,)), ((), ()))
    first = lax.dot_general(stacked, response[0, bin_], dims, preferred_element_type=F32)
    second = lax.dot_general(stacked, response[1, bin_], dims, preferred_element_type=F32)
    return first[:FP] - second[FP:], first[FP:] + second[:FP]


def first_forward_kernel(place, mine, other, direct, response, out):
    even = place[3] == 0
    for bin_ in range(response.shape[1]):
        columns = []
        for pair in range(mine.shape[0]):
            here, there = mine[pair, bin_], other[pair, bin_]
            columns.append(jnp.where(even, here, there))
            columns.append(jnp.where(even, there, here))
        parts = forward_dots(jnp.concatenate(columns, axis=1), response, bin_)
        for half in range(2):
            lanes = slice(half * LANES, (half + 1) * LANES)
            for part in range(2):
                start = (half * 2 + part) * 8 + bin_
                out[pl.ds(start, FP, stride=32), :] = parts[part][:, lanes]
                out[pl.ds(start + 4, FP, stride=32), :] = direct[part, bin_, :, lanes]


def first_forward(place, mine, other, direct, response):
    return pl.pallas_call(
        first_forward_kernel,
        out_shape=jax.ShapeDtypeStruct((2 * NF, LANES), F32),
        in_specs=[SMEM, VMEM, VMEM, VMEM, VMEM],
        out_specs=VMEM,
        compiler_params=PARAMS,
        name="first_forward",
    )(place, mine, other, direct, in_vmem(response))


def forward_kernel(update, response, out, held):
    held[...] = update[...].astype(F32)
    tiles = update.shape[0] // NF
    for bin_ in range(response.shape[1]):
        columns = []
        for tile in range(tiles):
            for half in range(2):
                both = []
                for part in range(2):
                    start = tile * NF + (half * 2 + part) * 4 + bin_
                    both.append(held[pl.ds(start, FP, stride=16), :])
                columns.append(jnp.concatenate(both, axis=0).astype(BF16))
        parts = forward_dots(jnp.concatenate(columns, axis=1), response, bin_)
        for half in range(2):
            for part in range(2):
                start = (half * 2 + part) * 4 + bin_
                out[pl.ds(start, FP, stride=16), :] = parts[part][:, half * LANES : (half + 1) * LANES]


def forward_product(update, response):
    return pl.pallas_call(
        forward_kernel,
        out_shape=jax.ShapeDtypeStruct((NF, LANES), F32),
        in_specs=[VMEM, VMEM],
        out_specs=VMEM,
        scratch_shapes=[pltpu.VMEM(update.shape, F32)],
        compiler_params=PARAMS,
        name="forward_product",
    )(update, in_vmem(response))


def adjoint_kernel(blocks, response, out, minus, held):
    tiles = response.shape[3] // (2 * LANES)
    for bin_ in range(response.shape[1]):
        rows = []
        for part in range(2):
            halves = []
            for half in range(2):
                start = (half * 2 + part) * 4 + bin_
                halves.append(blocks[pl.ds(start, FP, stride=16), :])
            rows.append(jnp.concatenate(halves, axis=1))
            minus[part, bin_] = rows[-1]
        stacked = jnp.concatenate(rows, axis=0).astype(BF16)
        first = jnp.dot(stacked, response[0, bin_], preferred_element_type=F32)
        second = jnp.dot(stacked, response[1, bin_], preferred_element_type=F32)
        parts = (first[:FP] + second[FP:], first[FP:] - second[:FP])
        for tile in range(tiles):
            for half in range(2):
                lane = (tile * 2 + half) * LANES
                for part in range(2):
                    start = tile * NF + (half * 2 + part) * 4 + bin_
                    held[pl.ds(start, FP, stride=16), :] = parts[part][:, lane : lane + LANES]
    out[...] = held[...].astype(out.dtype)


def adjoint_product(blocks, response):
    bins, receivers, sources = response.shape[1:]
    rows = NF * sources // (2 * LANES)
    return pl.pallas_call(
        adjoint_kernel,
        out_shape=(
            jax.ShapeDtypeStruct((rows, LANES), BF16),
            jax.ShapeDtypeStruct((2, bins, FP, receivers), F32),
        ),
        in_specs=[VMEM, VMEM],
        out_specs=(VMEM, VMEM),
        scratch_shapes=[pltpu.VMEM((rows, LANES), F32)],
        compiler_params=PARAMS,
        name="adjoint_product",
    )(blocks, in_vmem(response))


def lag_domain(spectrum, place, inverse, forward, onset):
    signal = jnp.dot(inverse[0], pieces(spectrum), preferred_element_type=F32)
    focal = lax.broadcasted_iota(jnp.int32, onset.shape, 0)
    limit = jnp.sum(jnp.where(focal == place[1], onset[...], 0), axis=0, keepdims=True)
    lag = lax.broadcasted_iota(jnp.int32, signal.shape, 0)
    signal = jnp.where(lag < limit, signal, 0.0)
    return jnp.dot(forward[0], pieces(signal), preferred_element_type=F32)


def minus_kernel(place, inverse, forward, onset, blocks, out):
    out[...] = lag_domain(blocks[...], place, inverse, forward, onset)


def plus_kernel(place, inverse, forward, onset, blocks, direct, out, held):
    spectrum = blocks[:NF, :].astype(F32)
    for tile in range(1, blocks.shape[0] // NF):
        spectrum += blocks[tile * NF : (tile + 1) * NF, :].astype(F32)
    held[...] = lag_domain(spectrum, place, inverse, forward, onset)
    senders = NF // 4
    for bin_ in range(4):
        held[pl.ds(bin_, senders, stride=4), :] += direct[pl.ds(4 + bin_, senders, stride=8), :]
    result = held[...].astype(out.dtype)
    for copy in range(out.shape[0] // NF):
        out[copy * NF : (copy + 1) * NF, :] = result


def roundtrip(kernel, place, tables, onset, operands, copies, dtype, scratch=()):
    whole = lambda i, place: (0, 0)
    part = lambda i, place: (place[0], 0, 0)
    in_specs = [pl.BlockSpec((1,) + table.shape[1:], part) for table in tables]
    in_specs.append(pl.BlockSpec((FP, LANES), lambda i, place: (0, place[2])))
    in_specs += [pl.BlockSpec(operand.shape, whole) for operand in operands]
    return pl.pallas_call(
        kernel,
        out_shape=jax.ShapeDtypeStruct((copies * NF, LANES), dtype),
        grid_spec=pltpu.PrefetchScalarGridSpec(
            num_scalar_prefetch=1,
            grid=(1,),
            in_specs=in_specs,
            out_specs=pl.BlockSpec((copies * NF, LANES), whole),
            scratch_shapes=list(scratch),
        ),
        compiler_params=PARAMS,
        name="roundtrip",
    )(place, *tables, onset, *operands)


def finish_kernel(blocks, out):
    for bin_ in range(out.shape[1]):
        for part in range(2):
            for half in range(2):
                value = blocks[pl.ds((half * 2 + part) * 4 + bin_, FP, stride=16), :]
                out[part, bin_, :, half * LANES : (half + 1) * LANES] = value


def finish(blocks, shape):
    return pl.pallas_call(
        finish_kernel,
        out_shape=jax.ShapeDtypeStruct(shape, F32),
        in_specs=[VMEM],
        out_specs=VMEM,
        compiler_params=PARAMS,
        name="finish",
    )(blocks)


def exchange(blocks, axes, count):
    shaped = blocks.reshape(count, blocks.shape[0] // count, LANES)
    return lax.all_to_all(shaped, axes, 0, 0, tiled=True).reshape(blocks.shape)


def on_device(response, direct, onset):
    groups = lax.axis_size("freq")
    tiles = lax.axis_size("tile")
    everyone = ("tile", "freq")
    own = lax.axis_index("freq")
    place = jnp.stack([own & 1, own >> 2, (own >> 1) & 1, lax.axis_index("tile") & 1]).astype(jnp.int32)
    inverse, spread, forward = (jnp.asarray(table) for table in tables())
    held = hold(response)
    pairs = tiles // 2
    chips = [[core + 2 * pair for pair in range(pairs)] for core in range(2)]
    mine = lax.all_to_all(prepare(direct, pairs), "tile", 0, 0, axis_index_groups=chips, tiled=True)
    other = lax.ppermute(mine, "tile", [(tile, tile ^ 1) for tile in range(tiles)])
    update, owned = None, None
    for step in range(ITERS):
        if step == 0:
            owned = exchange(first_forward(place, mine, other, direct, held), "freq", groups)
            blocks = roundtrip(minus_kernel, place, (spread, forward), onset, (owned,), 1, F32)
        else:
            upgoing = exchange(forward_product(update, held), "freq", groups)
            blocks = roundtrip(minus_kernel, place, (inverse, forward), onset, (upgoing,), 1, F32)
        partial, minus = adjoint_product(exchange(blocks, "freq", groups), held)
        partial = exchange(partial, everyone, groups * tiles)
        last = step + 1 == ITERS
        copies, dtype = (1, F32) if last else (tiles, BF16)
        scratch = (pltpu.VMEM((NF, LANES), F32),)
        plus = roundtrip(plus_kernel, place, (inverse, forward), onset, (partial, owned), copies, dtype, scratch)
        if last:
            plus = finish(exchange(plus, "freq", groups), direct.shape)
        else:
            update = exchange(plus, everyone, groups * tiles)
    return (minus, plus)


def solution(mesh):
    return jax.shard_map(
        on_device,
        mesh=mesh,
        in_specs=(P(None, "freq", "tile", None), P(None, "freq", None, "tile"), P(None, "tile")),
        out_specs=(P(None, "freq", None, "tile"), P(None, "freq", None, "tile")),
        check_vma=False,
    )
```

time: 1460 us -> 161 us (0.11); the launches traced: 1440 us -> 161 us
  waiting for transfers between devices: 1290 us -> 0.01 us
  blocking collectives: 57.2 us -> 140 us
  matrix products: 62.4 us -> 0 us
  Pallas kernels: 0 us -> 16.1 us
    all_gather x8 -> x0, waiting for transfers between devices: 1180 us -> none  [the longest x4 642 us: roundtrip(): piece = lax.all_gather(signal, 'freq', axis=1, tiled=True)]
    all_to_all x0 -> x9, blocking collectives: none -> 140 us  [the longest x8 124 us: exchange(): return lax.all_to_all(shaped, axes, 0, 0, tiled=True).reshape(blocks.shape)]
    reduce_scatter x2 -> x0, waiting for transfers between devices: 112 us -> none  [on_device(): lax.psum_scatter(partial_sources, 'tile', scatter_dimension=3, tiled=True)]
    dot_general x24 -> x0, matrix products: 62.4 us -> none  [the longest x4 18.2 us: roundtrip(): imag = jnp.einsum('jt,ptn->jpn', sine, piece, precision=highest)]
    all_gather x2 -> x0, blocking collectives: 57.2 us -> none  [on_device(): lax.all_gather(plus.astype(jnp.bfloat16), 'tile', axis=3, tiled=True)]
    pallas_call x0 -> x11, Pallas kernels: none -> 16.1 us  [the longest x4 3.96 us: roundtrip(): pl.pallas_call(kernel, out_shape=jax.ShapeDtypeStruct((copies * NF, LANES...]
  transfers between devices with their start and end apart: 10 -> 1, of which waited for: 10 -> 0; matrix products, arithmetic and copies ran while one was open for 0% -> 0% of each run, Pallas kernels for 0% -> 2%
where the time goes in v2:
time: 161 us
  blocking collectives  140 us (87%)
  Pallas kernels  16.1 us (10%)
  starting transfers between devices  2.97 us (2%)
    all_to_all x8, blocking collectives, exchange(): return lax.all_to_all(shaped, axes, 0, 0, tiled=True).reshape(blocks.shape)  124 us
    all_to_all x1, blocking collectives, on_device(): lax.all_to_all(prepare(direct, pairs), 'tile', 0, 0, axis_index_groups=ch...  16 us
    pallas_call x4, Pallas kernels, roundtrip(): pl.pallas_call(kernel, out_shape=jax.ShapeDtypeStruct((copies * NF, LANES...  3.96 us
    pallas_call x1, Pallas kernels, hold(): pl.pallas_call(hold_kernel, out_shape=pltpu.VMEM(response.shape, response...  3.42 us
  transfers between devices with their start and end apart: 1, of which 0 were waited for; matrix products, arithmetic and copies ran while one was open for 0% of the time, Pallas kernels for 2%

profile of v2, /device:TPU:1, one launch (start us, length us, event | category | flops | bytes accessed | tf_op | source)
XLA Modules:
  0.0 161.1 jit_solution(15797062507006730425)
XLA Ops:
  0.6 0.8 copy-done.3
  1.5 16.0 %all_to_all.45.mine = bf16[4,4,16,256]{3,2,1,0:T(8,128)(2,1)S(1)} all-to-all(bf16[4,4,16,256]{3,2,1,0:T(8,128)(2,1)S(1)} %prepare.1), channel_id=1, replica_groups={{0,2,4,6},{1,3,5,7},{8,10,12,14},{9,11,13,15},{16,18,20,22},{17,19,21,2..., dimensions={0} | all-to-all | bytes 262144 | tf_op jit(solution)/shard_map/all_to_all | solution.py:287
  17.5 3.0 %collective-permute-start = (bf16[4,4,16,256]{3,2,1,0:T(8,128)(2,1)S(1)}, bf16[4,4,16,256]{3,2,1,0:T(8,128)(2,1)S(1)}, u32[]{:S(2)}, u32[]{:S(2)}) collective-permute-start(bf16[4,4,16,256]{3,2,1,0:T(8,128)(2,1)S(1)} %all_to_all.45.mine), channel_id=1, source_target_pairs={{0,1},{1,0},{2,3},{3,2},{4,5},{5,4},{6,7},{7,6},{8,9},{9,8},{10,11... | collective-permute-start | bytes 393224 | tf_op jit(solution)/shard_map/ppermute | solution.py:288
  20.5 3.4 %hold.1.response = bf16[2,4,256,2048]{3,2,1,0:T(8,128)(2,1)S(1)} custom-call(bf16[2,4,256,2048]{3,2,1,0:T(8,128)(2,1)} %response.1), custom_call_target="tpu_custom_call" | custom-call | tf_op jit(solution)/shard_map/hold/pallas_call | solution.py:69
  23.9 0.0 copy-start
  23.9 0.0 copy-start.2
  24.0 0.1 pad_add_fusion.place
  24.1 2.8 %first_forward.1 = f32[256,128]{1,0:T(8,128)S(1)} custom-call(s32[4]{0:T(128)S(1)} %pad_add_fusion.place, bf16[4,4,16,256]{3,2,1,0:T(8,128)(2,1)S(1)} %all_to_all.45.mine, bf16[4,4,16,256]{3,2,1,0:T(8,128)(2,1)S(1)} %collective-permute-done.other, f32[2,4,8,256]{3,2,1,0:T(8,128)S(1)} %copy-done.4, bf16[2,4,256,2048]{3,2,1,0:T(8,128)(2,1)S(1)} %hold.1.response), custom_call_target="tpu_custom_call" | custom-call | tf_op jit(solution)/shard_map/first_forward/pallas_call | solution.py:124
  26.9 14.7 %all_to_all.46 = f32[32,8,128]{2,1,0:T(8,128)S(1)} all-to-all(f32[32,8,128]{2,1,0:T(8,128)S(1)} %bitcast.27), channel_id=1, replica_groups=mesh['freq'=32,'tile'=8] {'freq'}, dimensions={0} | all-to-all | bytes 262144 | tf_op jit(solution)/shard_map/all_to_all | solution.py:274
  41.6 1.0 roundtrip.4
  42.6 10.7 %all_to_all.47 = f32[32,4,128]{2,1,0:T(4,128)S(1)} all-to-all(f32[32,4,128]{2,1,0:T(4,128)S(1)} %bitcast.32), channel_id=1, replica_groups=mesh['freq'=32,'tile'=8] {'freq'}, dimensions={0} | all-to-all | bytes 131072 | tf_op jit(solution)/shard_map/all_to_all | solution.py:274
  53.3 1.4 adjoint_product.2
  54.7 22.8 %all_to_all.48 = bf16[256,4,128]{2,1,0:T(4,128)(2,1)S(1)} all-to-all(bf16[256,4,128]{2,1,0:T(4,128)(2,1)S(1)} %bitcast.36), channel_id=1, replica_groups=mesh['freq'=32,'tile'=8] {'tile','freq'}, dimensions={0} | all-to-all | bytes 524288 | tf_op jit(solution)/shard_map/all_to_all | solution.py:274
  77.5 1.0 roundtrip.5
  78.5 20.5 %all_to_all.49 = bf16[256,4,128]{2,1,0:T(4,128)(2,1)S(1)} all-to-all(bf16[256,4,128]{2,1,0:T(4,128)(2,1)S(1)} %bitcast.24), channel_id=1, replica_groups=mesh['freq'=32,'tile'=8] {'tile','freq'}, dimensions={0} | all-to-all | bytes 524288 | tf_op jit(solution)/shard_map/all_to_all | solution.py:274
  99.0 2.3 %forward_product.1 = f32[128,128]{1,0:T(8,128)S(1)} custom-call(bf16[1024,128]{1,0:T(8,128)(2,1)S(1)} %bitcast.25, bf16[2,4,256,2048]{3,2,1,0:T(8,128)(2,1)S(1)} %hold.1.response), custom_call_target="tpu_custom_call" | custom-call | tf_op jit(solution)/shard_map/forward_product/pallas_call | solution.py:154
  101.3 10.9 %all_to_all.50 = f32[32,4,128]{2,1,0:T(4,128)S(1)} all-to-all(f32[32,4,128]{2,1,0:T(4,128)S(1)} %bitcast.30), channel_id=1, replica_groups=mesh['freq'=32,'tile'=8] {'freq'}, dimensions={0} | all-to-all | bytes 131072 | tf_op jit(solution)/shard_map/all_to_all | solution.py:274
  112.2 0.9 roundtrip.6
  113.2 10.5 %all_to_all.51 = f32[32,4,128]{2,1,0:T(4,128)S(1)} all-to-all(f32[32,4,128]{2,1,0:T(4,128)S(1)} %bitcast.34), channel_id=1, replica_groups=mesh['freq'=32,'tile'=8] {'freq'}, dimensions={0} | all-to-all | bytes 131072 | tf_op jit(solution)/shard_map/all_to_all | solution.py:274
  123.7 1.4 adjoint_product.3
  125.1 23.4 %all_to_all.52 = bf16[256,4,128]{2,1,0:T(4,128)(2,1)S(1)} all-to-all(bf16[256,4,128]{2,1,0:T(4,128)(2,1)S(1)} %bitcast.35), channel_id=1, replica_groups=mesh['freq'=32,'tile'=8] {'tile','freq'}, dimensions={0} | all-to-all | bytes 524288 | tf_op jit(solution)/shard_map/all_to_all | solution.py:274
  148.5 1.0 roundtrip.7
  149.5 10.9 %all_to_all.53 = f32[32,4,128]{2,1,0:T(4,128)S(1)} all-to-all(f32[32,4,128]{2,1,0:T(4,128)S(1)} %bitcast.31), channel_id=1, replica_groups=mesh['freq'=32,'tile'=8] {'freq'}, dimensions={0} | all-to-all | bytes 131072 | tf_op jit(solution)/shard_map/all_to_all | solution.py:274
  160.4 0.7 finish.1
  (11 shorter events, 0.0 us)
Async XLA Ops:
  0.6 0.8 copy-start.3
  17.5 6.5 %collective-permute-start = (bf16[4,4,16,256]{3,2,1,0:T(8,128)(2,1)S(1)}, bf16[4,4,16,256]{3,2,1,0:T(8,128)(2,1)S(1)}, u32[]{:S(2)}, u32[]{:S(2)}) collective-permute-start(bf16[4,4,16,256]{3,2,1,0:T(8,128)(2,1)S(1)} %all_to_all.45.mine), channel_id=1, source_target_pairs={{0,1},{1,0},{2,3},{3,2},{4,5},{5,4},{6,7},{7,6},{8,9},{9,8},{10,11... | collective-permute-start | bytes 393224 | tf_op jit(solution)/shard_map/ppermute | solution.py:288
  20.5 3.6 %copy-start.4 = (f32[2,4,8,256]{3,2,1,0:T(8,128)S(1)}, f32[2,4,8,256]{3,2,1,0:T(8,128)}, u32[]{:S(2)}) copy-start(f32[2,4,8,256]{3,2,1,0:T(8,128)} %direct.3) | copy-start | bytes 196612
  23.9 17.7 %copy-start = (bf16[2,128,672]{2,1,0:T(8,128)(2,1)S(1)}, bf16[2,128,672]{2,1,0:T(8,128)(2,1)}, u32[]{:S(2)}) copy-start(bf16[2,128,672]{2,1,0:T(8,128)(2,1)} %constant.21.clone.forward) | copy-start | bytes 1032196
  23.9 17.7 %copy-start.2 = (bf16[2,224,768]{2,1,0:T(8,128)(2,1)S(1)}, bf16[2,224,768]{2,1,0:T(8,128)(2,1)}, u32[]{:S(2)}) copy-start(bf16[2,224,768]{2,1,0:T(8,128)(2,1)} %constant.20.clone.inverse) | copy-start | bytes 2064388
  23.9 17.7 %copy-start.5 = (s32[8,256]{1,0:T(8,128)S(1)}, s32[8,256]{1,0:T(8,128)}, u32[]{:S(2)}) copy-start(s32[8,256]{1,0:T(8,128)} %onset.7) | copy-start | bytes 24580
  24.0 53.5 %copy-start.1 = (bf16[2,224,384]{2,1,0:T(8,128)(2,1)S(1)}, bf16[2,224,384]{2,1,0:T(8,128)(2,1)}, u32[]{:S(2)}) copy-start(bf16[2,224,384]{2,1,0:T(8,128)(2,1)} %constant.19.clone.inverse) | copy-start | bytes 1032196

commit v3 on v2

v3 whole, which is shorter than its diff:
```python
import functools
import math

import jax
import jax.numpy as jnp
import numpy as np
from jax import lax
from jax.experimental import pallas as pl
from jax.experimental.pallas import tpu as pltpu
from jax.sharding import PartitionSpec as P

NT = 512
ITERS = 2
FIRST_BIN = 16
NF = 128
FP = 8
LAGS = 224
LANES = 128
BF16 = jnp.bfloat16
F32 = jnp.float32
VMEM_LIMIT = 24 * 1024 * 1024

SHARED = 64
PIECES = 16
OWNERS = 32


def split(table):
    high = table.astype(np.float32).astype(jnp.bfloat16)
    low = (table - high.astype(np.float64)).astype(np.float32).astype(jnp.bfloat16)
    return high, low


def tables():
    bins = FIRST_BIN + np.arange(NF)
    lags = np.arange(LAGS)
    angle = 2.0 * math.pi / NT * ((lags[:, None] * bins[None, :]) % NT)
    weight = np.where(lags == 0, 2.0 / NT, 4.0 / NT)
    rounded, inverse, forward, own = [], [], [], []
    devices = np.arange(OWNERS)
    pair = np.stack([devices, devices ^ (OWNERS // 2)], axis=1)
    for part, table in enumerate((np.cos(angle), np.sin(angle))):
        high, low = split(table)
        rounded.append(np.concatenate([high, low], axis=1))
        inverse.append(np.concatenate([high, high, low], axis=1))
        high, low = split((table * weight[:, None]).T)
        forward.append(np.concatenate([high, high, low], axis=1))
        high, low = (piece.reshape(OWNERS, 4, LAGS)[pair].reshape(OWNERS, 8, LAGS) for piece in (high, low))
        rows = np.concatenate(
            [np.concatenate([high, high], axis=2), np.concatenate([low, np.zeros_like(low)], axis=2)], axis=1
        )
        own.append(rows[part * OWNERS // 2 : (part + 1) * OWNERS // 2])
    return np.stack(rounded), np.concatenate(own), np.stack(inverse), np.stack(forward)


def high_low(value):
    high = value.astype(BF16)
    return high, (value - high.astype(F32)).astype(BF16)


def pieces(value):
    high, low = high_low(value)
    return jnp.concatenate([high, low, high], axis=0)


def in_vmem(array):
    return pltpu.with_memory_space_constraint(array, pltpu.VMEM)


VMEM = pl.BlockSpec(memory_space=pltpu.VMEM)
SMEM = pl.BlockSpec(memory_space=pltpu.SMEM)
PARAMS = pltpu.CompilerParams(vmem_limit_bytes=VMEM_LIMIT)


def prepare_kernel(direct, out):
    for bin_ in range(direct.shape[1]):
        value = jnp.concatenate([direct[0, bin_], direct[1, bin_]], axis=0).astype(BF16)
        for copy in range(out.shape[0]):
            out[copy, bin_] = value


def prepare(direct, copies):
    parts, bins, focal, positions = direct.shape
    return pl.pallas_call(
        prepare_kernel,
        out_shape=jax.ShapeDtypeStruct((copies, bins, parts * focal, positions), BF16),
        in_specs=[VMEM],
        out_specs=VMEM,
        compiler_params=PARAMS,
        name="prepare",
    )(direct)


def forward_dots(stacked, response, bin_):
    dims = (((1,), (1,)), ((), ()))
    first = lax.dot_general(stacked, response[0, bin_], dims, preferred_element_type=F32)
    second = lax.dot_general(stacked, response[1, bin_], dims, preferred_element_type=F32)
    return first[:FP] - second[FP:], first[FP:] + second[:FP]


def share(parts, bin_, out, stride):
    for part in range(2):
        tile = jnp.concatenate([parts[part][:, :LANES], parts[part][:, LANES:]], axis=0).astype(BF16)
        for owner in range(part * OWNERS // 2, (part + 1) * OWNERS // 2):
            start = owner * stride + bin_ * 16
            out[start : start + 16, :] = tile


def first_forward_kernel(place, mine, other, direct, response, out, kept, held, done):
    bins = response.shape[1]
    copies = [
        [pltpu.make_async_copy(response.at[part, bin_], kept.at[part, bin_], done.at[part, bin_]) for part in range(2)]
        for bin_ in range(bins)
    ]
    for both in copies:
        for copy in both:
            copy.start()
    stride = SHARED + PIECES
    held[...] = jnp.zeros_like(held)
    for bin_ in range(bins):
        for half in range(2):
            for part in range(2):
                value = direct[part, bin_, :, half * LANES : (half + 1) * LANES]
                start = (half * 2 + part) * PIECES + bin_
                for row, piece in enumerate(high_low(value)):
                    held[pl.ds(start + 4 * row, FP, stride=4 * PIECES), :] = piece.astype(F32)
    for owner in range(OWNERS):
        start = owner * stride + SHARED
        out[start : start + PIECES, :] = held[owner * PIECES : (owner + 1) * PIECES, :].astype(BF16)
    even = place[3] == 0
    for bin_ in range(bins):
        columns = []
        for pair in range(mine.shape[0]):
            here, there = mine[pair, bin_], other[pair, bin_]
            columns.append(jnp.where(even, here, there))
            columns.append(jnp.where(even, there, here))
        for copy in copies[bin_]:
            copy.wait()
        share(forward_dots(jnp.concatenate(columns, axis=1), kept, bin_), bin_, out, stride)


def first_forward(place, mine, other, direct, response):
    return pl.pallas_call(
        first_forward_kernel,
        out_shape=(
            jax.ShapeDtypeStruct((OWNERS * (SHARED + PIECES), LANES), BF16),
            pltpu.VMEM(response.shape, response.dtype),
        ),
        in_specs=[SMEM, VMEM, VMEM, VMEM, pl.BlockSpec(memory_space=pltpu.HBM)],
        out_specs=(VMEM, VMEM),
        scratch_shapes=[
            pltpu.VMEM((OWNERS * PIECES, LANES), F32),
            pltpu.SemaphoreType.DMA(response.shape[:2]),
        ],
        compiler_params=PARAMS,
        name="first_forward",
    )(place, mine, other, direct, pltpu.with_memory_space_constraint(response, pltpu.HBM))


def forward_kernel(update, response, out, held):
    held[...] = update[...].astype(F32)
    tiles = update.shape[0] // NF
    for bin_ in range(response.shape[1]):
        columns = []
        for tile in range(tiles):
            for half in range(2):
                both = []
                for part in range(2):
                    start = tile * NF + (half * 2 + part) * 4 + bin_
                    both.append(held[pl.ds(start, FP, stride=16), :])
                columns.append(jnp.concatenate(both, axis=0).astype(BF16))
        share(forward_dots(jnp.concatenate(columns, axis=1), response, bin_), bin_, out, SHARED)


def forward_product(update, response):
    return pl.pallas_call(
        forward_kernel,
        out_shape=jax.ShapeDtypeStruct((OWNERS * SHARED, LANES), BF16),
        in_specs=[VMEM, VMEM],
        out_specs=VMEM,
        scratch_shapes=[pltpu.VMEM(update.shape, F32)],
        compiler_params=PARAMS,
        name="forward_product",
    )(update, in_vmem(response))


def minus_kernel(stride, place, rounded, own, onset, blocks, mine, other, *refs):
    *owned, spectra = refs
    for owner in range(OWNERS):
        start = owner * stride
        spectra[owner * SHARED : (owner + 1) * SHARED, :] = blocks[start : start + SHARED, :].astype(F32)
    inverse = rounded[place[4] // (OWNERS // 2)]
    forward = own[place[4]]
    wide = 2
    for half in range(2):
        lanes = slice(half * LANES, (half + 1) * LANES)
        for focal in range(0, FP, wide):
            first = half * FP + focal
            spectrum = jnp.concatenate(
                [spectra[pl.ds(first + i, NF, stride=16), :].astype(BF16) for i in range(wide)], axis=1
            )
            spectrum = jnp.concatenate([spectrum, spectrum], axis=0)
            signal = jnp.dot(inverse, spectrum, preferred_element_type=F32)
            limit = jnp.concatenate([onset[focal + i : focal + i + 1, lanes] for i in range(wide)], axis=1)
            lag = lax.broadcasted_iota(jnp.int32, signal.shape, 0)
            signal = jnp.where(lag < limit, signal, 0.0)
            signal = jnp.concatenate(high_low(signal), axis=0)
            result = jnp.dot(forward, signal, preferred_element_type=F32)
            result = result[:8] + result[8:]
            for i in range(wide):
                block = result[:, i * LANES : (i + 1) * LANES]
                mine[pl.ds(first + i, 4, stride=16), :] = block[:4]
                other[pl.ds(first + i, 4, stride=16), :] = block[4:]
    if owned:
        (owned,) = owned
        for owner in range(OWNERS):
            start = owner * stride + SHARED
            spectra[owner * PIECES : (owner + 1) * PIECES, :] = blocks[start : start + PIECES, :].astype(F32)
        for bin_ in range(4):
            high, low = (spectra[pl.ds(bin_ + 4 * i, OWNERS, stride=PIECES), :] for i in range(2))
            owned[pl.ds(bin_, OWNERS, stride=4), :] = high + low


def minus_roundtrip(place, rounded, own, onset, blocks, carried):
    stride = SHARED + PIECES if carried else SHARED
    out_shape = [jax.ShapeDtypeStruct((SHARED, LANES), F32)] * 2
    if carried:
        out_shape.append(jax.ShapeDtypeStruct((NF, LANES), F32))
    return pl.pallas_call(
        functools.partial(minus_kernel, stride),
        out_shape=out_shape,
        in_specs=[SMEM] + [VMEM] * 4,
        out_specs=[VMEM] * len(out_shape),
        scratch_shapes=[pltpu.VMEM((OWNERS * SHARED, LANES), F32)],
        compiler_params=PARAMS,
        name="minus_roundtrip",
    )(place, rounded, own, onset, blocks)


def adjoint_kernel(place, mine, other, response, out, minus, held):
    lower = place[4] < OWNERS // 2
    tiles = response.shape[3] // (2 * LANES)
    for bin_ in range(response.shape[1]):
        here, there = (
            jnp.concatenate([part[start : start + FP, :] for start in (bin_ * 16, bin_ * 16 + FP)], axis=1)
            for part in (mine, other)
        )
        both = jnp.where(lower, here, there), jnp.where(lower, there, here)
        for part in range(2):
            minus[part, bin_] = both[part]
        stacked = jnp.concatenate(both, axis=0).astype(BF16)
        first = jnp.dot(stacked, response[0, bin_], preferred_element_type=F32)
        second = jnp.dot(stacked, response[1, bin_], preferred_element_type=F32)
        parts = (first[:FP] + second[FP:], first[FP:] - second[:FP])
        for tile in range(tiles):
            for half in range(2):
                lane = (tile * 2 + half) * LANES
                for part in range(2):
                    start = tile * NF + (half * 2 + part) * 4 + bin_
                    held[pl.ds(start, FP, stride=16), :] = parts[part][:, lane : lane + LANES]
    out[...] = held[...].astype(out.dtype)


def adjoint_product(place, mine, other, response):
    bins, receivers, sources = response.shape[1:]
    rows = NF * sources // (2 * LANES)
    return pl.pallas_call(
        adjoint_kernel,
        out_shape=(
            jax.ShapeDtypeStruct((rows, LANES), BF16),
            jax.ShapeDtypeStruct((2, bins, FP, receivers), F32),
        ),
        in_specs=[SMEM] + [VMEM] * 3,
        out_specs=(VMEM, VMEM),
        scratch_shapes=[pltpu.VMEM((rows, LANES), F32)],
        compiler_params=PARAMS,
        name="adjoint_product",
    )(place, mine, other, in_vmem(response))


def plus_kernel(place, inverse, forward, onset, blocks, direct, out):
    spectrum = blocks[:NF, :].astype(F32)
    for tile in range(1, blocks.shape[0] // NF):
        spectrum += blocks[tile * NF : (tile + 1) * NF, :].astype(F32)
    signal = jnp.dot(inverse[place[0]], pieces(spectrum), preferred_element_type=F32)
    limits = jnp.where(place[2] == 0, onset[:, :LANES], onset[:, LANES:])
    focal = lax.broadcasted_iota(jnp.int32, limits.shape, 0)
    limit = jnp.sum(jnp.where(focal == place[1], limits, 0), axis=0, keepdims=True)
    lag = lax.broadcasted_iota(jnp.int32, signal.shape, 0)
    signal = jnp.where(lag < limit, signal, 0.0)
    result = jnp.dot(forward[place[0]], pieces(signal), preferred_element_type=F32)
    result = (direct[...] + result).astype(out.dtype)
    for copy in range(out.shape[0] // NF):
        out[copy * NF : (copy + 1) * NF, :] = result


def plus_roundtrip(place, inverse, forward, onset, blocks, direct, copies, dtype):
    return pl.pallas_call(
        plus_kernel,
        out_shape=jax.ShapeDtypeStruct((copies * NF, LANES), dtype),
        in_specs=[SMEM] + [VMEM] * 5,
        out_specs=VMEM,
        compiler_params=PARAMS,
        name="plus_roundtrip",
    )(place, inverse, forward, onset, blocks, direct)


def finish_kernel(blocks, out):
    for bin_ in range(out.shape[1]):
        for part in range(2):
            for half in range(2):
                value = blocks[pl.ds((half * 2 + part) * 4 + bin_, FP, stride=16), :]
                out[part, bin_, :, half * LANES : (half + 1) * LANES] = value


def finish(blocks, shape):
    return pl.pallas_call(
        finish_kernel,
        out_shape=jax.ShapeDtypeStruct(shape, F32),
        in_specs=[VMEM],
        out_specs=VMEM,
        compiler_params=PARAMS,
        name="finish",
    )(blocks)


def exchange(blocks, axes, count):
    shaped = blocks.reshape(count, blocks.shape[0] // count, LANES)
    return lax.all_to_all(shaped, axes, 0, 0, tiled=True).reshape(blocks.shape)


def on_device(response, direct, onset):
    groups = lax.axis_size("freq")
    tiles = lax.axis_size("tile")
    everyone = ("tile", "freq")
    own = lax.axis_index("freq")
    place = [own & 1, own >> 2, (own >> 1) & 1, lax.axis_index("tile") & 1, own]
    place = jnp.stack(place).astype(jnp.int32)
    rounded, own_bins, inverse, forward = (jnp.asarray(table) for table in tables())
    pairs = tiles // 2
    chips = [[core + 2 * pair for pair in range(pairs)] for core in range(2)]
    cores = [(tile, tile ^ 1) for tile in range(tiles)]
    partners = [(owner, owner ^ (OWNERS // 2)) for owner in range(OWNERS)]
    mine = lax.all_to_all(prepare(direct, pairs), "tile", 0, 0, axis_index_groups=chips, tiled=True)
    other = lax.ppermute(mine, "tile", cores)
    for step in range(ITERS):
        if step == 0:
            upgoing, held = first_forward(place, mine, other, direct, response)
        else:
            upgoing = forward_product(update, held)
        upgoing = exchange(upgoing, "freq", groups)
        mine, other, *owned = minus_roundtrip(place, rounded, own_bins, onset, upgoing, step == 0)
        if step == 0:
            (direct_columns,) = owned
        partial, minus = adjoint_product(place, mine, lax.ppermute(other, "freq", partners), held)
        partial = exchange(partial, everyone, groups * tiles)
        last = step + 1 == ITERS
        copies, dtype = (1, F32) if last else (tiles, BF16)
        plus = plus_roundtrip(place, inverse, forward, onset, partial, direct_columns, copies, dtype)
        if last:
            plus = finish(exchange(plus, "freq", groups), direct.shape)
        else:
            update = exchange(plus, everyone, groups * tiles)
    return (minus, plus)


def solution(mesh):
    return jax.shard_map(
        on_device,
        mesh=mesh,
        in_specs=(P(None, "freq", "tile", None), P(None, "freq", None, "tile"), P(None, "tile")),
        out_specs=(P(None, "freq", None, "tile"), P(None, "freq", None, "tile")),
        check_vma=False,
    )
```

time: 161 us -> 157 us (0.975)
  blocking collectives: 140 us -> 127 us
  waiting for transfers between devices: 0.01 us -> 4.33 us
  starting transfers between devices: 2.97 us -> 5.34 us
    all_to_all x8 -> x6, blocking collectives: 124 us -> 111 us  [exchange(): return lax.all_to_all(shaped, axes, 0, 0, tiled=True).reshape(blocks.shape)]
    ppermute x1 -> x3, waiting for transfers between devices: 0.01 us -> 4.33 us  [the longest x2 3.43 us: on_device(): lax.ppermute(other, 'freq', partners)]
    ppermute x1 -> x3, starting transfers between devices: 2.97 us -> 5.34 us  [the longest x1 2.97 us: on_device(): other = lax.ppermute(mine, 'tile', cores)]
    pallas_call x7 -> x6, Pallas kernels: 12.5 us -> 12.2 us  [the longest x1 4.83 us: first_forward(): pl.pallas_call(first_forward_kernel, out_shape=(jax.ShapeDtypeStruct((OWN...]
  transfers between devices with their start and end apart: 1 -> 3, of which waited for: 0 -> 3; matrix products, arithmetic and copies ran while one was open for 0% -> 0% of each run, Pallas kernels for 2% -> 0%
where the time goes in v3:
time: 157 us; the launch traced here: 156 us
  blocking collectives  127 us (81%)
  Pallas kernels  16.8 us (11%)
  starting transfers between devices  5.34 us (3%)
  waiting for transfers between devices  4.33 us (3%)
  local copies, waits for them, and re-layouts  1.85 us (1%)
    all_to_all x6, blocking collectives, exchange(): return lax.all_to_all(shaped, axes, 0, 0, tiled=True).reshape(blocks.shape)  111 us
    all_to_all x1, blocking collectives, on_device(): lax.all_to_all(prepare(direct, pairs), 'tile', 0, 0, axis_index_groups=ch...  16 us
    pallas_call x1, Pallas kernels, first_forward(): pl.pallas_call(first_forward_kernel, out_shape=(jax.ShapeDtypeStruct((OWN...  4.83 us
    pallas_call x2, Pallas kernels, adjoint_product(): pl.pallas_call(adjoint_kernel, out_shape=(jax.ShapeDtypeStruct((rows, LAN...  3.92 us
    ppermute x2, waiting for transfers between devices, on_device(): lax.ppermute(other, 'freq', partners)  3.43 us
  transfers between devices with their start and end apart: 3, of which 3 were waited for; matrix products, arithmetic and copies ran while one was open for 0% of the time, Pallas kernels for 0%

profile of v3, /device:TPU:1, one launch (start us, length us, event | category | flops | bytes accessed | tf_op | source)
XLA Modules:
  0.0 156.2 jit_solution(4907879788462230256)
XLA Ops:
  0.7 0.9 copy-done.4
  1.6 16.0 %all_to_all.35.mine = bf16[4,4,16,256]{3,2,1,0:T(8,128)(2,1)S(1)} all-to-all(bf16[4,4,16,256]{3,2,1,0:T(8,128)(2,1)S(1)} %prepare.1), channel_id=1, replica_groups={{0,2,4,6},{1,3,5,7},{8,10,12,14},{9,11,13,15},{16,18,20,22},{17,19,21,2..., dimensions={0} | all-to-all | bytes 262144 | tf_op jit(solution)/shard_map/all_to_all | solution.py:344
  17.6 3.0 %collective-permute-start = (bf16[4,4,16,256]{3,2,1,0:T(8,128)(2,1)S(1)}, bf16[4,4,16,256]{3,2,1,0:T(8,128)(2,1)S(1)}, u32[]{:S(2)}, u32[]{:S(2)}) collective-permute-start(bf16[4,4,16,256]{3,2,1,0:T(8,128)(2,1)S(1)} %all_to_all.35.mine), channel_id=1, source_target_pairs={{0,1},{1,0},{2,3},{3,2},{4,5},{5,4},{6,7},{7,6},{8,9},{9,8},{10,11... | collective-permute-start | bytes 393224 | tf_op jit(solution)/shard_map/ppermute | solution.py:345
  20.7 0.9 collective-permute-done.other
  21.6 0.8 copy-done.5
  22.4 4.8 %first_forward.1 = (bf16[2560,128]{1,0:T(8,128)(2,1)S(1)}, bf16[2,4,256,2048]{3,2,1,0:T(8,128)(2,1)S(1)}) custom-call(s32[5]{0:T(128)S(1)} %stack.23.place, bf16[4,4,16,256]{3,2,1,0:T(8,128)(2,1)S(1)} %all_to_all.35.mine, bf16[4,4,16,256]{3,2,1,0:T(8,128)(2,1)S(1)} %collective-permute-done.other, f32[2,4,8,256]{3,2,1,0:T(8,128)S(1)} %copy-done.5, ...), custom_call_target="tpu_custom_call" | custom-call | tf_op jit(solution)/shard_map/first_forward/pallas_call | solution.py:143
  27.2 18.4 %all_to_all.36 = bf16[32,80,128]{2,1,0:T(8,128)(2,1)S(1)} all-to-all(bf16[32,80,128]{2,1,0:T(8,128)(2,1)S(1)} %bitcast.24), channel_id=1, replica_groups=mesh['freq'=32,'tile'=8] {'freq'}, dimensions={0} | all-to-all | bytes 1310720 | tf_op jit(solution)/shard_map/all_to_all | solution.py:329
  45.7 1.6 %minus_roundtrip.2 = (f32[64,128]{1,0:T(8,128)S(1)}, f32[64,128]{1,0:T(8,128)S(1)}, f32[128,128]{1,0:T(8,128)S(1)}) custom-call(s32[5]{0:T(128)S(1)} %stack.23.place, bf16[2,224,256]{2,1,0:T(8,128)(2,1)S(1)} %copy-done.3, bf16[32,16,448]{2,1,0:T(8,128)(2,1)S(1)} %copy-done, s32[8,256]{1,0:T(8,128)S(1)} %copy-done.6, bf16[2560,128]{1,0:T(8,128)(2,1)S(1)} %bitcast.17), custom_call_target="tpu_custom_call" | custom-call | tf_op jit(solution)/shard_map/minus_roundtrip/pallas_call | solution.py:229
  47.3 1.3 collective-permute-start.1
  48.6 1.5 collective-permute-done.1.other
  50.1 2.0 %adjoint_product.2 = (bf16[1024,128]{1,0:T(8,128)(2,1)S(1)}, f32[2,4,8,256]{3,2,1,0:T(8,128)}) custom-call(s32[5]{0:T(128)S(1)} %stack.23.place, f32[64,128]{1,0:T(8,128)S(1)} %get-tuple-element.13.mine, f32[64,128]{1,0:T(8,128)S(1)} %collective-permute-done.1.other, bf16[2,4,256,2048]{3,2,1,0:T(8,128)(2,1)S(1)} %get-tuple-element.15.response), custom_call_target="tpu_custom_call" | custom-call | tf_op jit(solution)/shard_map/adjoint_product/pallas_call | solution.py:267
  52.0 24.0 %all_to_all.37 = bf16[256,4,128]{2,1,0:T(4,128)(2,1)S(1)} all-to-all(bf16[256,4,128]{2,1,0:T(4,128)(2,1)S(1)} %bitcast.27), channel_id=1, replica_groups=mesh['freq'=32,'tile'=8] {'tile','freq'}, dimensions={0} | all-to-all | bytes 524288 | tf_op jit(solution)/shard_map/all_to_all | solution.py:329
  76.0 1.0 plus_roundtrip.2
  77.0 20.5 %all_to_all.38 = bf16[256,4,128]{2,1,0:T(4,128)(2,1)S(1)} all-to-all(bf16[256,4,128]{2,1,0:T(4,128)(2,1)S(1)} %bitcast.21), channel_id=1, replica_groups=mesh['freq'=32,'tile'=8] {'tile','freq'}, dimensions={0} | all-to-all | bytes 524288 | tf_op jit(solution)/shard_map/all_to_all | solution.py:329
  97.5 2.3 %forward_product.1 = bf16[2048,128]{1,0:T(8,128)(2,1)S(1)} custom-call(bf16[1024,128]{1,0:T(8,128)(2,1)S(1)} %bitcast.22, bf16[2,4,256,2048]{3,2,1,0:T(8,128)(2,1)S(1)} %get-tuple-element.15.response), custom_call_target="tpu_custom_call" | custom-call | tf_op jit(solution)/shard_map/forward_product/pallas_call | solution.py:176
  99.8 14.0 %all_to_all.39 = bf16[32,64,128]{2,1,0:T(8,128)(2,1)S(1)} all-to-all(bf16[32,64,128]{2,1,0:T(8,128)(2,1)S(1)} %bitcast.19), channel_id=1, replica_groups=mesh['freq'=32,'tile'=8] {'freq'}, dimensions={0} | all-to-all | bytes 1048576 | tf_op jit(solution)/shard_map/all_to_all | solution.py:329
  113.8 1.5 minus_roundtrip.3
  115.3 1.0 collective-permute-start.2
  116.3 2.0 %collective-permute-done.2.other = f32[64,128]{1,0:T(8,128)S(1)} collective-permute-done((f32[64,128]{1,0:T(8,128)S(1)}, f32[64,128]{1,0:T(8,128)S(1)}, u32[]{:S(2)}, u32[]{:S(2)}) %collective-permute-start.2) | collective-permute-done | bytes 32800 | tf_op jit(solution)/shard_map/ppermute | solution.py:355
  118.3 2.0 %adjoint_product.3 = (bf16[1024,128]{1,0:T(8,128)(2,1)S(1)}, f32[2,4,8,256]{3,2,1,0:T(8,128)}) custom-call(s32[5]{0:T(128)S(1)} %stack.23.place, f32[64,128]{1,0:T(8,128)S(1)} %get-tuple-element.18.mine, f32[64,128]{1,0:T(8,128)S(1)} %collective-permute-done.2.other, bf16[2,4,256,2048]{3,2,1,0:T(8,128)(2,1)S(1)} %get-tuple-element.15.response), custom_call_target="tpu_custom_call" | custom-call | tf_op jit(solution)/shard_map/adjoint_product/pallas_call | solution.py:267
  120.2 23.5 %all_to_all.40 = bf16[256,4,128]{2,1,0:T(4,128)(2,1)S(1)} all-to-all(bf16[256,4,128]{2,1,0:T(4,128)(2,1)S(1)} %bitcast.26), channel_id=1, replica_groups=mesh['freq'=32,'tile'=8] {'tile','freq'}, dimensions={0} | all-to-all | bytes 524288 | tf_op jit(solution)/shard_map/all_to_all | solution.py:329
  143.7 1.0 plus_roundtrip.3
  144.7 10.9 %all_to_all.41 = f32[32,4,128]{2,1,0:T(4,128)S(1)} all-to-all(f32[32,4,128]{2,1,0:T(4,128)S(1)} %bitcast.25), channel_id=1, replica_groups=mesh['freq'=32,'tile'=8] {'freq'}, dimensions={0} | all-to-all | bytes 131072 | tf_op jit(solution)/shard_map/all_to_all | solution.py:329
  155.6 0.7 finish.1
  (14 shorter events, 0.1 us)
Async XLA Ops:
  0.6 45.0 %copy-start = (bf16[32,16,448]{2,1,0:T(8,128)(2,1)S(1)}, bf16[32,16,448]{2,1,0:T(8,128)(2,1)}, u32[]{:S(2)}) copy-start(bf16[32,16,448]{2,1,0:T(8,128)(2,1)} %constant.22.clone.own) | copy-start | bytes 1376260
  0.6 45.0 %copy-start.3 = (bf16[2,224,256]{2,1,0:T(8,128)(2,1)S(1)}, bf16[2,224,256]{2,1,0:T(8,128)(2,1)}, u32[]{:S(2)}) copy-start(bf16[2,224,256]{2,1,0:T(8,128)(2,1)} %constant.21.clone.rounded) | copy-start | bytes 688132
  0.7 0.9 copy-start.4
  17.6 4.0 %collective-permute-start = (bf16[4,4,16,256]{3,2,1,0:T(8,128)(2,1)S(1)}, bf16[4,4,16,256]{3,2,1,0:T(8,128)(2,1)S(1)}, u32[]{:S(2)}, u32[]{:S(2)}) collective-permute-start(bf16[4,4,16,256]{3,2,1,0:T(8,128)(2,1)S(1)} %all_to_all.35.mine), channel_id=1, source_target_pairs={{0,1},{1,0},{2,3},{3,2},{4,5},{5,4},{6,7},{7,6},{8,9},{9,8},{10,11... | collective-permute-start | bytes 393224 | tf_op jit(solution)/shard_map/ppermute | solution.py:345
  20.7 55.3 %copy-start.1 = (bf16[2,128,672]{2,1,0:T(8,128)(2,1)S(1)}, bf16[2,128,672]{2,1,0:T(8,128)(2,1)}, u32[]{:S(2)}) copy-start(bf16[2,128,672]{2,1,0:T(8,128)(2,1)} %constant.24.clone.forward) | copy-start | bytes 1032196
  20.7 55.3 %copy-start.2 = (bf16[2,224,384]{2,1,0:T(8,128)(2,1)S(1)}, bf16[2,224,384]{2,1,0:T(8,128)(2,1)}, u32[]{:S(2)}) copy-start(bf16[2,224,384]{2,1,0:T(8,128)(2,1)} %constant.23.clone.inverse) | copy-start | bytes 1032196
  21.6 0.8 copy-start.5
  22.4 23.3 %copy-start.6 = (s32[8,256]{1,0:T(8,128)S(1)}, s32[8,256]{1,0:T(8,128)}, u32[]{:S(2)}) copy-start(s32[8,256]{1,0:T(8,128)} %onset.7) | copy-start | bytes 24580
  47.3 2.8 %collective-permute-start.1 = (f32[64,128]{1,0:T(8,128)S(1)}, f32[64,128]{1,0:T(8,128)S(1)}, u32[]{:S(2)}, u32[]{:S(2)}) collective-permute-start(f32[64,128]{1,0:T(8,128)S(1)} %get-tuple-element.14), channel_id=1, source_target_pairs={{0,128},{8,136},{16,144},{24,152},{32,160},{40,168},{48,176},{56,1... | collective-permute-start | bytes 98312 | tf_op jit(solution)/shard_map/ppermute | solution.py:355
  115.3 3.0 %collective-permute-start.2 = (f32[64,128]{1,0:T(8,128)S(1)}, f32[64,128]{1,0:T(8,128)S(1)}, u32[]{:S(2)}, u32[]{:S(2)}) collective-permute-start(f32[64,128]{1,0:T(8,128)S(1)} %get-tuple-element.19), channel_id=1, source_target_pairs={{0,128},{8,136},{16,144},{24,152},{32,160},{40,168},{48,176},{56,1... | collective-permute-start | bytes 98312 | tf_op jit(solution)/shard_map/ppermute | solution.py:355

commit v4 on v3

--- a/solution.py
+++ b/solution.py
@@ -67,28 +67,52 @@
     return pltpu.with_memory_space_constraint(array, pltpu.VMEM)
 
 
+def in_hbm(array):
+    return pltpu.with_memory_space_constraint(array, pltpu.HBM)
+
+
 VMEM = pl.BlockSpec(memory_space=pltpu.VMEM)
-SMEM = pl.BlockSpec(memory_space=pltpu.SMEM)
+HBM = pl.BlockSpec(memory_space=pltpu.HBM)
 PARAMS = pltpu.CompilerParams(vmem_limit_bytes=VMEM_LIMIT)
 
 
-def prepare_kernel(direct, out):
-    for bin_ in range(direct.shape[1]):
-        value = jnp.concatenate([direct[0, bin_], direct[1, bin_]], axis=0).astype(BF16)
-        for copy in range(out.shape[0]):
-            out[copy, bin_] = value
-
-
-def prepare(direct, copies):
-    parts, bins, focal, positions = direct.shape
+def hold_kernel(response, held, done):
+    copy = pltpu.make_async_copy(response, held, done)
+    copy.start()
+    copy.wait()
+
+
+def hold(response):
+    return pl.pallas_call(
+        hold_kernel,
+        out_shape=pltpu.VMEM(response.shape, response.dtype),
+        in_specs=[HBM],
+        out_specs=VMEM,
+        scratch_shapes=[pltpu.SemaphoreType.DMA],
+        compiler_params=PARAMS,
+        cost_estimate=pl.CostEstimate(flops=0, bytes_accessed=4 * response.size, transcendentals=0),
+        name="hold",
+    )(in_hbm(response))
+
+
+def prepare_kernel(mine, other, out):
+    even = lax.axis_index("core") == 0
+    for bin_ in range(mine.shape[1]):
+        here, there = (jnp.concatenate([direct[0, bin_], direct[1, bin_]], axis=0) for direct in (mine, other))
+        out[0, bin_] = jnp.where(even, here, there).astype(BF16)
+        out[1, bin_] = jnp.where(even, there, here).astype(BF16)
+
+
+def prepare(mine, other):
+    parts, bins, focal, positions = mine.shape
     return pl.pallas_call(
         prepare_kernel,
-        out_shape=jax.ShapeDtypeStruct((copies, bins, parts * focal, positions), BF16),
-        in_specs=[VMEM],
+        out_shape=jax.ShapeDtypeStruct((2, bins, parts * focal, positions), BF16),
+        in_specs=[VMEM, VMEM],
         out_specs=VMEM,
         compiler_params=PARAMS,
         name="prepare",
-    )(direct)
+    )(mine, other)
 
 
 def forward_dots(stacked, response, bin_):
@@ -106,18 +130,9 @@
             out[start : start + 16, :] = tile
 
 
-def first_forward_kernel(place, mine, other, direct, response, out, kept, held, done):
-    bins = response.shape[1]
-    copies = [
-        [pltpu.make_async_copy(response.at[part, bin_], kept.at[part, bin_], done.at[part, bin_]) for part in range(2)]
-        for bin_ in range(bins)
-    ]
-    for both in copies:
-        for copy in both:
-            copy.start()
-    stride = SHARED + PIECES
+def spread_direct(direct, held, out, stride):
     held[...] = jnp.zeros_like(held)
-    for bin_ in range(bins):
+    for bin_ in range(direct.shape[1]):
         for half in range(2):
             for part in range(2):
                 value = direct[part, bin_, :, half * LANES : (half + 1) * LANES]
@@ -127,42 +142,55 @@
     for owner in range(OWNERS):
         start = owner * stride + SHARED
         out[start : start + PIECES, :] = held[owner * PIECES : (owner + 1) * PIECES, :].astype(BF16)
-    even = place[3] == 0
-    for bin_ in range(bins):
-        columns = []
-        for pair in range(mine.shape[0]):
-            here, there = mine[pair, bin_], other[pair, bin_]
-            columns.append(jnp.where(even, here, there))
-            columns.append(jnp.where(even, there, here))
-        for copy in copies[bin_]:
-            copy.wait()
-        share(forward_dots(jnp.concatenate(columns, axis=1), kept, bin_), bin_, out, stride)
-
-
-def first_forward(place, mine, other, direct, response):
+
+
+def first_forward_kernel(*refs):
+    *gathered, direct, response, out, near, stacked, held, near_done = refs
+    fetch = pltpu.make_async_copy(direct, near, near_done)
+    fetch.start()
+    stride = SHARED + PIECES
+    pairs = len(gathered)
+    positions = gathered[0].shape[3]
+    for shift in range(pairs):
+        pair = (lax.axis_index("pair") - shift + pairs) & (pairs - 1)
+        for core in range(2):
+            start = pl.multiple_of((2 * pair + core) * positions, positions)
+            for bin_ in range(response.shape[1]):
+                stacked[bin_, :, pl.ds(start, positions)] = gathered[shift][core, bin_]
+    for bin_ in range(response.shape[1]):
+        share(forward_dots(stacked[bin_], response, bin_), bin_, out, stride)
+    fetch.wait()
+    spread_direct(near, held, out, stride)
+
+
+def first_forward(gathered, direct, response):
+    bins, sources = response.shape[1], response.shape[3]
     return pl.pallas_call(
         first_forward_kernel,
-        out_shape=(
-            jax.ShapeDtypeStruct((OWNERS * (SHARED + PIECES), LANES), BF16),
-            pltpu.VMEM(response.shape, response.dtype),
-        ),
-        in_specs=[SMEM, VMEM, VMEM, VMEM, pl.BlockSpec(memory_space=pltpu.HBM)],
-        out_specs=(VMEM, VMEM),
+        out_shape=jax.ShapeDtypeStruct((OWNERS * (SHARED + PIECES), LANES), BF16),
+        in_specs=[VMEM] * len(gathered) + [HBM, VMEM],
+        out_specs=VMEM,
         scratch_shapes=[
+            pltpu.VMEM(direct.shape, F32),
+            pltpu.VMEM((bins, 2 * FP, sources), BF16),
             pltpu.VMEM((OWNERS * PIECES, LANES), F32),
-            pltpu.SemaphoreType.DMA(response.shape[:2]),
+            pltpu.SemaphoreType.DMA,
         ],
         compiler_params=PARAMS,
         name="first_forward",
-    )(place, mine, other, direct, pltpu.with_memory_space_constraint(response, pltpu.HBM))
-
-
-def forward_kernel(update, response, out, held):
-    held[...] = update[...].astype(F32)
-    tiles = update.shape[0] // NF
+    )(*gathered, in_hbm(direct), in_vmem(response))
+
+
+def forward_kernel(mine, other, response, out, held):
+    own_core = lax.axis_index("core")
+    pairs = mine.shape[0] // NF
+    for pair in range(pairs):
+        for source, core in ((mine, own_core), (other, 1 - own_core)):
+            start = pl.multiple_of((2 * pair + core) * NF, NF)
+            held[pl.ds(start, NF), :] = source[pair * NF : (pair + 1) * NF, :].astype(F32)
     for bin_ in range(response.shape[1]):
         columns = []
-        for tile in range(tiles):
+        for tile in range(2 * pairs):
             for half in range(2):
                 both = []
                 for part in range(2):
@@ -172,25 +200,26 @@
         share(forward_dots(jnp.concatenate(columns, axis=1), response, bin_), bin_, out, SHARED)
 
 
-def forward_product(update, response):
+def forward_product(mine, other, response):
     return pl.pallas_call(
         forward_kernel,
         out_shape=jax.ShapeDtypeStruct((OWNERS * SHARED, LANES), BF16),
-        in_specs=[VMEM, VMEM],
-        out_specs=VMEM,
-        scratch_shapes=[pltpu.VMEM(update.shape, F32)],
+        in_specs=[VMEM] * 3,
+        out_specs=VMEM,
+        scratch_shapes=[pltpu.VMEM((2 * mine.shape[0], LANES), F32)],
         compiler_params=PARAMS,
         name="forward_product",
-    )(update, in_vmem(response))
-
-
-def minus_kernel(stride, place, rounded, own, onset, blocks, mine, other, *refs):
+    )(mine, other, in_vmem(response))
+
+
+def minus_kernel(stride, rounded, own, onset, blocks, mine, other, *refs):
     *owned, spectra = refs
     for owner in range(OWNERS):
         start = owner * stride
         spectra[owner * SHARED : (owner + 1) * SHARED, :] = blocks[start : start + SHARED, :].astype(F32)
-    inverse = rounded[place[4] // (OWNERS // 2)]
-    forward = own[place[4]]
+    device = lax.axis_index("freq")
+    inverse = rounded[device >> 4]
+    forward = own[device]
     wide = 2
     for half in range(2):
         lanes = slice(half * LANES, (half + 1) * LANES)
@@ -221,7 +250,7 @@
             owned[pl.ds(bin_, OWNERS, stride=4), :] = high + low
 
 
-def minus_roundtrip(place, rounded, own, onset, blocks, carried):
+def minus_roundtrip(rounded, own, onset, blocks, carried):
     stride = SHARED + PIECES if carried else SHARED
     out_shape = [jax.ShapeDtypeStruct((SHARED, LANES), F32)] * 2
     if carried:
@@ -229,16 +258,16 @@
     return pl.pallas_call(
         functools.partial(minus_kernel, stride),
         out_shape=out_shape,
-        in_specs=[SMEM] + [VMEM] * 4,
+        in_specs=[VMEM] * 4,
         out_specs=[VMEM] * len(out_shape),
         scratch_shapes=[pltpu.VMEM((OWNERS * SHARED, LANES), F32)],
         compiler_params=PARAMS,
         name="minus_roundtrip",
-    )(place, rounded, own, onset, blocks)
-
-
-def adjoint_kernel(place, mine, other, response, out, minus, held):
-    lower = place[4] < OWNERS // 2
+    )(rounded, own, onset, blocks)
+
+
+def adjoint_kernel(mine, other, response, out, minus, held):
+    lower = lax.axis_index("freq") < OWNERS // 2
     tiles = response.shape[3] // (2 * LANES)
     for bin_ in range(response.shape[1]):
         here, there = (
@@ -261,7 +290,7 @@
     out[...] = held[...].astype(out.dtype)
 
 
-def adjoint_product(place, mine, other, response):
+def adjoint_product(mine, other, response):
     bins, receivers, sources = response.shape[1:]
     rows = NF * sources // (2 * LANES)
     return pl.pallas_call(
@@ -270,39 +299,41 @@
             jax.ShapeDtypeStruct((rows, LANES), BF16),
             jax.ShapeDtypeStruct((2, bins, FP, receivers), F32),
         ),
-        in_specs=[SMEM] + [VMEM] * 3,
+        in_specs=[VMEM] * 3,
         out_specs=(VMEM, VMEM),
         scratch_shapes=[pltpu.VMEM((rows, LANES), F32)],
         compiler_params=PARAMS,
         name="adjoint_product",
-    )(place, mine, other, in_vmem(response))
-
-
-def plus_kernel(place, inverse, forward, onset, blocks, direct, out):
+    )(mine, other, in_vmem(response))
+
+
+def plus_kernel(inverse, forward, onset, blocks, direct, out):
+    device = lax.axis_index("freq")
+    part, own_half, own_focal = device & 1, (device >> 1) & 1, device >> 2
     spectrum = blocks[:NF, :].astype(F32)
     for tile in range(1, blocks.shape[0] // NF):
         spectrum += blocks[tile * NF : (tile + 1) * NF, :].astype(F32)
-    signal = jnp.dot(inverse[place[0]], pieces(spectrum), preferred_element_type=F32)
-    limits = jnp.where(place[2] == 0, onset[:, :LANES], onset[:, LANES:])
+    signal = jnp.dot(inverse[part], pieces(spectrum), preferred_element_type=F32)
+    limits = jnp.where(own_half == 0, onset[:, :LANES], onset[:, LANES:])
     focal = lax.broadcasted_iota(jnp.int32, limits.shape, 0)
-    limit = jnp.sum(jnp.where(focal == place[1], limits, 0), axis=0, keepdims=True)
+    limit = jnp.sum(jnp.where(focal == own_focal, limits, 0), axis=0, keepdims=True)
     lag = lax.broadcasted_iota(jnp.int32, signal.shape, 0)
     signal = jnp.where(lag < limit, signal, 0.0)
-    result = jnp.dot(forward[place[0]], pieces(signal), preferred_element_type=F32)
+    result = jnp.dot(forward[part], pieces(signal), preferred_element_type=F32)
     result = (direct[...] + result).astype(out.dtype)
     for copy in range(out.shape[0] // NF):
         out[copy * NF : (copy + 1) * NF, :] = result
 
 
-def plus_roundtrip(place, inverse, forward, onset, blocks, direct, copies, dtype):
+def plus_roundtrip(inverse, forward, onset, blocks, direct, copies, dtype):
     return pl.pallas_call(
         plus_kernel,
         out_shape=jax.ShapeDtypeStruct((copies * NF, LANES), dtype),
-        in_specs=[SMEM] + [VMEM] * 5,
+        in_specs=[VMEM] * 5,
         out_specs=VMEM,
         compiler_params=PARAMS,
         name="plus_roundtrip",
-    )(place, inverse, forward, onset, blocks, direct)
+    )(inverse, forward, onset, blocks, direct)
 
 
 def finish_kernel(blocks, out):
@@ -330,45 +361,45 @@
 
 
 def on_device(response, direct, onset):
-    groups = lax.axis_size("freq")
-    tiles = lax.axis_size("tile")
-    everyone = ("tile", "freq")
-    own = lax.axis_index("freq")
-    place = [own & 1, own >> 2, (own >> 1) & 1, lax.axis_index("tile") & 1, own]
-    place = jnp.stack(place).astype(jnp.int32)
+    groups, pairs, cores = (lax.axis_size(axis) for axis in ("freq", "pair", "core"))
     rounded, own_bins, inverse, forward = (jnp.asarray(table) for table in tables())
-    pairs = tiles // 2
-    chips = [[core + 2 * pair for pair in range(pairs)] for core in range(2)]
-    cores = [(tile, tile ^ 1) for tile in range(tiles)]
+    other_core = functools.partial(lax.ppermute, axis_name="core", perm=[(0, 1), (1, 0)])
     partners = [(owner, owner ^ (OWNERS // 2)) for owner in range(OWNERS)]
-    mine = lax.all_to_all(prepare(direct, pairs), "tile", 0, 0, axis_index_groups=chips, tiled=True)
-    other = lax.ppermute(mine, "tile", cores)
+    chip = prepare(direct, other_core(direct))
+    gathered = [chip]
+    for shift in range(1, pairs):
+        gathered.append(lax.ppermute(chip, "pair", [(pair, (pair + shift) % pairs) for pair in range(pairs)]))
+    held = hold(response)
     for step in range(ITERS):
         if step == 0:
-            upgoing, held = first_forward(place, mine, other, direct, response)
+            upgoing = first_forward(gathered, direct, held)
         else:
-            upgoing = forward_product(update, held)
+            upgoing = forward_product(mine, other, held)
         upgoing = exchange(upgoing, "freq", groups)
-        mine, other, *owned = minus_roundtrip(place, rounded, own_bins, onset, upgoing, step == 0)
+        mine, other, *owned = minus_roundtrip(rounded, own_bins, onset, upgoing, step == 0)
         if step == 0:
             (direct_columns,) = owned
-        partial, minus = adjoint_product(place, mine, lax.ppermute(other, "freq", partners), held)
-        partial = exchange(partial, everyone, groups * tiles)
+        partial, minus = adjoint_product(mine, lax.ppermute(other, "freq", partners), held)
+        partial = exchange(partial, ("pair", "core", "freq"), pairs * cores * groups)
         last = step + 1 == ITERS
-        copies, dtype = (1, F32) if last else (tiles, BF16)
-        plus = plus_roundtrip(place, inverse, forward, onset, partial, direct_columns, copies, dtype)
+        copies, dtype = (1, F32) if last else (pairs, BF16)
+        plus = plus_roundtrip(inverse, forward, onset, partial, direct_columns, copies, dtype)
         if last:
             plus = finish(exchange(plus, "freq", groups), direct.shape)
         else:
-            update = exchange(plus, everyone, groups * tiles)
+            mine = exchange(plus, ("pair", "freq"), pairs * groups)
+            other = other_core(mine)
     return (minus, plus)
 
 
 def solution(mesh):
+    groups, tiles = mesh.devices.shape
+    devices = mesh.devices.reshape(groups, tiles // 2, 2)
+    tile = ("pair", "core")
     return jax.shard_map(
         on_device,
-        mesh=mesh,
-        in_specs=(P(None, "freq", "tile", None), P(None, "freq", None, "tile"), P(None, "tile")),
-        out_specs=(P(None, "freq", None, "tile"), P(None, "freq", None, "tile")),
+        mesh=jax.sharding.Mesh(devices, ("freq",) + tile),
+        in_specs=(P(None, "freq", tile, None), P(None, "freq", None, tile), P(None, tile)),
+        out_specs=(P(None, "freq", None, tile), P(None, "freq", None, tile)),
         check_vma=False,
     )

time: 157 us -> 150 us (0.955)
  blocking collectives: 127 us -> 111 us
  starting transfers between devices: 5.34 us -> 15.2 us
  waiting for transfers between devices: 4.33 us -> 6.91 us
  Pallas kernels: 16.8 us -> 14.6 us
    all_to_all x1 -> x0, blocking collectives: 16 us -> none  [on_device(): lax.all_to_all(prepare(direct, pairs), 'tile', 0, 0, axis_index_groups=ch...]
    ppermute x1 -> x5, starting transfers between devices: 2.97 us -> 13.2 us  [the longest x3 7.62 us: on_device(): lax.ppermute(chip, 'pair', [(pair, (pair + shift) % pairs) for pair in ra...]
    ppermute x1 -> x5, waiting for transfers between devices: 0.9 us -> 3.36 us  [the longest x3 1.26 us: on_device(): lax.ppermute(chip, 'pair', [(pair, (pair + shift) % pairs) for pair in ra...]
    pallas_call x2 -> x3, Pallas kernels: 4.84 us -> 6.02 us  [the longest x1 3.39 us: hold(): pl.pallas_call(hold_kernel, out_shape=pltpu.VMEM(response.shape, response...]
  transfers between devices with their start and end apart: 3 -> 7, of which waited for: 3 -> 6; matrix products, arithmetic and copies ran while one was open for 0% -> 0% of each run, Pallas kernels for 0% -> 2%
where the time goes in v4:
time: 150 us
  blocking collectives  111 us (74%)
  starting transfers between devices  15.2 us (10%)
  Pallas kernels  14.6 us (10%)
  waiting for transfers between devices  6.91 us (5%)
    all_to_all x6, blocking collectives, exchange(): return lax.all_to_all(shaped, axes, 0, 0, tiled=True).reshape(blocks.shape)  111 us
    ppermute x3, starting transfers between devices, on_device(): lax.ppermute(chip, 'pair', [(pair, (pair + shift) % pairs) for pair in ra...  7.62 us
    ppermute x2, waiting for transfers between devices, on_device(): lax.ppermute(other, 'freq', partners)  3.55 us
    pallas_call x1, Pallas kernels, hold(): pl.pallas_call(hold_kernel, out_shape=pltpu.VMEM(response.shape, response...  3.39 us
    ppermute x1, starting transfers between devices, on_device(): chip = prepare(direct, other_core(direct))  3.33 us
  transfers between devices with their start and end apart: 7, of which 6 were waited for; matrix products, arithmetic and copies ran while one was open for 0% of the time, Pallas kernels for 2%

profile of v4, /device:TPU:1, one launch (start us, length us, event | category | flops | bytes accessed | tf_op | source)
XLA Modules:
  0.0 149.8 jit_solution(14636738439770793811)
XLA Ops:
  0.6 3.3 %collective-permute-start = (f32[2,4,8,256]{3,2,1,0:T(8,128)}, f32[2,4,8,256]{3,2,1,0:T(8,128)S(1)}, u32[]{:S(2)}, u32[]{:S(2)}) collective-permute-start(f32[2,4,8,256]{3,2,1,0:T(8,128)} %refs_4_.1), channel_id=1, source_target_pairs={{0,1},{1,0},{2,3},{3,2},{4,5},{5,4},{6,7},{7,6},{8,9},{9,8},{10,11... | collective-permute-start | bytes 196616 | tf_op jit(solution)/shard_map/ppermute | solution.py:368
  4.0 1.1 collective-permute-done.other
  5.9 4.4 %collective-permute-start.3 = (bf16[2,4,16,256]{3,2,1,0:T(8,128)(2,1)S(1)}, bf16[2,4,16,256]{3,2,1,0:T(8,128)(2,1)S(1)}, u32[]{:S(2)}, u32[]{:S(2)}) collective-permute-start(bf16[2,4,16,256]{3,2,1,0:T(8,128)(2,1)S(1)} %prepare.1.refs_0_), channel_id=1, source_target_pairs={{0,6},{2,0},{4,2},{6,4},{1,7},{3,1},{5,3},{7,5},{8,14},{10,8},{12,... | collective-permute-start | bytes 196616 | tf_op jit(solution)/shard_map/ppermute | solution.py:371
  10.3 1.0 collective-permute-start.2
  11.3 2.3 %collective-permute-start.1 = (bf16[2,4,16,256]{3,2,1,0:T(8,128)(2,1)S(1)}, bf16[2,4,16,256]{3,2,1,0:T(8,128)(2,1)S(1)}, u32[]{:S(2)}, u32[]{:S(2)}) collective-permute-start(bf16[2,4,16,256]{3,2,1,0:T(8,128)(2,1)S(1)} %prepare.1.refs_0_), channel_id=1, source_target_pairs={{0,2},{2,4},{4,6},{6,0},{1,3},{3,5},{5,7},{7,1},{8,10},{10,12},{12... | collective-permute-start | bytes 196616 | tf_op jit(solution)/shard_map/ppermute | solution.py:371
  13.5 3.4 %hold.1.refs_5_.response = bf16[2,4,256,2048]{3,2,1,0:T(8,128)(2,1)S(1)} custom-call(bf16[2,4,256,2048]{3,2,1,0:T(8,128)(2,1)} %response.1), custom_call_target="tpu_custom_call" | custom-call | bytes 16777216 | tf_op jit(solution)/shard_map/hold/pallas_call | solution.py:86
  18.3 2.6 %first_forward.1 = bf16[2560,128]{1,0:T(8,128)(2,1)S(1)} custom-call(bf16[2,4,16,256]{3,2,1,0:T(8,128)(2,1)S(1)} %prepare.1.refs_0_, bf16[2,4,16,256]{3,2,1,0:T(8,128)(2,1)S(1)} %collective-permute-done.1.refs_1_, bf16[2,4,16,256]{3,2,1,0:T(8,128)(2,1)S(1)} %collective-permute-done.2.refs_2_, bf16[2,4,16,256]{3,2,1,0:T(8,128)(2,1)S(1)} %collective-permute-done.3.refs_3_, ...), custom_call_target="tpu_custom_call" | custom-call | tf_op jit(solution)/shard_map/first_forward/pallas_call | solution.py:168
  20.9 17.8 %all_to_all.30 = bf16[32,80,128]{2,1,0:T(8,128)(2,1)S(1)} all-to-all(bf16[32,80,128]{2,1,0:T(8,128)(2,1)S(1)} %bitcast.12), channel_id=1, replica_groups=mesh['freq'=32,'pair'=4,'core'=2] {'freq'}, dimensions={0} | all-to-all | bytes 1310720 | tf_op jit(solution)/shard_map/all_to_all | solution.py:360
  38.7 1.0 minus_roundtrip.2
  39.7 1.1 collective-permute-start.4
  40.9 1.7 %collective-permute-done.4.other = f32[64,128]{1,0:T(8,128)S(1)} collective-permute-done((f32[64,128]{1,0:T(8,128)S(1)}, f32[64,128]{1,0:T(8,128)S(1)}, u32[]{:S(2)}, u32[]{:S(2)}) %collective-permute-start.4) | collective-permute-done | bytes 32800 | tf_op jit(solution)/shard_map/ppermute | solution.py:382
  42.6 1.4 adjoint_product.2
  44.0 28.9 %all_to_all.31 = bf16[256,4,128]{2,1,0:T(4,128)(2,1)S(1)} all-to-all(bf16[256,4,128]{2,1,0:T(4,128)(2,1)S(1)} %bitcast.23), channel_id=1, replica_groups=mesh['freq'=32,'pair'=4,'core'=2] {'pair','core','freq'}, dimensions={0} | all-to-all | bytes 524288 | tf_op jit(solution)/shard_map/all_to_all | solution.py:360
  73.3 17.0 %all_to_all.32 = bf16[128,4,128]{2,1,0:T(4,128)(2,1)S(1)} all-to-all(bf16[128,4,128]{2,1,0:T(4,128)(2,1)S(1)} %bitcast.20), channel_id=1, replica_groups=mesh['freq'=32,'pair'=4,'core'=2] {'pair','freq'}, dimensions={0} | all-to-all | bytes 262144 | tf_op jit(solution)/shard_map/all_to_all | solution.py:360
  90.3 2.2 %collective-permute-start.5 = (bf16[512,128]{1,0:T(8,128)(2,1)S(1)}, bf16[512,128]{1,0:T(8,128)(2,1)S(1)}, u32[]{:S(2)}, u32[]{:S(2)}) collective-permute-start(bf16[512,128]{1,0:T(8,128)(2,1)S(1)} %bitcast.18), channel_id=1, source_target_pairs={{0,1},{1,0},{2,3},{3,2},{4,5},{5,4},{6,7},{7,6},{8,9},{9,8},{10,11... | collective-permute-start | bytes 393224 | tf_op jit(solution)/shard_map/ppermute | solution.py:391
  92.5 1.0 collective-permute-done.5.other
  93.5 2.3 %forward_product.1 = bf16[2048,128]{1,0:T(8,128)(2,1)S(1)} custom-call(bf16[512,128]{1,0:T(8,128)(2,1)S(1)} %bitcast.19, bf16[512,128]{1,0:T(8,128)(2,1)S(1)} %collective-permute-done.5.other, bf16[2,4,256,2048]{3,2,1,0:T(8,128)(2,1)S(1)} %hold.1.refs_5_.response), custom_call_target="tpu_custom_call" | custom-call | tf_op jit(solution)/shard_map/forward_product/pallas_call | solution.py:204
  95.8 13.5 %all_to_all.33 = bf16[32,64,128]{2,1,0:T(8,128)(2,1)S(1)} all-to-all(bf16[32,64,128]{2,1,0:T(8,128)(2,1)S(1)} %bitcast.14), channel_id=1, replica_groups=mesh['freq'=32,'pair'=4,'core'=2] {'freq'}, dimensions={0} | all-to-all | bytes 1048576 | tf_op jit(solution)/shard_map/all_to_all | solution.py:360
  109.3 0.9 minus_roundtrip.3
  110.2 0.9 collective-permute-start.6
  111.2 1.9 %collective-permute-done.6.other = f32[64,128]{1,0:T(8,128)S(1)} collective-permute-done((f32[64,128]{1,0:T(8,128)S(1)}, f32[64,128]{1,0:T(8,128)S(1)}, u32[]{:S(2)}, u32[]{:S(2)}) %collective-permute-start.6) | collective-permute-done | bytes 32800 | tf_op jit(solution)/shard_map/ppermute | solution.py:382
  113.1 1.4 adjoint_product.3
  114.5 23.3 %all_to_all.34 = bf16[256,4,128]{2,1,0:T(4,128)(2,1)S(1)} all-to-all(bf16[256,4,128]{2,1,0:T(4,128)(2,1)S(1)} %bitcast.22), channel_id=1, replica_groups=mesh['freq'=32,'pair'=4,'core'=2] {'pair','core','freq'}, dimensions={0} | all-to-all | bytes 524288 | tf_op jit(solution)/shard_map/all_to_all | solution.py:360
  138.2 10.9 %all_to_all.35 = f32[32,4,128]{2,1,0:T(4,128)S(1)} all-to-all(f32[32,4,128]{2,1,0:T(4,128)S(1)} %bitcast.21), channel_id=1, replica_groups=mesh['freq'=32,'pair'=4,'core'=2] {'freq'}, dimensions={0} | all-to-all | bytes 131072 | tf_op jit(solution)/shard_map/all_to_all | solution.py:360
  (19 shorter events, 3.7 us)
Async XLA Ops:
  0.6 4.4 %collective-permute-start = (f32[2,4,8,256]{3,2,1,0:T(8,128)}, f32[2,4,8,256]{3,2,1,0:T(8,128)S(1)}, u32[]{:S(2)}, u32[]{:S(2)}) collective-permute-start(f32[2,4,8,256]{3,2,1,0:T(8,128)} %refs_4_.1), channel_id=1, source_target_pairs={{0,1},{1,0},{2,3},{3,2},{4,5},{5,4},{6,7},{7,6},{8,9},{9,8},{10,11... | collective-permute-start | bytes 196616 | tf_op jit(solution)/shard_map/ppermute | solution.py:368
  5.1 0.8 copy-start.4
  5.9 11.1 %collective-permute-start.3 = (bf16[2,4,16,256]{3,2,1,0:T(8,128)(2,1)S(1)}, bf16[2,4,16,256]{3,2,1,0:T(8,128)(2,1)S(1)}, u32[]{:S(2)}, u32[]{:S(2)}) collective-permute-start(bf16[2,4,16,256]{3,2,1,0:T(8,128)(2,1)S(1)} %prepare.1.refs_0_), channel_id=1, source_target_pairs={{0,6},{2,0},{4,2},{6,4},{1,7},{3,1},{5,3},{7,5},{8,14},{10,8},{12,... | collective-permute-start | bytes 196616 | tf_op jit(solution)/shard_map/ppermute | solution.py:371
  10.3 7.2 %collective-permute-start.2 = (bf16[2,4,16,256]{3,2,1,0:T(8,128)(2,1)S(1)}, bf16[2,4,16,256]{3,2,1,0:T(8,128)(2,1)S(1)}, u32[]{:S(2)}, u32[]{:S(2)}) collective-permute-start(bf16[2,4,16,256]{3,2,1,0:T(8,128)(2,1)S(1)} %prepare.1.refs_0_), channel_id=1, source_target_pairs={{0,4},{2,6},{4,0},{6,2},{1,5},{3,7},{5,1},{7,3},{8,12},{10,14},{12... | collective-permute-start | bytes 196616 | tf_op jit(solution)/shard_map/ppermute | solution.py:371
  11.3 7.0 %collective-permute-start.1 = (bf16[2,4,16,256]{3,2,1,0:T(8,128)(2,1)S(1)}, bf16[2,4,16,256]{3,2,1,0:T(8,128)(2,1)S(1)}, u32[]{:S(2)}, u32[]{:S(2)}) collective-permute-start(bf16[2,4,16,256]{3,2,1,0:T(8,128)(2,1)S(1)} %prepare.1.refs_0_), channel_id=1, source_target_pairs={{0,2},{2,4},{4,6},{6,0},{1,3},{3,5},{5,7},{7,1},{8,10},{10,12},{12... | collective-permute-start | bytes 196616 | tf_op jit(solution)/shard_map/ppermute | solution.py:371
  16.9 21.8 %copy-start = (bf16[32,16,448]{2,1,0:T(8,128)(2,1)S(1)}, bf16[32,16,448]{2,1,0:T(8,128)(2,1)}, u32[]{:S(2)}) copy-start(bf16[32,16,448]{2,1,0:T(8,128)(2,1)} %constant.9.clone.own) | copy-start | bytes 1376260
  17.0 21.8 %copy-start.3 = (bf16[2,224,256]{2,1,0:T(8,128)(2,1)S(1)}, bf16[2,224,256]{2,1,0:T(8,128)(2,1)}, u32[]{:S(2)}) copy-start(bf16[2,224,256]{2,1,0:T(8,128)(2,1)} %constant.8.clone.rounded) | copy-start | bytes 688132
  17.0 21.8 %copy-start.5 = (s32[8,256]{1,0:T(8,128)S(1)}, s32[8,256]{1,0:T(8,128)}, u32[]{:S(2)}) copy-start(s32[8,256]{1,0:T(8,128)} %onset.7) | copy-start | bytes 24580
  17.0 55.9 %copy-start.1 = (bf16[2,128,672]{2,1,0:T(8,128)(2,1)S(1)}, bf16[2,128,672]{2,1,0:T(8,128)(2,1)}, u32[]{:S(2)}) copy-start(bf16[2,128,672]{2,1,0:T(8,128)(2,1)} %constant.11.clone.forward) | copy-start | bytes 1032196
  17.0 55.9 %copy-start.2 = (bf16[2,224,384]{2,1,0:T(8,128)(2,1)S(1)}, bf16[2,224,384]{2,1,0:T(8,128)(2,1)}, u32[]{:S(2)}) copy-start(bf16[2,224,384]{2,1,0:T(8,128)(2,1)} %constant.10.clone.inverse) | copy-start | bytes 1032196
  39.7 2.8 %collective-permute-start.4 = (f32[64,128]{1,0:T(8,128)S(1)}, f32[64,128]{1,0:T(8,128)S(1)}, u32[]{:S(2)}, u32[]{:S(2)}) collective-permute-start(f32[64,128]{1,0:T(8,128)S(1)} %get-tuple-element.11), channel_id=1, source_target_pairs={{0,128},{8,136},{16,144},{24,152},{32,160},{40,168},{48,176},{56,1... | collective-permute-start | bytes 98312 | tf_op jit(solution)/shard_map/ppermute | solution.py:382
  90.3 3.2 %collective-permute-start.5 = (bf16[512,128]{1,0:T(8,128)(2,1)S(1)}, bf16[512,128]{1,0:T(8,128)(2,1)S(1)}, u32[]{:S(2)}, u32[]{:S(2)}) collective-permute-start(bf16[512,128]{1,0:T(8,128)(2,1)S(1)} %bitcast.18), channel_id=1, source_target_pairs={{0,1},{1,0},{2,3},{3,2},{4,5},{5,4},{6,7},{7,6},{8,9},{9,8},{10,11... | collective-permute-start | bytes 393224 | tf_op jit(solution)/shard_map/ppermute | solution.py:391
  110.2 2.8 %collective-permute-start.6 = (f32[64,128]{1,0:T(8,128)S(1)}, f32[64,128]{1,0:T(8,128)S(1)}, u32[]{:S(2)}, u32[]{:S(2)}) collective-permute-start(f32[64,128]{1,0:T(8,128)S(1)} %get-tuple-element.15), channel_id=1, source_target_pairs={{0,128},{8,136},{16,144},{24,152},{32,160},{40,168},{48,176},{56,1... | collective-permute-start | bytes 98312 | tf_op jit(solution)/shard_map/ppermute | solution.py:382

commit v5 on v4

--- a/solution.py
+++ b/solution.py
@@ -95,24 +95,39 @@
     )(in_hbm(response))
 
 
-def prepare_kernel(mine, other, out):
-    even = lax.axis_index("core") == 0
-    for bin_ in range(mine.shape[1]):
-        here, there = (jnp.concatenate([direct[0, bin_], direct[1, bin_]], axis=0) for direct in (mine, other))
-        out[0, bin_] = jnp.where(even, here, there).astype(BF16)
-        out[1, bin_] = jnp.where(even, there, here).astype(BF16)
-
-
-def prepare(mine, other):
-    parts, bins, focal, positions = mine.shape
+def prepare_kernel(direct, out):
+    for bin_ in range(direct.shape[1]):
+        out[bin_] = jnp.concatenate([direct[0, bin_], direct[1, bin_]], axis=0).astype(BF16)
+
+
+def prepare(direct):
+    parts, bins, focal, positions = direct.shape
     return pl.pallas_call(
         prepare_kernel,
-        out_shape=jax.ShapeDtypeStruct((2, bins, parts * focal, positions), BF16),
-        in_specs=[VMEM, VMEM],
+        out_shape=jax.ShapeDtypeStruct((bins, parts * focal, positions), BF16),
+        in_specs=[VMEM],
         out_specs=VMEM,
         compiler_params=PARAMS,
         name="prepare",
-    )(mine, other)
+    )(direct)
+
+
+def order_kernel(*refs):
+    *shifted, _, out = refs
+    pairs = len(shifted)
+    for shift in range(pairs):
+        out[(lax.axis_index("pair") - shift + pairs) & (pairs - 1)] = shifted[shift][...]
+
+
+def order(shifted, held):
+    return pl.pallas_call(
+        order_kernel,
+        out_shape=jax.ShapeDtypeStruct((len(shifted),) + shifted[0].shape, BF16),
+        in_specs=[VMEM] * (len(shifted) + 1),
+        out_specs=VMEM,
+        compiler_params=PARAMS,
+        name="order",
+    )(*shifted, in_vmem(held))
 
 
 def forward_dots(stacked, response, bin_):
@@ -144,31 +159,29 @@
         out[start : start + PIECES, :] = held[owner * PIECES : (owner + 1) * PIECES, :].astype(BF16)
 
 
-def first_forward_kernel(*refs):
-    *gathered, direct, response, out, near, stacked, held, near_done = refs
+def first_forward_kernel(mine, other, direct, response, out, near, stacked, held, near_done):
     fetch = pltpu.make_async_copy(direct, near, near_done)
     fetch.start()
     stride = SHARED + PIECES
-    pairs = len(gathered)
-    positions = gathered[0].shape[3]
-    for shift in range(pairs):
-        pair = (lax.axis_index("pair") - shift + pairs) & (pairs - 1)
-        for core in range(2):
+    own_core = lax.axis_index("core")
+    pairs, bins, _, positions = mine.shape
+    for pair in range(pairs):
+        for source, core in ((mine, own_core), (other, 1 - own_core)):
             start = pl.multiple_of((2 * pair + core) * positions, positions)
-            for bin_ in range(response.shape[1]):
-                stacked[bin_, :, pl.ds(start, positions)] = gathered[shift][core, bin_]
-    for bin_ in range(response.shape[1]):
+            for bin_ in range(bins):
+                stacked[bin_, :, pl.ds(start, positions)] = source[pair, bin_]
+    for bin_ in range(bins):
         share(forward_dots(stacked[bin_], response, bin_), bin_, out, stride)
     fetch.wait()
     spread_direct(near, held, out, stride)
 
 
-def first_forward(gathered, direct, response):
+def first_forward(mine, other, direct, response):
     bins, sources = response.shape[1], response.shape[3]
     return pl.pallas_call(
         first_forward_kernel,
         out_shape=jax.ShapeDtypeStruct((OWNERS * (SHARED + PIECES), LANES), BF16),
-        in_specs=[VMEM] * len(gathered) + [HBM, VMEM],
+        in_specs=[VMEM, VMEM, HBM, VMEM],
         out_specs=VMEM,
         scratch_shapes=[
             pltpu.VMEM(direct.shape, F32),
@@ -178,7 +191,7 @@
         ],
         compiler_params=PARAMS,
         name="first_forward",
-    )(*gathered, in_hbm(direct), in_vmem(response))
+    )(mine, other, in_hbm(direct), in_vmem(response))
 
 
 def forward_kernel(mine, other, response, out, held):
@@ -266,7 +279,7 @@
     )(rounded, own, onset, blocks)
 
 
-def adjoint_kernel(mine, other, response, out, minus, held):
+def adjoint_kernel(mine, other, response, near, far, minus, held):
     lower = lax.axis_index("freq") < OWNERS // 2
     tiles = response.shape[3] // (2 * LANES)
     for bin_ in range(response.shape[1]):
@@ -285,9 +298,12 @@
             for half in range(2):
                 lane = (tile * 2 + half) * LANES
                 for part in range(2):
-                    start = tile * NF + (half * 2 + part) * 4 + bin_
+                    start = (tile % 2 * tiles // 2 + tile // 2) * NF + (half * 2 + part) * 4 + bin_
                     held[pl.ds(start, FP, stride=16), :] = parts[part][:, lane : lane + LANES]
-    out[...] = held[...].astype(out.dtype)
+    core = lax.axis_index("core")
+    rows = near.shape[0]
+    near[...] = held[pl.ds(pl.multiple_of(core * rows, rows), rows), :]
+    far[...] = held[pl.ds(pl.multiple_of((1 - core) * rows, rows), rows), :].astype(far.dtype)
 
 
 def adjoint_product(mine, other, response):
@@ -296,15 +312,31 @@
     return pl.pallas_call(
         adjoint_kernel,
         out_shape=(
-            jax.ShapeDtypeStruct((rows, LANES), BF16),
+            jax.ShapeDtypeStruct((rows // 2, LANES), F32),
+            jax.ShapeDtypeStruct((rows // 2, LANES), BF16),
             jax.ShapeDtypeStruct((2, bins, FP, receivers), F32),
         ),
         in_specs=[VMEM] * 3,
-        out_specs=(VMEM, VMEM),
+        out_specs=(VMEM, VMEM, VMEM),
         scratch_shapes=[pltpu.VMEM((rows, LANES), F32)],
         compiler_params=PARAMS,
         name="adjoint_product",
     )(mine, other, in_vmem(response))
+
+
+def add_kernel(near, far, out):
+    out[...] = (near[...] + far[...].astype(F32)).astype(out.dtype)
+
+
+def add(near, far):
+    return pl.pallas_call(
+        add_kernel,
+        out_shape=jax.ShapeDtypeStruct(near.shape, BF16),
+        in_specs=[VMEM, VMEM],
+        out_specs=VMEM,
+        compiler_params=PARAMS,
+        name="add",
+    )(near, far)
 
 
 def plus_kernel(inverse, forward, onset, blocks, direct, out):
@@ -361,26 +393,28 @@
 
 
 def on_device(response, direct, onset):
-    groups, pairs, cores = (lax.axis_size(axis) for axis in ("freq", "pair", "core"))
+    groups, pairs = lax.axis_size("freq"), lax.axis_size("pair")
     rounded, own_bins, inverse, forward = (jnp.asarray(table) for table in tables())
     other_core = functools.partial(lax.ppermute, axis_name="core", perm=[(0, 1), (1, 0)])
     partners = [(owner, owner ^ (OWNERS // 2)) for owner in range(OWNERS)]
-    chip = prepare(direct, other_core(direct))
-    gathered = [chip]
+    shifted = [prepare(direct)]
     for shift in range(1, pairs):
-        gathered.append(lax.ppermute(chip, "pair", [(pair, (pair + shift) % pairs) for pair in range(pairs)]))
+        perm = [(pair, (pair + shift) % pairs) for pair in range(pairs)]
+        shifted.append(lax.ppermute(shifted[0], "pair", perm))
     held = hold(response)
+    mine = order(shifted, held)
+    other = other_core(mine)
     for step in range(ITERS):
         if step == 0:
-            upgoing = first_forward(gathered, direct, held)
+            upgoing = first_forward(mine, other, direct, held)
         else:
             upgoing = forward_product(mine, other, held)
         upgoing = exchange(upgoing, "freq", groups)
         mine, other, *owned = minus_roundtrip(rounded, own_bins, onset, upgoing, step == 0)
         if step == 0:
             (direct_columns,) = owned
-        partial, minus = adjoint_product(mine, lax.ppermute(other, "freq", partners), held)
-        partial = exchange(partial, ("pair", "core", "freq"), pairs * cores * groups)
+        near, far, minus = adjoint_product(mine, lax.ppermute(other, "freq", partners), held)
+        partial = exchange(add(near, other_core(far)), ("pair", "freq"), pairs * groups)
         last = step + 1 == ITERS
         copies, dtype = (1, F32) if last else (pairs, BF16)
         plus = plus_roundtrip(inverse, forward, onset, partial, direct_columns, copies, dtype)

time: 150 us -> 146 us (0.973)
  blocking collectives: 111 us -> 96.2 us
  starting transfers between devices: 15.2 us -> 24.9 us
    all_to_all x6, blocking collectives: 111 us -> 96.2 us  [exchange(): return lax.all_to_all(shaped, axes, 0, 0, tiled=True).reshape(blocks.shape)]
    ppermute x4 -> x5, starting transfers between devices: 10.9 us -> 17.1 us  [the longest x3 10.1 us: on_device(): shifted.append(lax.ppermute(shifted[0], 'pair', perm))]
    ppermute x1 -> x2, starting transfers between devices: 2.24 us -> 5.51 us  [on_device(): other = other_core(mine)]
  transfers between devices with their start and end apart: 7 -> 9, of which waited for: 6 -> 6; matrix products, arithmetic and copies ran while one was open for 0% -> 0% of each run, Pallas kernels for 2% -> 2%
where the time goes in v5:
time: 146 us; the launch traced here: 145 us
  blocking collectives  96.2 us (66%)
  starting transfers between devices  24.9 us (17%)
  Pallas kernels  14.5 us (10%)
  waiting for transfers between devices  7.28 us (5%)
    all_to_all x6, blocking collectives, exchange(): return lax.all_to_all(shaped, axes, 0, 0, tiled=True).reshape(blocks.shape)  96.2 us
    ppermute x3, starting transfers between devices, on_device(): shifted.append(lax.ppermute(shifted[0], 'pair', perm))  10.1 us
    ppermute x2, starting transfers between devices, on_device(): other_core(far)  6.99 us
    ppermute x2, starting transfers between devices, on_device(): other = other_core(mine)  5.51 us
    pallas_call x1, Pallas kernels, hold(): pl.pallas_call(hold_kernel, out_shape=pltpu.VMEM(response.shape, response...  3.39 us
    ppermute x2, waiting for transfers between devices, on_device(): lax.ppermute(other, 'freq', partners)  3.33 us
  transfers between devices with their start and end apart: 9, of which 6 were waited for; matrix products, arithmetic and copies ran while one was open for 0% of the time, Pallas kernels for 2%

profile of v5, /device:TPU:1, one launch (start us, length us, event | category | flops | bytes accessed | tf_op | source)
XLA Modules:
  0.0 144.5 jit_solution(3639619802382235506)
XLA Ops:
  1.5 6.8 %collective-permute-start.2 = (bf16[4,16,256]{2,1,0:T(8,128)(2,1)S(1)}, bf16[4,16,256]{2,1,0:T(8,128)(2,1)S(1)}, u32[]{:S(2)}, u32[]{:S(2)}) collective-permute-start(bf16[4,16,256]{2,1,0:T(8,128)(2,1)S(1)} %prepare.1.refs_0_), channel_id=1, source_target_pairs={{0,6},{2,0},{4,2},{6,4},{1,7},{3,1},{5,3},{7,5},{8,14},{10,8},{12,... | collective-permute-start | bytes 98312 | tf_op jit(solution)/shard_map/ppermute | solution.py:403
  9.3 2.3 %collective-permute-start = (bf16[4,16,256]{2,1,0:T(8,128)(2,1)S(1)}, bf16[4,16,256]{2,1,0:T(8,128)(2,1)S(1)}, u32[]{:S(2)}, u32[]{:S(2)}) collective-permute-start(bf16[4,16,256]{2,1,0:T(8,128)(2,1)S(1)} %prepare.1.refs_0_), channel_id=1, source_target_pairs={{0,2},{2,4},{4,6},{6,0},{1,3},{3,5},{5,7},{7,1},{8,10},{10,12},{12... | collective-permute-start | bytes 98312 | tf_op jit(solution)/shard_map/ppermute | solution.py:403
  11.6 3.4 %hold.1.refs_4_.response = bf16[2,4,256,2048]{3,2,1,0:T(8,128)(2,1)S(1)} custom-call(bf16[2,4,256,2048]{3,2,1,0:T(8,128)(2,1)} %response.1), custom_call_target="tpu_custom_call" | custom-call | bytes 16777216 | tf_op jit(solution)/shard_map/hold/pallas_call | solution.py:86
  15.1 2.3 %collective-permute-start.3 = (bf16[4,4,16,256]{3,2,1,0:T(8,128)(2,1)S(1)}, bf16[4,4,16,256]{3,2,1,0:T(8,128)(2,1)S(1)}, u32[]{:S(2)}, u32[]{:S(2)}) collective-permute-start(bf16[4,4,16,256]{3,2,1,0:T(8,128)(2,1)S(1)} %order.1.mine), channel_id=1, source_target_pairs={{0,1},{1,0},{2,3},{3,2},{4,5},{5,4},{6,7},{7,6},{8,9},{9,8},{10,11... | collective-permute-start | bytes 393224 | tf_op jit(solution)/shard_map/ppermute | solution.py:406
  17.4 1.0 collective-permute-done.3.other
  18.4 2.4 %first_forward.1 = bf16[2560,128]{1,0:T(8,128)(2,1)S(1)} custom-call(bf16[4,4,16,256]{3,2,1,0:T(8,128)(2,1)S(1)} %order.1.mine, bf16[4,4,16,256]{3,2,1,0:T(8,128)(2,1)S(1)} %collective-permute-done.3.other, f32[2,4,8,256]{3,2,1,0:T(8,128)} %direct.3, bf16[2,4,256,2048]{3,2,1,0:T(8,128)(2,1)S(1)} %hold.1.refs_4_.response), custom_call_target="tpu_custom_call" | custom-call | tf_op jit(solution)/shard_map/first_forward/pallas_call | solution.py:181
  20.8 18.3 %all_to_all.30 = bf16[32,80,128]{2,1,0:T(8,128)(2,1)S(1)} all-to-all(bf16[32,80,128]{2,1,0:T(8,128)(2,1)S(1)} %bitcast.12), channel_id=1, replica_groups=mesh['freq'=32,'pair'=4,'core'=2] {'freq'}, dimensions={0} | all-to-all | bytes 1310720 | tf_op jit(solution)/shard_map/all_to_all | solution.py:392
  39.1 1.0 minus_roundtrip.2
  40.1 1.3 collective-permute-start.4
  41.5 1.5 %collective-permute-done.4.other = f32[64,128]{1,0:T(8,128)S(1)} collective-permute-done((f32[64,128]{1,0:T(8,128)S(1)}, f32[64,128]{1,0:T(8,128)S(1)}, u32[]{:S(2)}, u32[]{:S(2)}) %collective-permute-start.4) | collective-permute-done | bytes 32800 | tf_op jit(solution)/shard_map/ppermute | solution.py:416
  42.9 1.4 adjoint_product.2
  44.3 3.8 %collective-permute-start.5 = (bf16[512,128]{1,0:T(8,128)(2,1)S(1)}, bf16[512,128]{1,0:T(8,128)(2,1)S(1)}, u32[]{:S(2)}, u32[]{:S(2)}) collective-permute-start(bf16[512,128]{1,0:T(8,128)(2,1)S(1)} %get-tuple-element.15), channel_id=1, source_target_pairs={{0,1},{1,0},{2,3},{3,2},{4,5},{5,4},{6,7},{7,6},{8,9},{9,8},{10,11... | collective-permute-start | bytes 393224 | tf_op jit(solution)/shard_map/ppermute | solution.py:417
  48.2 1.0 collective-permute-done.5.far
  49.2 20.2 %all_to_all.31 = bf16[128,4,128]{2,1,0:T(4,128)(2,1)S(1)} all-to-all(bf16[128,4,128]{2,1,0:T(4,128)(2,1)S(1)} %bitcast.19), channel_id=1, replica_groups=mesh['freq'=32,'pair'=4,'core'=2] {'pair','freq'}, dimensions={0} | all-to-all | bytes 262144 | tf_op jit(solution)/shard_map/all_to_all | solution.py:392
  69.8 16.8 %all_to_all.32 = bf16[128,4,128]{2,1,0:T(4,128)(2,1)S(1)} all-to-all(bf16[128,4,128]{2,1,0:T(4,128)(2,1)S(1)} %bitcast.22), channel_id=1, replica_groups=mesh['freq'=32,'pair'=4,'core'=2] {'pair','freq'}, dimensions={0} | all-to-all | bytes 262144 | tf_op jit(solution)/shard_map/all_to_all | solution.py:392
  86.6 3.2 %collective-permute-start.6 = (bf16[512,128]{1,0:T(8,128)(2,1)S(1)}, bf16[512,128]{1,0:T(8,128)(2,1)S(1)}, u32[]{:S(2)}, u32[]{:S(2)}) collective-permute-start(bf16[512,128]{1,0:T(8,128)(2,1)S(1)} %bitcast.16), channel_id=1, source_target_pairs={{0,1},{1,0},{2,3},{3,2},{4,5},{5,4},{6,7},{7,6},{8,9},{9,8},{10,11... | collective-permute-start | bytes 393224 | tf_op jit(solution)/shard_map/ppermute | solution.py:425
  89.8 1.0 collective-permute-done.6.other
  90.8 2.3 %forward_product.1 = bf16[2048,128]{1,0:T(8,128)(2,1)S(1)} custom-call(bf16[512,128]{1,0:T(8,128)(2,1)S(1)} %bitcast.17, bf16[512,128]{1,0:T(8,128)(2,1)S(1)} %collective-permute-done.6.other, bf16[2,4,256,2048]{3,2,1,0:T(8,128)(2,1)S(1)} %hold.1.refs_4_.response), custom_call_target="tpu_custom_call" | custom-call | tf_op jit(solution)/shard_map/forward_product/pallas_call | solution.py:217
  93.1 13.5 %all_to_all.33 = bf16[32,64,128]{2,1,0:T(8,128)(2,1)S(1)} all-to-all(bf16[32,64,128]{2,1,0:T(8,128)(2,1)S(1)} %bitcast.14), channel_id=1, replica_groups=mesh['freq'=32,'pair'=4,'core'=2] {'freq'}, dimensions={0} | all-to-all | bytes 1048576 | tf_op jit(solution)/shard_map/all_to_all | solution.py:392
  108.4 1.9 %collective-permute-done.7.other = f32[64,128]{1,0:T(8,128)S(1)} collective-permute-done((f32[64,128]{1,0:T(8,128)S(1)}, f32[64,128]{1,0:T(8,128)S(1)}, u32[]{:S(2)}, u32[]{:S(2)}) %collective-permute-start.7) | collective-permute-done | bytes 32800 | tf_op jit(solution)/shard_map/ppermute | solution.py:416
  110.3 1.4 adjoint_product.3
  111.7 3.2 %collective-permute-start.8 = (bf16[512,128]{1,0:T(8,128)(2,1)S(1)}, bf16[512,128]{1,0:T(8,128)(2,1)S(1)}, u32[]{:S(2)}, u32[]{:S(2)}) collective-permute-start(bf16[512,128]{1,0:T(8,128)(2,1)S(1)} %get-tuple-element.21), channel_id=1, source_target_pairs={{0,1},{1,0},{2,3},{3,2},{4,5},{5,4},{6,7},{7,6},{8,9},{9,8},{10,11... | collective-permute-start | bytes 393224 | tf_op jit(solution)/shard_map/ppermute | solution.py:417
  115.9 17.4 %all_to_all.34 = bf16[128,4,128]{2,1,0:T(4,128)(2,1)S(1)} all-to-all(bf16[128,4,128]{2,1,0:T(4,128)(2,1)S(1)} %bitcast.20), channel_id=1, replica_groups=mesh['freq'=32,'pair'=4,'core'=2] {'pair','freq'}, dimensions={0} | all-to-all | bytes 262144 | tf_op jit(solution)/shard_map/all_to_all | solution.py:392
  133.7 10.2 %all_to_all.35 = f32[32,4,128]{2,1,0:T(4,128)S(1)} all-to-all(f32[32,4,128]{2,1,0:T(4,128)S(1)} %bitcast.24), channel_id=1, replica_groups=mesh['freq'=32,'pair'=4,'core'=2] {'freq'}, dimensions={0} | all-to-all | bytes 131072 | tf_op jit(solution)/shard_map/all_to_all | solution.py:392
  (26 shorter events, 6.3 us)
Async XLA Ops:
  0.6 0.8 copy-start.4
  1.5 13.5 %collective-permute-start.2 = (bf16[4,16,256]{2,1,0:T(8,128)(2,1)S(1)}, bf16[4,16,256]{2,1,0:T(8,128)(2,1)S(1)}, u32[]{:S(2)}, u32[]{:S(2)}) collective-permute-start(bf16[4,16,256]{2,1,0:T(8,128)(2,1)S(1)} %prepare.1.refs_0_), channel_id=1, source_target_pairs={{0,6},{2,0},{4,2},{6,4},{1,7},{3,1},{5,3},{7,5},{8,14},{10,8},{12,... | collective-permute-start | bytes 98312 | tf_op jit(solution)/shard_map/ppermute | solution.py:403
  8.3 6.7 %collective-permute-start.1 = (bf16[4,16,256]{2,1,0:T(8,128)(2,1)S(1)}, bf16[4,16,256]{2,1,0:T(8,128)(2,1)S(1)}, u32[]{:S(2)}, u32[]{:S(2)}) collective-permute-start(bf16[4,16,256]{2,1,0:T(8,128)(2,1)S(1)} %prepare.1.refs_0_), channel_id=1, source_target_pairs={{0,4},{2,6},{4,0},{6,2},{1,5},{3,7},{5,1},{7,3},{8,12},{10,14},{12... | collective-permute-start | bytes 98312 | tf_op jit(solution)/shard_map/ppermute | solution.py:403
  9.3 5.7 %collective-permute-start = (bf16[4,16,256]{2,1,0:T(8,128)(2,1)S(1)}, bf16[4,16,256]{2,1,0:T(8,128)(2,1)S(1)}, u32[]{:S(2)}, u32[]{:S(2)}) collective-permute-start(bf16[4,16,256]{2,1,0:T(8,128)(2,1)S(1)} %prepare.1.refs_0_), channel_id=1, source_target_pairs={{0,2},{2,4},{4,6},{6,0},{1,3},{3,5},{5,7},{7,1},{8,10},{10,12},{12... | collective-permute-start | bytes 98312 | tf_op jit(solution)/shard_map/ppermute | solution.py:403
  15.0 24.1 %copy-start = (bf16[32,16,448]{2,1,0:T(8,128)(2,1)S(1)}, bf16[32,16,448]{2,1,0:T(8,128)(2,1)}, u32[]{:S(2)}) copy-start(bf16[32,16,448]{2,1,0:T(8,128)(2,1)} %constant.9.clone.own) | copy-start | bytes 1376260
  15.0 24.1 %copy-start.3 = (bf16[2,224,256]{2,1,0:T(8,128)(2,1)S(1)}, bf16[2,224,256]{2,1,0:T(8,128)(2,1)}, u32[]{:S(2)}) copy-start(bf16[2,224,256]{2,1,0:T(8,128)(2,1)} %constant.8.clone.rounded) | copy-start | bytes 688132
  15.0 24.1 %copy-start.5 = (s32[8,256]{1,0:T(8,128)S(1)}, s32[8,256]{1,0:T(8,128)}, u32[]{:S(2)}) copy-start(s32[8,256]{1,0:T(8,128)} %onset.7) | copy-start | bytes 24580
  15.1 54.3 %copy-start.1 = (bf16[2,128,672]{2,1,0:T(8,128)(2,1)S(1)}, bf16[2,128,672]{2,1,0:T(8,128)(2,1)}, u32[]{:S(2)}) copy-start(bf16[2,128,672]{2,1,0:T(8,128)(2,1)} %constant.11.clone.forward) | copy-start | bytes 1032196
  15.1 54.3 %copy-start.2 = (bf16[2,224,384]{2,1,0:T(8,128)(2,1)S(1)}, bf16[2,224,384]{2,1,0:T(8,128)(2,1)}, u32[]{:S(2)}) copy-start(bf16[2,224,384]{2,1,0:T(8,128)(2,1)} %constant.10.clone.inverse) | copy-start | bytes 1032196
  15.1 3.3 %collective-permute-start.3 = (bf16[4,4,16,256]{3,2,1,0:T(8,128)(2,1)S(1)}, bf16[4,4,16,256]{3,2,1,0:T(8,128)(2,1)S(1)}, u32[]{:S(2)}, u32[]{:S(2)}) collective-permute-start(bf16[4,4,16,256]{3,2,1,0:T(8,128)(2,1)S(1)} %order.1.mine), channel_id=1, source_target_pairs={{0,1},{1,0},{2,3},{3,2},{4,5},{5,4},{6,7},{7,6},{8,9},{9,8},{10,11... | collective-permute-start | bytes 393224 | tf_op jit(solution)/shard_map/ppermute | solution.py:406
  40.1 2.8 %collective-permute-start.4 = (f32[64,128]{1,0:T(8,128)S(1)}, f32[64,128]{1,0:T(8,128)S(1)}, u32[]{:S(2)}, u32[]{:S(2)}) collective-permute-start(f32[64,128]{1,0:T(8,128)S(1)} %get-tuple-element.13), channel_id=1, source_target_pairs={{0,128},{8,136},{16,144},{24,152},{32,160},{40,168},{48,176},{56,1... | collective-permute-start | bytes 98312 | tf_op jit(solution)/shard_map/ppermute | solution.py:416
  44.3 4.8 %collective-permute-start.5 = (bf16[512,128]{1,0:T(8,128)(2,1)S(1)}, bf16[512,128]{1,0:T(8,128)(2,1)S(1)}, u32[]{:S(2)}, u32[]{:S(2)}) collective-permute-start(bf16[512,128]{1,0:T(8,128)(2,1)S(1)} %get-tuple-element.15), channel_id=1, source_target_pairs={{0,1},{1,0},{2,3},{3,2},{4,5},{5,4},{6,7},{7,6},{8,9},{9,8},{10,11... | collective-permute-start | bytes 393224 | tf_op jit(solution)/shard_map/ppermute | solution.py:417
  86.6 4.2 %collective-permute-start.6 = (bf16[512,128]{1,0:T(8,128)(2,1)S(1)}, bf16[512,128]{1,0:T(8,128)(2,1)S(1)}, u32[]{:S(2)}, u32[]{:S(2)}) collective-permute-start(bf16[512,128]{1,0:T(8,128)(2,1)S(1)} %bitcast.16), channel_id=1, source_target_pairs={{0,1},{1,0},{2,3},{3,2},{4,5},{5,4},{6,7},{7,6},{8,9},{9,8},{10,11... | collective-permute-start | bytes 393224 | tf_op jit(solution)/shard_map/ppermute | solution.py:425
  107.5 2.8 %collective-permute-start.7 = (f32[64,128]{1,0:T(8,128)S(1)}, f32[64,128]{1,0:T(8,128)S(1)}, u32[]{:S(2)}, u32[]{:S(2)}) collective-permute-start(f32[64,128]{1,0:T(8,128)S(1)} %get-tuple-element.18), channel_id=1, source_target_pairs={{0,128},{8,136},{16,144},{24,152},{32,160},{40,168},{48,176},{56,1... | collective-permute-start | bytes 98312 | tf_op jit(solution)/shard_map/ppermute | solution.py:416
  111.7 4.2 %collective-permute-start.8 = (bf16[512,128]{1,0:T(8,128)(2,1)S(1)}, bf16[512,128]{1,0:T(8,128)(2,1)S(1)}, u32[]{:S(2)}, u32[]{:S(2)}) collective-permute-start(bf16[512,128]{1,0:T(8,128)(2,1)S(1)} %get-tuple-element.21), channel_id=1, source_target_pairs={{0,1},{1,0},{2,3},{3,2},{4,5},{5,4},{6,7},{7,6},{8,9},{9,8},{10,11... | collective-permute-start | bytes 393224 | tf_op jit(solution)/shard_map/ppermute | solution.py:417

commit v6 on v5

--- a/solution.py
+++ b/solution.py
@@ -39,7 +39,7 @@
     rounded, inverse, forward, own = [], [], [], []
     devices = np.arange(OWNERS)
     pair = np.stack([devices, devices ^ (OWNERS // 2)], axis=1)
-    for part, table in enumerate((np.cos(angle), np.sin(angle))):
+    for table in (np.cos(angle), np.sin(angle)):
         high, low = split(table)
         rounded.append(np.concatenate([high, low], axis=1))
         inverse.append(np.concatenate([high, high, low], axis=1))
@@ -49,8 +49,8 @@
         rows = np.concatenate(
             [np.concatenate([high, high], axis=2), np.concatenate([low, np.zeros_like(low)], axis=2)], axis=1
         )
-        own.append(rows[part * OWNERS // 2 : (part + 1) * OWNERS // 2])
-    return np.stack(rounded), np.concatenate(own), np.stack(inverse), np.stack(forward)
+        own.append(rows)
+    return np.stack(rounded), np.stack(own, axis=1), np.stack(inverse), np.stack(forward)
 
 
 def high_low(value):
@@ -76,23 +76,35 @@
 PARAMS = pltpu.CompilerParams(vmem_limit_bytes=VMEM_LIMIT)
 
 
-def hold_kernel(response, held, done):
-    copy = pltpu.make_async_copy(response, held, done)
+def hold_kernel(direct, response, kept, pieces, near, held, done, near_done):
+    fetch = pltpu.make_async_copy(direct, near, near_done)
+    fetch.start()
+    copy = pltpu.make_async_copy(response, kept, done)
     copy.start()
+    fetch.wait()
+    spread_direct(near, held, pieces)
     copy.wait()
 
 
-def hold(response):
+def hold(direct, response):
     return pl.pallas_call(
         hold_kernel,
-        out_shape=pltpu.VMEM(response.shape, response.dtype),
-        in_specs=[HBM],
-        out_specs=VMEM,
-        scratch_shapes=[pltpu.SemaphoreType.DMA],
+        out_shape=(
+            pltpu.VMEM(response.shape, response.dtype),
+            jax.ShapeDtypeStruct((OWNERS * PIECES, LANES), BF16),
+        ),
+        in_specs=[HBM, HBM],
+        out_specs=(VMEM, VMEM),
+        scratch_shapes=[
+            pltpu.VMEM(direct.shape, F32),
+            pltpu.VMEM((OWNERS * PIECES, LANES), F32),
+            pltpu.SemaphoreType.DMA,
+            pltpu.SemaphoreType.DMA,
+        ],
         compiler_params=PARAMS,
         cost_estimate=pl.CostEstimate(flops=0, bytes_accessed=4 * response.size, transcendentals=0),
         name="hold",
-    )(in_hbm(response))
+    )(in_hbm(direct), in_hbm(response))
 
 
 def prepare_kernel(direct, out):
@@ -130,22 +142,26 @@
     )(*shifted, in_vmem(held))
 
 
-def forward_dots(stacked, response, bin_):
+def forward_dots(blocks, response, bin_, core):
     dims = (((1,), (1,)), ((), ()))
-    first = lax.dot_general(stacked, response[0, bin_], dims, preferred_element_type=F32)
-    second = lax.dot_general(stacked, response[1, bin_], dims, preferred_element_type=F32)
-    return first[:FP] - second[FP:], first[FP:] + second[:FP]
-
-
-def share(parts, bin_, out, stride):
-    for part in range(2):
-        tile = jnp.concatenate([parts[part][:, :LANES], parts[part][:, LANES:]], axis=0).astype(BF16)
-        for owner in range(part * OWNERS // 2, (part + 1) * OWNERS // 2):
-            start = owner * stride + bin_ * 16
-            out[start : start + 16, :] = tile
-
-
-def spread_direct(direct, held, out, stride):
+    first = second = 0.0
+    for pair, block in enumerate(blocks):
+        width = block.shape[1]
+        lanes = pl.ds(pl.multiple_of((2 * pair + core) * width, width), width)
+        first += lax.dot_general(block, response[0, bin_, :, lanes], dims, preferred_element_type=F32)
+        second += lax.dot_general(block, response[1, bin_, :, lanes], dims, preferred_element_type=F32)
+    return jnp.concatenate([first[:FP] - second[FP:], first[FP:] + second[:FP]], axis=0)
+
+
+def share(value, bin_, out, stride):
+    value = value.astype(BF16)
+    for owner in range(OWNERS):
+        half = owner // (OWNERS // 2)
+        start = owner * stride + bin_ * 16
+        out[start : start + 16, :] = value[:, half * LANES : (half + 1) * LANES]
+
+
+def spread_direct(direct, held, out):
     held[...] = jnp.zeros_like(held)
     for bin_ in range(direct.shape[1]):
         for half in range(2):
@@ -154,75 +170,101 @@
                 start = (half * 2 + part) * PIECES + bin_
                 for row, piece in enumerate(high_low(value)):
                     held[pl.ds(start + 4 * row, FP, stride=4 * PIECES), :] = piece.astype(F32)
+    out[...] = held[...].astype(BF16)
+
+
+def near_direct_kernel(mine, response, out):
+    pairs, bins = mine.shape[:2]
+    core = lax.axis_index("core")
+    for bin_ in range(bins):
+        out[bin_] = forward_dots([mine[pair, bin_] for pair in range(pairs)], response, bin_, core)
+
+
+def near_direct(mine, response):
+    bins, receivers = response.shape[1:3]
+    return pl.pallas_call(
+        near_direct_kernel,
+        out_shape=jax.ShapeDtypeStruct((bins, 2 * FP, receivers), F32),
+        in_specs=[VMEM] * 2,
+        out_specs=VMEM,
+        compiler_params=PARAMS,
+        name="near_direct",
+    )(mine, in_vmem(response))
+
+
+def far_direct_kernel(other, near, pieces, response, out):
+    stride = SHARED + PIECES
     for owner in range(OWNERS):
         start = owner * stride + SHARED
-        out[start : start + PIECES, :] = held[owner * PIECES : (owner + 1) * PIECES, :].astype(BF16)
-
-
-def first_forward_kernel(mine, other, direct, response, out, near, stacked, held, near_done):
-    fetch = pltpu.make_async_copy(direct, near, near_done)
-    fetch.start()
-    stride = SHARED + PIECES
-    own_core = lax.axis_index("core")
-    pairs, bins, _, positions = mine.shape
-    for pair in range(pairs):
-        for source, core in ((mine, own_core), (other, 1 - own_core)):
-            start = pl.multiple_of((2 * pair + core) * positions, positions)
-            for bin_ in range(bins):
-                stacked[bin_, :, pl.ds(start, positions)] = source[pair, bin_]
+        out[start : start + PIECES, :] = pieces[owner * PIECES : (owner + 1) * PIECES, :]
+    pairs, bins = other.shape[:2]
+    core = 1 - lax.axis_index("core")
     for bin_ in range(bins):
-        share(forward_dots(stacked[bin_], response, bin_), bin_, out, stride)
-    fetch.wait()
-    spread_direct(near, held, out, stride)
-
-
-def first_forward(mine, other, direct, response):
-    bins, sources = response.shape[1], response.shape[3]
-    return pl.pallas_call(
-        first_forward_kernel,
+        value = forward_dots([other[pair, bin_] for pair in range(pairs)], response, bin_, core)
+        share(near[bin_] + value, bin_, out, stride)
+
+
+def far_direct(other, near, pieces, response):
+    return pl.pallas_call(
+        far_direct_kernel,
         out_shape=jax.ShapeDtypeStruct((OWNERS * (SHARED + PIECES), LANES), BF16),
-        in_specs=[VMEM, VMEM, HBM, VMEM],
-        out_specs=VMEM,
-        scratch_shapes=[
-            pltpu.VMEM(direct.shape, F32),
-            pltpu.VMEM((bins, 2 * FP, sources), BF16),
-            pltpu.VMEM((OWNERS * PIECES, LANES), F32),
-            pltpu.SemaphoreType.DMA,
-        ],
-        compiler_params=PARAMS,
-        name="first_forward",
-    )(mine, other, in_hbm(direct), in_vmem(response))
-
-
-def forward_kernel(mine, other, response, out, held):
-    own_core = lax.axis_index("core")
-    pairs = mine.shape[0] // NF
-    for pair in range(pairs):
-        for source, core in ((mine, own_core), (other, 1 - own_core)):
-            start = pl.multiple_of((2 * pair + core) * NF, NF)
-            held[pl.ds(start, NF), :] = source[pair * NF : (pair + 1) * NF, :].astype(F32)
+        in_specs=[VMEM] * 4,
+        out_specs=VMEM,
+        compiler_params=PARAMS,
+        name="far_direct",
+    )(other, near, pieces, in_vmem(response))
+
+
+def columns_of(held, bin_):
+    blocks = []
+    for pair in range(held.shape[0] // NF):
+        halves = []
+        for half in range(2):
+            start = pair * NF + half * 8 + bin_
+            both = [held[pl.ds(start + part * 4, FP, stride=16), :] for part in range(2)]
+            halves.append(jnp.concatenate(both, axis=0))
+        blocks.append(jnp.concatenate(halves, axis=1).astype(BF16))
+    return blocks
+
+
+def near_forward_kernel(mine, response, out, held):
+    held[...] = mine[...].astype(F32)
+    core = lax.axis_index("core")
     for bin_ in range(response.shape[1]):
-        columns = []
-        for tile in range(2 * pairs):
-            for half in range(2):
-                both = []
-                for part in range(2):
-                    start = tile * NF + (half * 2 + part) * 4 + bin_
-                    both.append(held[pl.ds(start, FP, stride=16), :])
-                columns.append(jnp.concatenate(both, axis=0).astype(BF16))
-        share(forward_dots(jnp.concatenate(columns, axis=1), response, bin_), bin_, out, SHARED)
-
-
-def forward_product(mine, other, response):
-    return pl.pallas_call(
-        forward_kernel,
+        out[bin_] = forward_dots(columns_of(held, bin_), response, bin_, core)
+
+
+def near_forward(mine, response):
+    bins, receivers = response.shape[1:3]
+    return pl.pallas_call(
+        near_forward_kernel,
+        out_shape=jax.ShapeDtypeStruct((bins, 2 * FP, receivers), F32),
+        in_specs=[VMEM] * 2,
+        out_specs=VMEM,
+        scratch_shapes=[pltpu.VMEM(mine.shape, F32)],
+        compiler_params=PARAMS,
+        name="near_forward",
+    )(mine, in_vmem(response))
+
+
+def far_forward_kernel(other, near, response, out, held):
+    held[...] = other[...].astype(F32)
+    core = 1 - lax.axis_index("core")
+    for bin_ in range(response.shape[1]):
+        value = forward_dots(columns_of(held, bin_), response, bin_, core)
+        share(near[bin_] + value, bin_, out, SHARED)
+
+
+def far_forward(other, near, response):
+    return pl.pallas_call(
+        far_forward_kernel,
         out_shape=jax.ShapeDtypeStruct((OWNERS * SHARED, LANES), BF16),
         in_specs=[VMEM] * 3,
         out_specs=VMEM,
-        scratch_shapes=[pltpu.VMEM((2 * mine.shape[0], LANES), F32)],
-        compiler_params=PARAMS,
-        name="forward_product",
-    )(mine, other, in_vmem(response))
+        scratch_shapes=[pltpu.VMEM(other.shape, F32)],
+        compiler_params=PARAMS,
+        name="far_forward",
+    )(other, near, in_vmem(response))
 
 
 def minus_kernel(stride, rounded, own, onset, blocks, mine, other, *refs):
@@ -231,23 +273,21 @@
         start = owner * stride
         spectra[owner * SHARED : (owner + 1) * SHARED, :] = blocks[start : start + SHARED, :].astype(F32)
     device = lax.axis_index("freq")
-    inverse = rounded[device >> 4]
-    forward = own[device]
+    limits = jnp.where(device < OWNERS // 2, onset[:, :LANES], onset[:, LANES:])
     wide = 2
-    for half in range(2):
-        lanes = slice(half * LANES, (half + 1) * LANES)
+    for part in range(2):
         for focal in range(0, FP, wide):
-            first = half * FP + focal
+            first = part * FP + focal
             spectrum = jnp.concatenate(
                 [spectra[pl.ds(first + i, NF, stride=16), :].astype(BF16) for i in range(wide)], axis=1
             )
             spectrum = jnp.concatenate([spectrum, spectrum], axis=0)
-            signal = jnp.dot(inverse, spectrum, preferred_element_type=F32)
-            limit = jnp.concatenate([onset[focal + i : focal + i + 1, lanes] for i in range(wide)], axis=1)
+            signal = jnp.dot(rounded[part], spectrum, preferred_element_type=F32)
+            limit = jnp.concatenate([limits[focal + i : focal + i + 1, :] for i in range(wide)], axis=1)
             lag = lax.broadcasted_iota(jnp.int32, signal.shape, 0)
             signal = jnp.where(lag < limit, signal, 0.0)
             signal = jnp.concatenate(high_low(signal), axis=0)
-            result = jnp.dot(forward, signal, preferred_element_type=F32)
+            result = jnp.dot(own[device, part], signal, preferred_element_type=F32)
             result = result[:8] + result[8:]
             for i in range(wide):
                 block = result[:, i * LANES : (i + 1) * LANES]
@@ -279,49 +319,94 @@
     )(rounded, own, onset, blocks)
 
 
-def adjoint_kernel(mine, other, response, near, far, minus, held):
-    lower = lax.axis_index("freq") < OWNERS // 2
-    tiles = response.shape[3] // (2 * LANES)
+def adjoint_dots(block, response, bin_, half, core, held, start):
+    receivers, sources = response.shape[2:]
+    rows = pl.ds(pl.multiple_of(half * LANES, LANES), LANES)
+    width = 2 * LANES
+    for pair in range(sources // (2 * width)):
+        lanes = pl.ds(pl.multiple_of((2 * pair + core) * width, width), width)
+        first = jnp.dot(block, response[0, bin_, rows, lanes], preferred_element_type=F32)
+        second = jnp.dot(block, response[1, bin_, rows, lanes], preferred_element_type=F32)
+        parts = (first[:FP] + second[FP:], first[FP:] - second[:FP])
+        for side in range(2):
+            for part in range(2):
+                row = start + pair * NF + (side * 2 + part) * 4 + bin_
+                held[pl.ds(row, FP, stride=16), :] = parts[part][:, side * LANES : (side + 1) * LANES]
+
+
+def first_half_kernel(mine, response, out):
+    half = lax.axis_index("freq") >> 4
+    core = lax.axis_index("core")
     for bin_ in range(response.shape[1]):
-        here, there = (
-            jnp.concatenate([part[start : start + FP, :] for start in (bin_ * 16, bin_ * 16 + FP)], axis=1)
-            for part in (mine, other)
-        )
-        both = jnp.where(lower, here, there), jnp.where(lower, there, here)
+        block = mine[bin_ * 16 : (bin_ + 1) * 16, :].astype(BF16)
+        adjoint_dots(block, response, bin_, half, core, out, 0)
+        adjoint_dots(block, response, bin_, half, 1 - core, out, out.shape[0] // 2)
+
+
+def first_half(mine, response):
+    rows = NF * response.shape[3] // (2 * LANES)
+    return pl.pallas_call(
+        first_half_kernel,
+        out_shape=jax.ShapeDtypeStruct((rows, LANES), F32),
+        in_specs=[VMEM] * 2,
+        out_specs=VMEM,
+        compiler_params=PARAMS,
+        name="first_half",
+    )(mine, in_vmem(response))
+
+
+def far_half_kernel(other, partial, response, out, held):
+    half = 1 - (lax.axis_index("freq") >> 4)
+    core = 1 - lax.axis_index("core")
+    for bin_ in range(response.shape[1]):
+        block = other[bin_ * 16 : (bin_ + 1) * 16, :].astype(BF16)
+        adjoint_dots(block, response, bin_, half, core, held, 0)
+    out[...] = (held[...] + partial[held.shape[0] :, :]).astype(out.dtype)
+
+
+def far_half(other, partial, response):
+    rows = partial.shape[0] // 2
+    return pl.pallas_call(
+        far_half_kernel,
+        out_shape=jax.ShapeDtypeStruct((rows, LANES), BF16),
+        in_specs=[VMEM] * 3,
+        out_specs=VMEM,
+        scratch_shapes=[pltpu.VMEM((rows, LANES), F32)],
+        compiler_params=PARAMS,
+        name="far_half",
+    )(other, partial, in_vmem(response))
+
+
+def near_half_kernel(mine, other, partial, response, out, *refs):
+    *minus, held = refs
+    half = lax.axis_index("freq") >> 4
+    core = lax.axis_index("core")
+    for bin_ in range(response.shape[1]):
+        block = other[bin_ * 16 : (bin_ + 1) * 16, :].astype(BF16)
+        adjoint_dots(block, response, bin_, 1 - half, core, held, 0)
         for part in range(2):
-            minus[part, bin_] = both[part]
-        stacked = jnp.concatenate(both, axis=0).astype(BF16)
-        first = jnp.dot(stacked, response[0, bin_], preferred_element_type=F32)
-        second = jnp.dot(stacked, response[1, bin_], preferred_element_type=F32)
-        parts = (first[:FP] + second[FP:], first[FP:] - second[:FP])
-        for tile in range(tiles):
-            for half in range(2):
-                lane = (tile * 2 + half) * LANES
-                for part in range(2):
-                    start = (tile % 2 * tiles // 2 + tile // 2) * NF + (half * 2 + part) * 4 + bin_
-                    held[pl.ds(start, FP, stride=16), :] = parts[part][:, lane : lane + LANES]
-    core = lax.axis_index("core")
-    rows = near.shape[0]
-    near[...] = held[pl.ds(pl.multiple_of(core * rows, rows), rows), :]
-    far[...] = held[pl.ds(pl.multiple_of((1 - core) * rows, rows), rows), :].astype(far.dtype)
-
-
-def adjoint_product(mine, other, response):
-    bins, receivers, sources = response.shape[1:]
-    rows = NF * sources // (2 * LANES)
-    return pl.pallas_call(
-        adjoint_kernel,
-        out_shape=(
-            jax.ShapeDtypeStruct((rows // 2, LANES), F32),
-            jax.ShapeDtypeStruct((rows // 2, LANES), BF16),
-            jax.ShapeDtypeStruct((2, bins, FP, receivers), F32),
-        ),
-        in_specs=[VMEM] * 3,
-        out_specs=(VMEM, VMEM, VMEM),
+            rows = slice(bin_ * 16 + part * FP, bin_ * 16 + (part + 1) * FP)
+            for place, source in ((half, mine), (1 - half, other)):
+                lanes = pl.ds(pl.multiple_of(place * LANES, LANES), LANES)
+                for spectrum in minus:
+                    spectrum[part, bin_, :, lanes] = source[rows, :]
+    out[...] = held[...] + partial[: held.shape[0], :]
+
+
+def near_half(mine, other, partial, response, last):
+    rows = partial.shape[0] // 2
+    out_shape = [jax.ShapeDtypeStruct((rows, LANES), F32)]
+    if last:
+        out_shape.append(jax.ShapeDtypeStruct((2, response.shape[1], FP, response.shape[2]), F32))
+    return pl.pallas_call(
+        near_half_kernel,
+        out_shape=out_shape,
+        in_specs=[VMEM] * 4,
+        out_specs=[VMEM] * len(out_shape),
         scratch_shapes=[pltpu.VMEM((rows, LANES), F32)],
         compiler_params=PARAMS,
-        name="adjoint_product",
-    )(mine, other, in_vmem(response))
+        name="near_half",
+    )(mine, other, partial, in_vmem(response))
 
 
 def add_kernel(near, far, out):
@@ -401,21 +486,24 @@
     for shift in range(1, pairs):
         perm = [(pair, (pair + shift) % pairs) for pair in range(pairs)]
         shifted.append(lax.ppermute(shifted[0], "pair", perm))
-    held = hold(response)
+    held, sent = hold(direct, response)
     mine = order(shifted, held)
     other = other_core(mine)
     for step in range(ITERS):
         if step == 0:
-            upgoing = first_forward(mine, other, direct, held)
+            upgoing = far_direct(other, near_direct(mine, held), sent, held)
         else:
-            upgoing = forward_product(mine, other, held)
+            upgoing = far_forward(other, near_forward(mine, held), held)
         upgoing = exchange(upgoing, "freq", groups)
         mine, other, *owned = minus_roundtrip(rounded, own_bins, onset, upgoing, step == 0)
         if step == 0:
             (direct_columns,) = owned
-        near, far, minus = adjoint_product(mine, lax.ppermute(other, "freq", partners), held)
+        other = lax.ppermute(other, "freq", partners)
+        partial = first_half(mine, held)
+        far = far_half(other, partial, held)
+        last = step + 1 == ITERS
+        near, *minus = near_half(mine, other, partial, held, last)
         partial = exchange(add(near, other_core(far)), ("pair", "freq"), pairs * groups)
-        last = step + 1 == ITERS
         copies, dtype = (1, F32) if last else (pairs, BF16)
         plus = plus_roundtrip(inverse, forward, onset, partial, direct_columns, copies, dtype)
         if last:
@@ -423,7 +511,7 @@
         else:
             mine = exchange(plus, ("pair", "freq"), pairs * groups)
             other = other_core(mine)
-    return (minus, plus)
+    return (minus[0], plus)
 
 
 def solution(mesh):

time: 146 us -> 142 us (0.973)
  waiting for transfers between devices: 7.28 us -> 2.6 us
    ppermute x2, waiting for transfers between devices: 1.97 us -> 0.01 us  [on_device(): other = other_core(mine)]
    pallas_call x5 -> x11, Pallas kernels: 11 us -> 11.8 us  [the longest x1 3.44 us: hold(): pl.pallas_call(hold_kernel, out_shape=(pltpu.VMEM(response.shape, respons...]
  transfers between devices with their start and end apart: 9 -> 9, of which waited for: 6 -> 4; matrix products, arithmetic and copies ran while one was open for 0% -> 0% of each run, Pallas kernels for 2% -> 6%
where the time goes in v6:
time: 142 us; the launch traced here: 141 us
  blocking collectives  97.6 us (69%)
  starting transfers between devices  23.9 us (17%)
  Pallas kernels  15.4 us (11%)
  waiting for transfers between devices  2.6 us (2%)
    all_to_all x6, blocking collectives, exchange(): return lax.all_to_all(shaped, axes, 0, 0, tiled=True).reshape(blocks.shape)  97.6 us
    ppermute x3, starting transfers between devices, on_device(): shifted.append(lax.ppermute(shifted[0], 'pair', perm))  10.1 us
    ppermute x2, starting transfers between devices, on_device(): other_core(far)  6 us
    ppermute x2, starting transfers between devices, on_device(): other = other_core(mine)  5.5 us
    pallas_call x1, Pallas kernels, hold(): pl.pallas_call(hold_kernel, out_shape=(pltpu.VMEM(response.shape, respons...  3.44 us
  transfers between devices with their start and end apart: 9, of which 4 were waited for; matrix products, arithmetic and copies ran while one was open for 0% of the time, Pallas kernels for 6%

profile of v6, /device:TPU:1, one launch (start us, length us, event | category | flops | bytes accessed | tf_op | source)
XLA Modules:
  0.0 141.2 jit_solution(11871831918054438380)
XLA Ops:
  1.5 6.8 %collective-permute-start.2 = (bf16[4,16,256]{2,1,0:T(8,128)(2,1)S(1)}, bf16[4,16,256]{2,1,0:T(8,128)(2,1)S(1)}, u32[]{:S(2)}, u32[]{:S(2)}) collective-permute-start(bf16[4,16,256]{2,1,0:T(8,128)(2,1)S(1)} %prepare.1.refs_0_), channel_id=1, source_target_pairs={{0,6},{2,0},{4,2},{6,4},{1,7},{3,1},{5,3},{7,5},{8,14},{10,8},{12,... | collective-permute-start | bytes 98312 | tf_op jit(solution)/shard_map/ppermute | solution.py:488
  8.3 1.0 collective-permute-start.1
  9.3 2.3 %collective-permute-start = (bf16[4,16,256]{2,1,0:T(8,128)(2,1)S(1)}, bf16[4,16,256]{2,1,0:T(8,128)(2,1)S(1)}, u32[]{:S(2)}, u32[]{:S(2)}) collective-permute-start(bf16[4,16,256]{2,1,0:T(8,128)(2,1)S(1)} %prepare.1.refs_0_), channel_id=1, source_target_pairs={{0,2},{2,4},{4,6},{6,0},{1,3},{3,5},{5,7},{7,1},{8,10},{10,12},{12... | collective-permute-start | bytes 98312 | tf_op jit(solution)/shard_map/ppermute | solution.py:488
  11.6 3.4 %hold.1 = (bf16[2,4,256,2048]{3,2,1,0:T(8,128)(2,1)S(1)}, bf16[512,128]{1,0:T(8,128)(2,1)S(1)}) custom-call(f32[2,4,8,256]{3,2,1,0:T(8,128)} %direct.3, bf16[2,4,256,2048]{3,2,1,0:T(8,128)(2,1)} %response.1), custom_call_target="tpu_custom_call" | custom-call | bytes 16777216 | tf_op jit(solution)/shard_map/hold/pallas_call | solution.py:90
  15.1 2.3 %collective-permute-start.3 = (bf16[4,4,16,256]{3,2,1,0:T(8,128)(2,1)S(1)}, bf16[4,4,16,256]{3,2,1,0:T(8,128)(2,1)S(1)}, u32[]{:S(2)}, u32[]{:S(2)}) collective-permute-start(bf16[4,4,16,256]{3,2,1,0:T(8,128)(2,1)S(1)} %order.1.mine), channel_id=1, source_target_pairs={{0,1},{1,0},{2,3},{3,2},{4,5},{5,4},{6,7},{7,6},{8,9},{9,8},{10,11... | collective-permute-start | bytes 393224 | tf_op jit(solution)/shard_map/ppermute | solution.py:491
  17.4 1.2 near_direct.1.near
  18.6 1.2 far_direct.1
  19.8 18.8 %all_to_all.30 = bf16[32,80,128]{2,1,0:T(8,128)(2,1)S(1)} all-to-all(bf16[32,80,128]{2,1,0:T(8,128)(2,1)S(1)} %bitcast.12), channel_id=1, replica_groups=mesh['freq'=32,'pair'=4,'core'=2] {'freq'}, dimensions={0} | all-to-all | bytes 1310720 | tf_op jit(solution)/shard_map/all_to_all | solution.py:477
  38.6 1.0 minus_roundtrip.2
  39.7 1.2 collective-permute-start.4
  41.5 1.0 collective-permute-done.4.other
  42.9 3.3 %collective-permute-start.5 = (bf16[512,128]{1,0:T(8,128)(2,1)S(1)}, bf16[512,128]{1,0:T(8,128)(2,1)S(1)}, u32[]{:S(2)}, u32[]{:S(2)}) collective-permute-start(bf16[512,128]{1,0:T(8,128)(2,1)S(1)} %far_half.2), channel_id=1, source_target_pairs={{0,1},{1,0},{2,3},{3,2},{4,5},{5,4},{6,7},{7,6},{8,9},{9,8},{10,11... | collective-permute-start | bytes 393224 | tf_op jit(solution)/shard_map/ppermute | solution.py:506
  47.2 20.3 %all_to_all.31 = bf16[128,4,128]{2,1,0:T(4,128)(2,1)S(1)} all-to-all(bf16[128,4,128]{2,1,0:T(4,128)(2,1)S(1)} %bitcast.19), channel_id=1, replica_groups=mesh['freq'=32,'pair'=4,'core'=2] {'pair','freq'}, dimensions={0} | all-to-all | bytes 262144 | tf_op jit(solution)/shard_map/all_to_all | solution.py:477
  67.9 16.9 %all_to_all.32 = bf16[128,4,128]{2,1,0:T(4,128)(2,1)S(1)} all-to-all(bf16[128,4,128]{2,1,0:T(4,128)(2,1)S(1)} %bitcast.22), channel_id=1, replica_groups=mesh['freq'=32,'pair'=4,'core'=2] {'pair','freq'}, dimensions={0} | all-to-all | bytes 262144 | tf_op jit(solution)/shard_map/all_to_all | solution.py:477
  84.9 3.2 %collective-permute-start.6 = (bf16[512,128]{1,0:T(8,128)(2,1)S(1)}, bf16[512,128]{1,0:T(8,128)(2,1)S(1)}, u32[]{:S(2)}, u32[]{:S(2)}) collective-permute-start(bf16[512,128]{1,0:T(8,128)(2,1)S(1)} %bitcast.16), channel_id=1, source_target_pairs={{0,1},{1,0},{2,3},{3,2},{4,5},{5,4},{6,7},{7,6},{8,9},{9,8},{10,11... | collective-permute-start | bytes 393224 | tf_op jit(solution)/shard_map/ppermute | solution.py:513
  88.1 1.2 near_forward.1.near
  89.3 1.3 far_forward.1
  90.6 13.8 %all_to_all.33 = bf16[32,64,128]{2,1,0:T(8,128)(2,1)S(1)} all-to-all(bf16[32,64,128]{2,1,0:T(8,128)(2,1)S(1)} %bitcast.15), channel_id=1, replica_groups=mesh['freq'=32,'pair'=4,'core'=2] {'freq'}, dimensions={0} | all-to-all | bytes 1048576 | tf_op jit(solution)/shard_map/all_to_all | solution.py:477
  104.4 1.0 minus_roundtrip.3
  105.4 1.2 collective-permute-start.7
  107.2 1.0 collective-permute-done.7.other
  108.6 2.7 %collective-permute-start.8 = (bf16[512,128]{1,0:T(8,128)(2,1)S(1)}, bf16[512,128]{1,0:T(8,128)(2,1)S(1)}, u32[]{:S(2)}, u32[]{:S(2)}) collective-permute-start(bf16[512,128]{1,0:T(8,128)(2,1)S(1)} %far_half.3), channel_id=1, source_target_pairs={{0,1},{1,0},{2,3},{3,2},{4,5},{5,4},{6,7},{7,6},{8,9},{9,8},{10,11... | collective-permute-start | bytes 393224 | tf_op jit(solution)/shard_map/ppermute | solution.py:506
  112.3 17.6 %all_to_all.34 = bf16[128,4,128]{2,1,0:T(4,128)(2,1)S(1)} all-to-all(bf16[128,4,128]{2,1,0:T(4,128)(2,1)S(1)} %bitcast.20), channel_id=1, replica_groups=mesh['freq'=32,'pair'=4,'core'=2] {'pair','freq'}, dimensions={0} | all-to-all | bytes 262144 | tf_op jit(solution)/shard_map/all_to_all | solution.py:477
  130.3 10.2 %all_to_all.35 = f32[32,4,128]{2,1,0:T(4,128)S(1)} all-to-all(f32[32,4,128]{2,1,0:T(4,128)S(1)} %bitcast.24), channel_id=1, replica_groups=mesh['freq'=32,'pair'=4,'core'=2] {'freq'}, dimensions={0} | all-to-all | bytes 131072 | tf_op jit(solution)/shard_map/all_to_all | solution.py:477
  (32 shorter events, 6.6 us)
Async XLA Ops:
  0.6 0.8 copy-start.4
  1.5 13.6 %collective-permute-start.2 = (bf16[4,16,256]{2,1,0:T(8,128)(2,1)S(1)}, bf16[4,16,256]{2,1,0:T(8,128)(2,1)S(1)}, u32[]{:S(2)}, u32[]{:S(2)}) collective-permute-start(bf16[4,16,256]{2,1,0:T(8,128)(2,1)S(1)} %prepare.1.refs_0_), channel_id=1, source_target_pairs={{0,6},{2,0},{4,2},{6,4},{1,7},{3,1},{5,3},{7,5},{8,14},{10,8},{12,... | collective-permute-start | bytes 98312 | tf_op jit(solution)/shard_map/ppermute | solution.py:488
  8.3 6.7 %collective-permute-start.1 = (bf16[4,16,256]{2,1,0:T(8,128)(2,1)S(1)}, bf16[4,16,256]{2,1,0:T(8,128)(2,1)S(1)}, u32[]{:S(2)}, u32[]{:S(2)}) collective-permute-start(bf16[4,16,256]{2,1,0:T(8,128)(2,1)S(1)} %prepare.1.refs_0_), channel_id=1, source_target_pairs={{0,4},{2,6},{4,0},{6,2},{1,5},{3,7},{5,1},{7,3},{8,12},{10,14},{12... | collective-permute-start | bytes 98312 | tf_op jit(solution)/shard_map/ppermute | solution.py:488
  9.3 5.7 %collective-permute-start = (bf16[4,16,256]{2,1,0:T(8,128)(2,1)S(1)}, bf16[4,16,256]{2,1,0:T(8,128)(2,1)S(1)}, u32[]{:S(2)}, u32[]{:S(2)}) collective-permute-start(bf16[4,16,256]{2,1,0:T(8,128)(2,1)S(1)} %prepare.1.refs_0_), channel_id=1, source_target_pairs={{0,2},{2,4},{4,6},{6,0},{1,3},{3,5},{5,7},{7,1},{8,10},{10,12},{12... | collective-permute-start | bytes 98312 | tf_op jit(solution)/shard_map/ppermute | solution.py:488
  15.1 23.5 %copy-start = (bf16[32,2,16,448]{3,2,1,0:T(8,128)(2,1)S(1)}, bf16[32,2,16,448]{3,2,1,0:T(8,128)(2,1)}, u32[]{:S(2)}) copy-start(bf16[32,2,16,448]{3,2,1,0:T(8,128)(2,1)} %constant.9.clone.own) | copy-start | bytes 2752516
  15.1 23.5 %copy-start.3 = (bf16[2,224,256]{2,1,0:T(8,128)(2,1)S(1)}, bf16[2,224,256]{2,1,0:T(8,128)(2,1)}, u32[]{:S(2)}) copy-start(bf16[2,224,256]{2,1,0:T(8,128)(2,1)} %constant.8.clone.rounded) | copy-start | bytes 688132
  15.1 23.5 %copy-start.5 = (s32[8,256]{1,0:T(8,128)S(1)}, s32[8,256]{1,0:T(8,128)}, u32[]{:S(2)}) copy-start(s32[8,256]{1,0:T(8,128)} %onset.7) | copy-start | bytes 24580
  15.1 3.5 %collective-permute-start.3 = (bf16[4,4,16,256]{3,2,1,0:T(8,128)(2,1)S(1)}, bf16[4,4,16,256]{3,2,1,0:T(8,128)(2,1)S(1)}, u32[]{:S(2)}, u32[]{:S(2)}) collective-permute-start(bf16[4,4,16,256]{3,2,1,0:T(8,128)(2,1)S(1)} %order.1.mine), channel_id=1, source_target_pairs={{0,1},{1,0},{2,3},{3,2},{4,5},{5,4},{6,7},{7,6},{8,9},{9,8},{10,11... | collective-permute-start | bytes 393224 | tf_op jit(solution)/shard_map/ppermute | solution.py:491
  39.7 2.8 %collective-permute-start.4 = (f32[64,128]{1,0:T(8,128)S(1)}, f32[64,128]{1,0:T(8,128)S(1)}, u32[]{:S(2)}, u32[]{:S(2)}) collective-permute-start(f32[64,128]{1,0:T(8,128)S(1)} %get-tuple-element.14), channel_id=1, source_target_pairs={{0,128},{8,136},{16,144},{24,152},{32,160},{40,168},{48,176},{56,1... | collective-permute-start | bytes 98312 | tf_op jit(solution)/shard_map/ppermute | solution.py:501
  41.5 26.0 %copy-start.1 = (bf16[2,128,672]{2,1,0:T(8,128)(2,1)S(1)}, bf16[2,128,672]{2,1,0:T(8,128)(2,1)}, u32[]{:S(2)}) copy-start(bf16[2,128,672]{2,1,0:T(8,128)(2,1)} %constant.11.clone.forward) | copy-start | bytes 1032196
  41.5 26.0 %copy-start.2 = (bf16[2,224,384]{2,1,0:T(8,128)(2,1)S(1)}, bf16[2,224,384]{2,1,0:T(8,128)(2,1)}, u32[]{:S(2)}) copy-start(bf16[2,224,384]{2,1,0:T(8,128)(2,1)} %constant.10.clone.inverse) | copy-start | bytes 1032196
  42.9 4.3 %collective-permute-start.5 = (bf16[512,128]{1,0:T(8,128)(2,1)S(1)}, bf16[512,128]{1,0:T(8,128)(2,1)S(1)}, u32[]{:S(2)}, u32[]{:S(2)}) collective-permute-start(bf16[512,128]{1,0:T(8,128)(2,1)S(1)} %far_half.2), channel_id=1, source_target_pairs={{0,1},{1,0},{2,3},{3,2},{4,5},{5,4},{6,7},{7,6},{8,9},{9,8},{10,11... | collective-permute-start | bytes 393224 | tf_op jit(solution)/shard_map/ppermute | solution.py:506
  84.9 4.4 %collective-permute-start.6 = (bf16[512,128]{1,0:T(8,128)(2,1)S(1)}, bf16[512,128]{1,0:T(8,128)(2,1)S(1)}, u32[]{:S(2)}, u32[]{:S(2)}) collective-permute-start(bf16[512,128]{1,0:T(8,128)(2,1)S(1)} %bitcast.16), channel_id=1, source_target_pairs={{0,1},{1,0},{2,3},{3,2},{4,5},{5,4},{6,7},{7,6},{8,9},{9,8},{10,11... | collective-permute-start | bytes 393224 | tf_op jit(solution)/shard_map/ppermute | solution.py:513
  105.4 2.8 %collective-permute-start.7 = (f32[64,128]{1,0:T(8,128)S(1)}, f32[64,128]{1,0:T(8,128)S(1)}, u32[]{:S(2)}, u32[]{:S(2)}) collective-permute-start(f32[64,128]{1,0:T(8,128)S(1)} %get-tuple-element.17), channel_id=1, source_target_pairs={{0,128},{8,136},{16,144},{24,152},{32,160},{40,168},{48,176},{56,1... | collective-permute-start | bytes 98312 | tf_op jit(solution)/shard_map/ppermute | solution.py:501
  108.6 3.7 %collective-permute-start.8 = (bf16[512,128]{1,0:T(8,128)(2,1)S(1)}, bf16[512,128]{1,0:T(8,128)(2,1)S(1)}, u32[]{:S(2)}, u32[]{:S(2)}) collective-permute-start(bf16[512,128]{1,0:T(8,128)(2,1)S(1)} %far_half.3), channel_id=1, source_target_pairs={{0,1},{1,0},{2,3},{3,2},{4,5},{5,4},{6,7},{7,6},{8,9},{9,8},{10,11... | collective-permute-start | bytes 393224 | tf_op jit(solution)/shard_map/ppermute | solution.py:506

commit v7 on v6

--- a/solution.py
+++ b/solution.py
@@ -18,7 +18,7 @@
 LANES = 128
 BF16 = jnp.bfloat16
 F32 = jnp.float32
-VMEM_LIMIT = 24 * 1024 * 1024
+VMEM_LIMIT = 10 * 1024 * 1024
 
 SHARED = 64
 PIECES = 16
@@ -76,29 +76,43 @@
 PARAMS = pltpu.CompilerParams(vmem_limit_bytes=VMEM_LIMIT)
 
 
-def hold_kernel(direct, response, kept, pieces, near, held, done, near_done):
+def hold_kernel(direct, response, kept, turned, pieces, near, held, done, near_done):
+    copies = [
+        pltpu.make_async_copy(response.at[part, bin_], kept.at[part, bin_], done.at[part, bin_])
+        for bin_ in range(response.shape[1])
+        for part in range(2)
+    ]
+    ahead = 4
     fetch = pltpu.make_async_copy(direct, near, near_done)
+    copies[0].start()
     fetch.start()
-    copy = pltpu.make_async_copy(response, kept, done)
-    copy.start()
+    for copy in copies[1:ahead]:
+        copy.start()
     fetch.wait()
     spread_direct(near, held, pieces)
-    copy.wait()
+    for step, copy in enumerate(copies):
+        copy.wait()
+        for later in copies[step + ahead : step + ahead + 1]:
+            later.start()
+        part, bin_ = step % 2, step // 2
+        turned[part, bin_] = kept[part, bin_].T
 
 
 def hold(direct, response):
+    parts, bins, receivers, sources = response.shape
     return pl.pallas_call(
         hold_kernel,
         out_shape=(
             pltpu.VMEM(response.shape, response.dtype),
+            pltpu.VMEM((parts, bins, sources, receivers), response.dtype),
             jax.ShapeDtypeStruct((OWNERS * PIECES, LANES), BF16),
         ),
         in_specs=[HBM, HBM],
-        out_specs=(VMEM, VMEM),
+        out_specs=(VMEM, VMEM, VMEM),
         scratch_shapes=[
             pltpu.VMEM(direct.shape, F32),
             pltpu.VMEM((OWNERS * PIECES, LANES), F32),
-            pltpu.SemaphoreType.DMA,
+            pltpu.SemaphoreType.DMA((parts, bins)),
             pltpu.SemaphoreType.DMA,
         ],
         compiler_params=PARAMS,
@@ -142,14 +156,13 @@
     )(*shifted, in_vmem(held))
 
 
-def forward_dots(blocks, response, bin_, core):
-    dims = (((1,), (1,)), ((), ()))
+def forward_dots(blocks, turned, bin_, core):
     first = second = 0.0
     for pair, block in enumerate(blocks):
         width = block.shape[1]
-        lanes = pl.ds(pl.multiple_of((2 * pair + core) * width, width), width)
-        first += lax.dot_general(block, response[0, bin_, :, lanes], dims, preferred_element_type=F32)
-        second += lax.dot_general(block, response[1, bin_, :, lanes], dims, preferred_element_type=F32)
+        rows = pl.ds(pl.multiple_of((2 * pair + core) * width, width), width)
+        first += jnp.dot(block, turned[0, bin_, rows, :], preferred_element_type=F32)
+        second += jnp.dot(block, turned[1, bin_, rows, :], preferred_element_type=F32)
     return jnp.concatenate([first[:FP] - second[FP:], first[FP:] + second[:FP]], axis=0)
 
 
@@ -173,15 +186,15 @@
     out[...] = held[...].astype(BF16)
 
 
-def near_direct_kernel(mine, response, out):
+def near_direct_kernel(mine, turned, out):
     pairs, bins = mine.shape[:2]
     core = lax.axis_index("core")
     for bin_ in range(bins):
-        out[bin_] = forward_dots([mine[pair, bin_] for pair in range(pairs)], response, bin_, core)
-
-
-def near_direct(mine, response):
-    bins, receivers = response.shape[1:3]
+        out[bin_] = forward_dots([mine[pair, bin_] for pair in range(pairs)], turned, bin_, core)
+
+
+def near_direct(mine, turned):
+    bins, _, receivers = turned.shape[1:]
     return pl.pallas_call(
         near_direct_kernel,
         out_shape=jax.ShapeDtypeStruct((bins, 2 * FP, receivers), F32),
@@ -189,10 +202,10 @@
         out_specs=VMEM,
         compiler_params=PARAMS,
         name="near_direct",
-    )(mine, in_vmem(response))
-
-
-def far_direct_kernel(other, near, pieces, response, out):
+    )(mine, in_vmem(turned))
+
+
+def far_direct_kernel(other, near, pieces, turned, out):
     stride = SHARED + PIECES
     for owner in range(OWNERS):
         start = owner * stride + SHARED
@@ -200,11 +213,11 @@
     pairs, bins = other.shape[:2]
     core = 1 - lax.axis_index("core")
     for bin_ in range(bins):
-        value = forward_dots([other[pair, bin_] for pair in range(pairs)], response, bin_, core)
+        value = forward_dots([other[pair, bin_] for pair in range(pairs)], turned, bin_, core)
         share(near[bin_] + value, bin_, out, stride)
 
 
-def far_direct(other, near, pieces, response):
+def far_direct(other, near, pieces, turned):
     return pl.pallas_call(
         far_direct_kernel,
         out_shape=jax.ShapeDtypeStruct((OWNERS * (SHARED + PIECES), LANES), BF16),
@@ -212,7 +225,7 @@
         out_specs=VMEM,
         compiler_params=PARAMS,
         name="far_direct",
-    )(other, near, pieces, in_vmem(response))
+    )(other, near, pieces, in_vmem(turned))
 
 
 def columns_of(held, bin_):
@@ -227,15 +240,15 @@
     return blocks
 
 
-def near_forward_kernel(mine, response, out, held):
+def near_forward_kernel(mine, turned, out, held):
     held[...] = mine[...].astype(F32)
     core = lax.axis_index("core")
-    for bin_ in range(response.shape[1]):
-        out[bin_] = forward_dots(columns_of(held, bin_), response, bin_, core)
-
-
-def near_forward(mine, response):
-    bins, receivers = response.shape[1:3]
+    for bin_ in range(turned.shape[1]):
+        out[bin_] = forward_dots(columns_of(held, bin_), turned, bin_, core)
+
+
+def near_forward(mine, turned):
+    bins, _, receivers = turned.shape[1:]
     return pl.pallas_call(
         near_forward_kernel,
         out_shape=jax.ShapeDtypeStruct((bins, 2 * FP, receivers), F32),
@@ -244,18 +257,18 @@
         scratch_shapes=[pltpu.VMEM(mine.shape, F32)],
         compiler_params=PARAMS,
         name="near_forward",
-    )(mine, in_vmem(response))
-
-
-def far_forward_kernel(other, near, response, out, held):
+    )(mine, in_vmem(turned))
+
+
+def far_forward_kernel(other, near, turned, out, held):
     held[...] = other[...].astype(F32)
     core = 1 - lax.axis_index("core")
-    for bin_ in range(response.shape[1]):
-        value = forward_dots(columns_of(held, bin_), response, bin_, core)
+    for bin_ in range(turned.shape[1]):
+        value = forward_dots(columns_of(held, bin_), turned, bin_, core)
         share(near[bin_] + value, bin_, out, SHARED)
 
 
-def far_forward(other, near, response):
+def far_forward(other, near, turned):
     return pl.pallas_call(
         far_forward_kernel,
         out_shape=jax.ShapeDtypeStruct((OWNERS * SHARED, LANES), BF16),
@@ -264,7 +277,7 @@
         scratch_shapes=[pltpu.VMEM(other.shape, F32)],
         compiler_params=PARAMS,
         name="far_forward",
-    )(other, near, in_vmem(response))
+    )(other, near, in_vmem(turned))
 
 
 def minus_kernel(stride, rounded, own, onset, blocks, mine, other, *refs):
@@ -486,14 +499,14 @@
     for shift in range(1, pairs):
         perm = [(pair, (pair + shift) % pairs) for pair in range(pairs)]
         shifted.append(lax.ppermute(shifted[0], "pair", perm))
-    held, sent = hold(direct, response)
+    held, turned, sent = hold(direct, response)
     mine = order(shifted, held)
     other = other_core(mine)
     for step in range(ITERS):
         if step == 0:
-            upgoing = far_direct(other, near_direct(mine, held), sent, held)
+            upgoing = far_direct(other, near_direct(mine, turned), sent, turned)
         else:
-            upgoing = far_forward(other, near_forward(mine, held), held)
+            upgoing = far_forward(other, near_forward(mine, turned), turned)
         upgoing = exchange(upgoing, "freq", groups)
         mine, other, *owned = minus_roundtrip(rounded, own_bins, onset, upgoing, step == 0)
         if step == 0:

time: 142 us -> 141 us (level)
  blocking collectives: 97.6 us -> 95.6 us
    all_to_all x6, blocking collectives: 97.6 us -> 95.6 us  [exchange(): return lax.all_to_all(shaped, axes, 0, 0, tiled=True).reshape(blocks.shape)]
  transfers between devices with their start and end apart: 9 -> 9, of which waited for: 4 -> 6; matrix products, arithmetic and copies ran while one was open for 0% -> 0% of each run, Pallas kernels for 6% -> 6%
where the time goes in v7:
time: 141 us; the launch traced here: 139 us
  blocking collectives  95.6 us (68%)
  starting transfers between devices  24.4 us (17%)
  Pallas kernels  14.5 us (10%)
  waiting for transfers between devices  3.25 us (2%)
    all_to_all x6, blocking collectives, exchange(): return lax.all_to_all(shaped, axes, 0, 0, tiled=True).reshape(blocks.shape)  95.6 us
    ppermute x3, starting transfers between devices, on_device(): shifted.append(lax.ppermute(shifted[0], 'pair', perm))  10.1 us
    ppermute x2, starting transfers between devices, on_device(): other_core(far)  7.17 us
    ppermute x2, starting transfers between devices, on_device(): other = other_core(mine)  4.81 us
    pallas_call x1, Pallas kernels, hold(): pl.pallas_call(hold_kernel, out_shape=(pltpu.VMEM(response.shape, respons...  4.71 us
  transfers between devices with their start and end apart: 9, of which 6 were waited for; matrix products, arithmetic and copies ran while one was open for 0% of the time, Pallas kernels for 6%

profile of v7, /device:TPU:1, one launch (start us, length us, event | category | flops | bytes accessed | tf_op | source)
XLA Modules:
  0.0 139.4 jit_solution(9637889973887774965)
XLA Ops:
  0.6 0.8 copy-done.4
  1.5 6.8 %collective-permute-start.2 = (bf16[4,16,256]{2,1,0:T(8,128)(2,1)S(1)}, bf16[4,16,256]{2,1,0:T(8,128)(2,1)S(1)}, u32[]{:S(2)}, u32[]{:S(2)}) collective-permute-start(bf16[4,16,256]{2,1,0:T(8,128)(2,1)S(1)} %prepare.1.refs_0_), channel_id=1, source_target_pairs={{0,6},{2,0},{4,2},{6,4},{1,7},{3,1},{5,3},{7,5},{8,14},{10,8},{12,... | collective-permute-start | bytes 98312 | tf_op jit(solution)/shard_map/ppermute | solution.py:501
  8.3 1.0 collective-permute-start.1
  9.3 2.3 %collective-permute-start = (bf16[4,16,256]{2,1,0:T(8,128)(2,1)S(1)}, bf16[4,16,256]{2,1,0:T(8,128)(2,1)S(1)}, u32[]{:S(2)}, u32[]{:S(2)}) collective-permute-start(bf16[4,16,256]{2,1,0:T(8,128)(2,1)S(1)} %prepare.1.refs_0_), channel_id=1, source_target_pairs={{0,2},{2,4},{4,6},{6,0},{1,3},{3,5},{5,7},{7,1},{8,10},{10,12},{12... | collective-permute-start | bytes 98312 | tf_op jit(solution)/shard_map/ppermute | solution.py:501
  11.6 4.7 %hold.1 = (bf16[2,4,256,2048]{3,2,1,0:T(8,128)(2,1)S(1)}, bf16[2,4,2048,256]{3,2,1,0:T(8,128)(2,1)S(1)}, bf16[512,128]{1,0:T(8,128)(2,1)S(1)}) custom-call(f32[2,4,8,256]{3,2,1,0:T(8,128)} %direct.3, bf16[2,4,256,2048]{3,2,1,0:T(8,128)(2,1)} %response.1), custom_call_target="tpu_custom_call" | custom-call | bytes 16777216 | tf_op jit(solution)/shard_map/hold/pallas_call | solution.py:103
  16.4 1.6 %collective-permute-start.3 = (bf16[4,4,16,256]{3,2,1,0:T(8,128)(2,1)S(1)}, bf16[4,4,16,256]{3,2,1,0:T(8,128)(2,1)S(1)}, u32[]{:S(2)}, u32[]{:S(2)}) collective-permute-start(bf16[4,4,16,256]{3,2,1,0:T(8,128)(2,1)S(1)} %order.1.mine), channel_id=1, source_target_pairs={{0,1},{1,0},{2,3},{3,2},{4,5},{5,4},{6,7},{7,6},{8,9},{9,8},{10,11... | collective-permute-start | bytes 393224 | tf_op jit(solution)/shard_map/ppermute | solution.py:504
  18.9 0.7 far_direct.1
  19.6 18.4 %all_to_all.30 = bf16[32,80,128]{2,1,0:T(8,128)(2,1)S(1)} all-to-all(bf16[32,80,128]{2,1,0:T(8,128)(2,1)S(1)} %bitcast.12), channel_id=1, replica_groups=mesh['freq'=32,'pair'=4,'core'=2] {'freq'}, dimensions={0} | all-to-all | bytes 1310720 | tf_op jit(solution)/shard_map/all_to_all | solution.py:490
  38.1 1.1 minus_roundtrip.2
  39.1 1.3 collective-permute-start.4
  41.2 0.8 collective-permute-done.4.other
  42.4 3.9 %collective-permute-start.5 = (bf16[512,128]{1,0:T(8,128)(2,1)S(1)}, bf16[512,128]{1,0:T(8,128)(2,1)S(1)}, u32[]{:S(2)}, u32[]{:S(2)}) collective-permute-start(bf16[512,128]{1,0:T(8,128)(2,1)S(1)} %far_half.2), channel_id=1, source_target_pairs={{0,1},{1,0},{2,3},{3,2},{4,5},{5,4},{6,7},{7,6},{8,9},{9,8},{10,11... | collective-permute-start | bytes 393224 | tf_op jit(solution)/shard_map/ppermute | solution.py:519
  47.3 19.4 %all_to_all.31 = bf16[128,4,128]{2,1,0:T(4,128)(2,1)S(1)} all-to-all(bf16[128,4,128]{2,1,0:T(4,128)(2,1)S(1)} %bitcast.19), channel_id=1, replica_groups=mesh['freq'=32,'pair'=4,'core'=2] {'pair','freq'}, dimensions={0} | all-to-all | bytes 262144 | tf_op jit(solution)/shard_map/all_to_all | solution.py:490
  67.2 16.8 %all_to_all.32 = bf16[128,4,128]{2,1,0:T(4,128)(2,1)S(1)} all-to-all(bf16[128,4,128]{2,1,0:T(4,128)(2,1)S(1)} %bitcast.22), channel_id=1, replica_groups=mesh['freq'=32,'pair'=4,'core'=2] {'pair','freq'}, dimensions={0} | all-to-all | bytes 262144 | tf_op jit(solution)/shard_map/all_to_all | solution.py:490
  83.9 3.2 %collective-permute-start.6 = (bf16[512,128]{1,0:T(8,128)(2,1)S(1)}, bf16[512,128]{1,0:T(8,128)(2,1)S(1)}, u32[]{:S(2)}, u32[]{:S(2)}) collective-permute-start(bf16[512,128]{1,0:T(8,128)(2,1)S(1)} %bitcast.16), channel_id=1, source_target_pairs={{0,1},{1,0},{2,3},{3,2},{4,5},{5,4},{6,7},{7,6},{8,9},{9,8},{10,11... | collective-permute-start | bytes 393224 | tf_op jit(solution)/shard_map/ppermute | solution.py:526
  88.1 0.7 far_forward.1
  88.8 13.5 %all_to_all.33 = bf16[32,64,128]{2,1,0:T(8,128)(2,1)S(1)} all-to-all(bf16[32,64,128]{2,1,0:T(8,128)(2,1)S(1)} %bitcast.15), channel_id=1, replica_groups=mesh['freq'=32,'pair'=4,'core'=2] {'freq'}, dimensions={0} | all-to-all | bytes 1048576 | tf_op jit(solution)/shard_map/all_to_all | solution.py:490
  102.3 1.0 minus_roundtrip.3
  103.3 0.9 collective-permute-start.7
  104.9 1.2 collective-permute-done.7.other
  106.5 3.3 %collective-permute-start.8 = (bf16[512,128]{1,0:T(8,128)(2,1)S(1)}, bf16[512,128]{1,0:T(8,128)(2,1)S(1)}, u32[]{:S(2)}, u32[]{:S(2)}) collective-permute-start(bf16[512,128]{1,0:T(8,128)(2,1)S(1)} %far_half.3), channel_id=1, source_target_pairs={{0,1},{1,0},{2,3},{3,2},{4,5},{5,4},{6,7},{7,6},{8,9},{9,8},{10,11... | collective-permute-start | bytes 393224 | tf_op jit(solution)/shard_map/ppermute | solution.py:519
  109.8 0.9 near_half.3
  110.8 17.4 %all_to_all.34 = bf16[128,4,128]{2,1,0:T(4,128)(2,1)S(1)} all-to-all(bf16[128,4,128]{2,1,0:T(4,128)(2,1)S(1)} %bitcast.20), channel_id=1, replica_groups=mesh['freq'=32,'pair'=4,'core'=2] {'pair','freq'}, dimensions={0} | all-to-all | bytes 262144 | tf_op jit(solution)/shard_map/all_to_all | solution.py:490
  128.6 10.2 %all_to_all.35 = f32[32,4,128]{2,1,0:T(4,128)S(1)} all-to-all(f32[32,4,128]{2,1,0:T(4,128)S(1)} %bitcast.24), channel_id=1, replica_groups=mesh['freq'=32,'pair'=4,'core'=2] {'freq'}, dimensions={0} | all-to-all | bytes 131072 | tf_op jit(solution)/shard_map/all_to_all | solution.py:490
  (32 shorter events, 6.8 us)
Async XLA Ops:
  0.6 0.8 copy-start.4
  1.5 14.8 %collective-permute-start.2 = (bf16[4,16,256]{2,1,0:T(8,128)(2,1)S(1)}, bf16[4,16,256]{2,1,0:T(8,128)(2,1)S(1)}, u32[]{:S(2)}, u32[]{:S(2)}) collective-permute-start(bf16[4,16,256]{2,1,0:T(8,128)(2,1)S(1)} %prepare.1.refs_0_), channel_id=1, source_target_pairs={{0,6},{2,0},{4,2},{6,4},{1,7},{3,1},{5,3},{7,5},{8,14},{10,8},{12,... | collective-permute-start | bytes 98312 | tf_op jit(solution)/shard_map/ppermute | solution.py:501
  8.3 8.0 %collective-permute-start.1 = (bf16[4,16,256]{2,1,0:T(8,128)(2,1)S(1)}, bf16[4,16,256]{2,1,0:T(8,128)(2,1)S(1)}, u32[]{:S(2)}, u32[]{:S(2)}) collective-permute-start(bf16[4,16,256]{2,1,0:T(8,128)(2,1)S(1)} %prepare.1.refs_0_), channel_id=1, source_target_pairs={{0,4},{2,6},{4,0},{6,2},{1,5},{3,7},{5,1},{7,3},{8,12},{10,14},{12... | collective-permute-start | bytes 98312 | tf_op jit(solution)/shard_map/ppermute | solution.py:501
  9.3 7.0 %collective-permute-start = (bf16[4,16,256]{2,1,0:T(8,128)(2,1)S(1)}, bf16[4,16,256]{2,1,0:T(8,128)(2,1)S(1)}, u32[]{:S(2)}, u32[]{:S(2)}) collective-permute-start(bf16[4,16,256]{2,1,0:T(8,128)(2,1)S(1)} %prepare.1.refs_0_), channel_id=1, source_target_pairs={{0,2},{2,4},{4,6},{6,0},{1,3},{3,5},{5,7},{7,1},{8,10},{10,12},{12... | collective-permute-start | bytes 98312 | tf_op jit(solution)/shard_map/ppermute | solution.py:501
  16.4 2.6 %collective-permute-start.3 = (bf16[4,4,16,256]{3,2,1,0:T(8,128)(2,1)S(1)}, bf16[4,4,16,256]{3,2,1,0:T(8,128)(2,1)S(1)}, u32[]{:S(2)}, u32[]{:S(2)}) collective-permute-start(bf16[4,4,16,256]{3,2,1,0:T(8,128)(2,1)S(1)} %order.1.mine), channel_id=1, source_target_pairs={{0,1},{1,0},{2,3},{3,2},{4,5},{5,4},{6,7},{7,6},{8,9},{9,8},{10,11... | collective-permute-start | bytes 393224 | tf_op jit(solution)/shard_map/ppermute | solution.py:504
  18.0 20.1 %copy-start = (bf16[32,2,16,448]{3,2,1,0:T(8,128)(2,1)S(1)}, bf16[32,2,16,448]{3,2,1,0:T(8,128)(2,1)}, u32[]{:S(2)}) copy-start(bf16[32,2,16,448]{3,2,1,0:T(8,128)(2,1)} %constant.9.clone.own) | copy-start | bytes 2752516
  18.0 20.1 %copy-start.3 = (bf16[2,224,256]{2,1,0:T(8,128)(2,1)S(1)}, bf16[2,224,256]{2,1,0:T(8,128)(2,1)}, u32[]{:S(2)}) copy-start(bf16[2,224,256]{2,1,0:T(8,128)(2,1)} %constant.8.clone.rounded) | copy-start | bytes 688132
  18.0 20.1 %copy-start.5 = (s32[8,256]{1,0:T(8,128)S(1)}, s32[8,256]{1,0:T(8,128)}, u32[]{:S(2)}) copy-start(s32[8,256]{1,0:T(8,128)} %onset.7) | copy-start | bytes 24580
  39.1 2.8 %collective-permute-start.4 = (f32[64,128]{1,0:T(8,128)S(1)}, f32[64,128]{1,0:T(8,128)S(1)}, u32[]{:S(2)}, u32[]{:S(2)}) collective-permute-start(f32[64,128]{1,0:T(8,128)S(1)} %get-tuple-element.16), channel_id=1, source_target_pairs={{0,128},{8,136},{16,144},{24,152},{32,160},{40,168},{48,176},{56,1... | collective-permute-start | bytes 98312 | tf_op jit(solution)/shard_map/ppermute | solution.py:514
  41.2 25.6 %copy-start.1 = (bf16[2,128,672]{2,1,0:T(8,128)(2,1)S(1)}, bf16[2,128,672]{2,1,0:T(8,128)(2,1)}, u32[]{:S(2)}) copy-start(bf16[2,128,672]{2,1,0:T(8,128)(2,1)} %constant.11.clone.forward) | copy-start | bytes 1032196
  41.2 25.6 %copy-start.2 = (bf16[2,224,384]{2,1,0:T(8,128)(2,1)S(1)}, bf16[2,224,384]{2,1,0:T(8,128)(2,1)}, u32[]{:S(2)}) copy-start(bf16[2,224,384]{2,1,0:T(8,128)(2,1)} %constant.10.clone.inverse) | copy-start | bytes 1032196
  42.4 4.9 %collective-permute-start.5 = (bf16[512,128]{1,0:T(8,128)(2,1)S(1)}, bf16[512,128]{1,0:T(8,128)(2,1)S(1)}, u32[]{:S(2)}, u32[]{:S(2)}) collective-permute-start(bf16[512,128]{1,0:T(8,128)(2,1)S(1)} %far_half.2), channel_id=1, source_target_pairs={{0,1},{1,0},{2,3},{3,2},{4,5},{5,4},{6,7},{7,6},{8,9},{9,8},{10,11... | collective-permute-start | bytes 393224 | tf_op jit(solution)/shard_map/ppermute | solution.py:519
  83.9 4.2 %collective-permute-start.6 = (bf16[512,128]{1,0:T(8,128)(2,1)S(1)}, bf16[512,128]{1,0:T(8,128)(2,1)S(1)}, u32[]{:S(2)}, u32[]{:S(2)}) collective-permute-start(bf16[512,128]{1,0:T(8,128)(2,1)S(1)} %bitcast.16), channel_id=1, source_target_pairs={{0,1},{1,0},{2,3},{3,2},{4,5},{5,4},{6,7},{7,6},{8,9},{9,8},{10,11... | collective-permute-start | bytes 393224 | tf_op jit(solution)/shard_map/ppermute | solution.py:526
  103.3 2.8 %collective-permute-start.7 = (f32[64,128]{1,0:T(8,128)S(1)}, f32[64,128]{1,0:T(8,128)S(1)}, u32[]{:S(2)}, u32[]{:S(2)}) collective-permute-start(f32[64,128]{1,0:T(8,128)S(1)} %get-tuple-element.19), channel_id=1, source_target_pairs={{0,128},{8,136},{16,144},{24,152},{32,160},{40,168},{48,176},{56,1... | collective-permute-start | bytes 98312 | tf_op jit(solution)/shard_map/ppermute | solution.py:514
  106.5 4.3 %collective-permute-start.8 = (bf16[512,128]{1,0:T(8,128)(2,1)S(1)}, bf16[512,128]{1,0:T(8,128)(2,1)S(1)}, u32[]{:S(2)}, u32[]{:S(2)}) collective-permute-start(bf16[512,128]{1,0:T(8,128)(2,1)S(1)} %far_half.3), channel_id=1, source_target_pairs={{0,1},{1,0},{2,3},{3,2},{4,5},{5,4},{6,7},{7,6},{8,9},{9,8},{10,11... | collective-permute-start | bytes 393224 | tf_op jit(solution)/shard_map/ppermute | solution.py:519

commit v8 on v7

--- a/solution.py
+++ b/solution.py
@@ -77,12 +77,16 @@
 
 
 def hold_kernel(direct, response, kept, turned, pieces, near, held, done, near_done):
-    copies = [
-        pltpu.make_async_copy(response.at[part, bin_], kept.at[part, bin_], done.at[part, bin_])
+    blocks = [
+        (part, bin_, slice(half * LANES, (half + 1) * LANES))
         for bin_ in range(response.shape[1])
         for part in range(2)
+        for half in range(2)
     ]
-    ahead = 4
+    copies = [
+        pltpu.make_async_copy(response.at[block], kept.at[block], done.at[step]) for step, block in enumerate(blocks)
+    ]
+    ahead = 6
     fetch = pltpu.make_async_copy(direct, near, near_done)
     copies[0].start()
     fetch.start()
@@ -94,8 +98,8 @@
         copy.wait()
         for later in copies[step + ahead : step + ahead + 1]:
             later.start()
-        part, bin_ = step % 2, step // 2
-        turned[part, bin_] = kept[part, bin_].T
+        part, bin_, rows = blocks[step]
+        turned[part, bin_, :, rows] = kept[part, bin_, rows, :].T
 
 
 def hold(direct, response):
@@ -112,7 +116,7 @@
         scratch_shapes=[
             pltpu.VMEM(direct.shape, F32),
             pltpu.VMEM((OWNERS * PIECES, LANES), F32),
-            pltpu.SemaphoreType.DMA((parts, bins)),
+            pltpu.SemaphoreType.DMA((2 * parts * bins,)),
             pltpu.SemaphoreType.DMA,
         ],
         compiler_params=PARAMS,
@@ -495,10 +499,10 @@
     rounded, own_bins, inverse, forward = (jnp.asarray(table) for table in tables())
     other_core = functools.partial(lax.ppermute, axis_name="core", perm=[(0, 1), (1, 0)])
     partners = [(owner, owner ^ (OWNERS // 2)) for owner in range(OWNERS)]
-    shifted = [prepare(direct)]
-    for shift in range(1, pairs):
+    shifted = [prepare(direct)] * pairs
+    for shift in (2, 3, 1):
         perm = [(pair, (pair + shift) % pairs) for pair in range(pairs)]
-        shifted.append(lax.ppermute(shifted[0], "pair", perm))
+        shifted[shift] = lax.ppermute(shifted[0], "pair", perm)
     held, turned, sent = hold(direct, response)
     mine = order(shifted, held)
     other = other_core(mine)

time: 141 us -> 141 us (level)
  no operation moved by 1% of the time
where the time goes in v8:
time: 141 us; the launch traced here: 139 us
  blocking collectives  95.3 us (68%)
  starting transfers between devices  24.4 us (17%)
  Pallas kernels  14.8 us (10%)
  waiting for transfers between devices  3.25 us (2%)
    all_to_all x6, blocking collectives, exchange(): return lax.all_to_all(shaped, axes, 0, 0, tiled=True).reshape(blocks.shape)  95.3 us
    ppermute x3, starting transfers between devices, on_device(): shifted[shift] = lax.ppermute(shifted[0], 'pair', perm)  10.1 us
    ppermute x2, starting transfers between devices, on_device(): other_core(far)  7.17 us
    pallas_call x1, Pallas kernels, hold(): pl.pallas_call(hold_kernel, out_shape=(pltpu.VMEM(response.shape, respons...  5.02 us
    ppermute x2, starting transfers between devices, on_device(): other = other_core(mine)  4.81 us
  transfers between devices with their start and end apart: 9, of which 6 were waited for; matrix products, arithmetic and copies ran while one was open for 0% of the time, Pallas kernels for 6%

profile of v8, /device:TPU:1, one launch (start us, length us, event | category | flops | bytes accessed | tf_op | source)
XLA Modules:
  0.0 139.4 jit_solution(11060779880415306569)
XLA Ops:
  0.6 0.8 copy-done.4
  1.5 6.8 %collective-permute-start.2 = (bf16[4,16,256]{2,1,0:T(8,128)(2,1)S(1)}, bf16[4,16,256]{2,1,0:T(8,128)(2,1)S(1)}, u32[]{:S(2)}, u32[]{:S(2)}) collective-permute-start(bf16[4,16,256]{2,1,0:T(8,128)(2,1)S(1)} %prepare.1.refs_0_), channel_id=1, source_target_pairs={{0,6},{2,0},{4,2},{6,4},{1,7},{3,1},{5,3},{7,5},{8,14},{10,8},{12,... | collective-permute-start | bytes 98312 | tf_op jit(solution)/shard_map/ppermute | solution.py:505
  8.3 1.0 collective-permute-start.1
  9.3 2.3 %collective-permute-start = (bf16[4,16,256]{2,1,0:T(8,128)(2,1)S(1)}, bf16[4,16,256]{2,1,0:T(8,128)(2,1)S(1)}, u32[]{:S(2)}, u32[]{:S(2)}) collective-permute-start(bf16[4,16,256]{2,1,0:T(8,128)(2,1)S(1)} %prepare.1.refs_0_), channel_id=1, source_target_pairs={{0,2},{2,4},{4,6},{6,0},{1,3},{3,5},{5,7},{7,1},{8,10},{10,12},{12... | collective-permute-start | bytes 98312 | tf_op jit(solution)/shard_map/ppermute | solution.py:505
  11.6 5.0 %hold.1 = (bf16[2,4,256,2048]{3,2,1,0:T(8,128)(2,1)S(1)}, bf16[2,4,2048,256]{3,2,1,0:T(8,128)(2,1)S(1)}, bf16[512,128]{1,0:T(8,128)(2,1)S(1)}) custom-call(f32[2,4,8,256]{3,2,1,0:T(8,128)} %direct.3, bf16[2,4,256,2048]{3,2,1,0:T(8,128)(2,1)} %response.1), custom_call_target="tpu_custom_call" | custom-call | bytes 16777216 | tf_op jit(solution)/shard_map/hold/pallas_call | solution.py:107
  16.7 1.6 %collective-permute-start.3 = (bf16[4,4,16,256]{3,2,1,0:T(8,128)(2,1)S(1)}, bf16[4,4,16,256]{3,2,1,0:T(8,128)(2,1)S(1)}, u32[]{:S(2)}, u32[]{:S(2)}) collective-permute-start(bf16[4,4,16,256]{3,2,1,0:T(8,128)(2,1)S(1)} %order.1.mine), channel_id=1, source_target_pairs={{0,1},{1,0},{2,3},{3,2},{4,5},{5,4},{6,7},{7,6},{8,9},{9,8},{10,11... | collective-permute-start | bytes 393224 | tf_op jit(solution)/shard_map/ppermute | solution.py:508
  19.3 0.7 far_direct.1
  19.9 18.4 %all_to_all.30 = bf16[32,80,128]{2,1,0:T(8,128)(2,1)S(1)} all-to-all(bf16[32,80,128]{2,1,0:T(8,128)(2,1)S(1)} %bitcast.12), channel_id=1, replica_groups=mesh['freq'=32,'pair'=4,'core'=2] {'freq'}, dimensions={0} | all-to-all | bytes 1310720 | tf_op jit(solution)/shard_map/all_to_all | solution.py:494
  38.4 1.1 minus_roundtrip.2
  39.4 1.3 collective-permute-start.4
  41.5 0.8 collective-permute-done.4.other
  42.7 3.9 %collective-permute-start.5 = (bf16[512,128]{1,0:T(8,128)(2,1)S(1)}, bf16[512,128]{1,0:T(8,128)(2,1)S(1)}, u32[]{:S(2)}, u32[]{:S(2)}) collective-permute-start(bf16[512,128]{1,0:T(8,128)(2,1)S(1)} %far_half.2), channel_id=1, source_target_pairs={{0,1},{1,0},{2,3},{3,2},{4,5},{5,4},{6,7},{7,6},{8,9},{9,8},{10,11... | collective-permute-start | bytes 393224 | tf_op jit(solution)/shard_map/ppermute | solution.py:523
  47.6 19.1 %all_to_all.31 = bf16[128,4,128]{2,1,0:T(4,128)(2,1)S(1)} all-to-all(bf16[128,4,128]{2,1,0:T(4,128)(2,1)S(1)} %bitcast.19), channel_id=1, replica_groups=mesh['freq'=32,'pair'=4,'core'=2] {'pair','freq'}, dimensions={0} | all-to-all | bytes 262144 | tf_op jit(solution)/shard_map/all_to_all | solution.py:494
  67.2 16.8 %all_to_all.32 = bf16[128,4,128]{2,1,0:T(4,128)(2,1)S(1)} all-to-all(bf16[128,4,128]{2,1,0:T(4,128)(2,1)S(1)} %bitcast.22), channel_id=1, replica_groups=mesh['freq'=32,'pair'=4,'core'=2] {'pair','freq'}, dimensions={0} | all-to-all | bytes 262144 | tf_op jit(solution)/shard_map/all_to_all | solution.py:494
  83.9 3.2 %collective-permute-start.6 = (bf16[512,128]{1,0:T(8,128)(2,1)S(1)}, bf16[512,128]{1,0:T(8,128)(2,1)S(1)}, u32[]{:S(2)}, u32[]{:S(2)}) collective-permute-start(bf16[512,128]{1,0:T(8,128)(2,1)S(1)} %bitcast.16), channel_id=1, source_target_pairs={{0,1},{1,0},{2,3},{3,2},{4,5},{5,4},{6,7},{7,6},{8,9},{9,8},{10,11... | collective-permute-start | bytes 393224 | tf_op jit(solution)/shard_map/ppermute | solution.py:530
  88.1 0.7 far_forward.1
  88.8 13.5 %all_to_all.33 = bf16[32,64,128]{2,1,0:T(8,128)(2,1)S(1)} all-to-all(bf16[32,64,128]{2,1,0:T(8,128)(2,1)S(1)} %bitcast.15), channel_id=1, replica_groups=mesh['freq'=32,'pair'=4,'core'=2] {'freq'}, dimensions={0} | all-to-all | bytes 1048576 | tf_op jit(solution)/shard_map/all_to_all | solution.py:494
  102.3 1.0 minus_roundtrip.3
  103.3 0.9 collective-permute-start.7
  104.9 1.2 collective-permute-done.7.other
  106.5 3.3 %collective-permute-start.8 = (bf16[512,128]{1,0:T(8,128)(2,1)S(1)}, bf16[512,128]{1,0:T(8,128)(2,1)S(1)}, u32[]{:S(2)}, u32[]{:S(2)}) collective-permute-start(bf16[512,128]{1,0:T(8,128)(2,1)S(1)} %far_half.3), channel_id=1, source_target_pairs={{0,1},{1,0},{2,3},{3,2},{4,5},{5,4},{6,7},{7,6},{8,9},{9,8},{10,11... | collective-permute-start | bytes 393224 | tf_op jit(solution)/shard_map/ppermute | solution.py:523
  109.8 0.9 near_half.3
  110.8 17.4 %all_to_all.34 = bf16[128,4,128]{2,1,0:T(4,128)(2,1)S(1)} all-to-all(bf16[128,4,128]{2,1,0:T(4,128)(2,1)S(1)} %bitcast.20), channel_id=1, replica_groups=mesh['freq'=32,'pair'=4,'core'=2] {'pair','freq'}, dimensions={0} | all-to-all | bytes 262144 | tf_op jit(solution)/shard_map/all_to_all | solution.py:494
  128.6 10.2 %all_to_all.35 = f32[32,4,128]{2,1,0:T(4,128)S(1)} all-to-all(f32[32,4,128]{2,1,0:T(4,128)S(1)} %bitcast.24), channel_id=1, replica_groups=mesh['freq'=32,'pair'=4,'core'=2] {'freq'}, dimensions={0} | all-to-all | bytes 131072 | tf_op jit(solution)/shard_map/all_to_all | solution.py:494
  (32 shorter events, 6.8 us)
Async XLA Ops:
  0.6 0.8 copy-start.4
  1.5 15.1 %collective-permute-start.2 = (bf16[4,16,256]{2,1,0:T(8,128)(2,1)S(1)}, bf16[4,16,256]{2,1,0:T(8,128)(2,1)S(1)}, u32[]{:S(2)}, u32[]{:S(2)}) collective-permute-start(bf16[4,16,256]{2,1,0:T(8,128)(2,1)S(1)} %prepare.1.refs_0_), channel_id=1, source_target_pairs={{0,6},{2,0},{4,2},{6,4},{1,7},{3,1},{5,3},{7,5},{8,14},{10,8},{12,... | collective-permute-start | bytes 98312 | tf_op jit(solution)/shard_map/ppermute | solution.py:505
  8.3 8.3 %collective-permute-start.1 = (bf16[4,16,256]{2,1,0:T(8,128)(2,1)S(1)}, bf16[4,16,256]{2,1,0:T(8,128)(2,1)S(1)}, u32[]{:S(2)}, u32[]{:S(2)}) collective-permute-start(bf16[4,16,256]{2,1,0:T(8,128)(2,1)S(1)} %prepare.1.refs_0_), channel_id=1, source_target_pairs={{0,4},{2,6},{4,0},{6,2},{1,5},{3,7},{5,1},{7,3},{8,12},{10,14},{12... | collective-permute-start | bytes 98312 | tf_op jit(solution)/shard_map/ppermute | solution.py:505
  9.3 7.3 %collective-permute-start = (bf16[4,16,256]{2,1,0:T(8,128)(2,1)S(1)}, bf16[4,16,256]{2,1,0:T(8,128)(2,1)S(1)}, u32[]{:S(2)}, u32[]{:S(2)}) collective-permute-start(bf16[4,16,256]{2,1,0:T(8,128)(2,1)S(1)} %prepare.1.refs_0_), channel_id=1, source_target_pairs={{0,2},{2,4},{4,6},{6,0},{1,3},{3,5},{5,7},{7,1},{8,10},{10,12},{12... | collective-permute-start | bytes 98312 | tf_op jit(solution)/shard_map/ppermute | solution.py:505
  16.7 2.6 %collective-permute-start.3 = (bf16[4,4,16,256]{3,2,1,0:T(8,128)(2,1)S(1)}, bf16[4,4,16,256]{3,2,1,0:T(8,128)(2,1)S(1)}, u32[]{:S(2)}, u32[]{:S(2)}) collective-permute-start(bf16[4,4,16,256]{3,2,1,0:T(8,128)(2,1)S(1)} %order.1.mine), channel_id=1, source_target_pairs={{0,1},{1,0},{2,3},{3,2},{4,5},{5,4},{6,7},{7,6},{8,9},{9,8},{10,11... | collective-permute-start | bytes 393224 | tf_op jit(solution)/shard_map/ppermute | solution.py:508
  18.3 20.1 %copy-start = (bf16[32,2,16,448]{3,2,1,0:T(8,128)(2,1)S(1)}, bf16[32,2,16,448]{3,2,1,0:T(8,128)(2,1)}, u32[]{:S(2)}) copy-start(bf16[32,2,16,448]{3,2,1,0:T(8,128)(2,1)} %constant.9.clone.own) | copy-start | bytes 2752516
  18.3 20.1 %copy-start.3 = (bf16[2,224,256]{2,1,0:T(8,128)(2,1)S(1)}, bf16[2,224,256]{2,1,0:T(8,128)(2,1)}, u32[]{:S(2)}) copy-start(bf16[2,224,256]{2,1,0:T(8,128)(2,1)} %constant.8.clone.rounded) | copy-start | bytes 688132
  18.3 20.1 %copy-start.5 = (s32[8,256]{1,0:T(8,128)S(1)}, s32[8,256]{1,0:T(8,128)}, u32[]{:S(2)}) copy-start(s32[8,256]{1,0:T(8,128)} %onset.7) | copy-start | bytes 24580
  39.4 2.8 %collective-permute-start.4 = (f32[64,128]{1,0:T(8,128)S(1)}, f32[64,128]{1,0:T(8,128)S(1)}, u32[]{:S(2)}, u32[]{:S(2)}) collective-permute-start(f32[64,128]{1,0:T(8,128)S(1)} %get-tuple-element.16), channel_id=1, source_target_pairs={{0,128},{8,136},{16,144},{24,152},{32,160},{40,168},{48,176},{56,1... | collective-permute-start | bytes 98312 | tf_op jit(solution)/shard_map/ppermute | solution.py:518
  41.5 25.3 %copy-start.1 = (bf16[2,128,672]{2,1,0:T(8,128)(2,1)S(1)}, bf16[2,128,672]{2,1,0:T(8,128)(2,1)}, u32[]{:S(2)}) copy-start(bf16[2,128,672]{2,1,0:T(8,128)(2,1)} %constant.11.clone.forward) | copy-start | bytes 1032196
  41.5 25.2 %copy-start.2 = (bf16[2,224,384]{2,1,0:T(8,128)(2,1)S(1)}, bf16[2,224,384]{2,1,0:T(8,128)(2,1)}, u32[]{:S(2)}) copy-start(bf16[2,224,384]{2,1,0:T(8,128)(2,1)} %constant.10.clone.inverse) | copy-start | bytes 1032196
  42.7 4.9 %collective-permute-start.5 = (bf16[512,128]{1,0:T(8,128)(2,1)S(1)}, bf16[512,128]{1,0:T(8,128)(2,1)S(1)}, u32[]{:S(2)}, u32[]{:S(2)}) collective-permute-start(bf16[512,128]{1,0:T(8,128)(2,1)S(1)} %far_half.2), channel_id=1, source_target_pairs={{0,1},{1,0},{2,3},{3,2},{4,5},{5,4},{6,7},{7,6},{8,9},{9,8},{10,11... | collective-permute-start | bytes 393224 | tf_op jit(solution)/shard_map/ppermute | solution.py:523
  83.9 4.2 %collective-permute-start.6 = (bf16[512,128]{1,0:T(8,128)(2,1)S(1)}, bf16[512,128]{1,0:T(8,128)(2,1)S(1)}, u32[]{:S(2)}, u32[]{:S(2)}) collective-permute-start(bf16[512,128]{1,0:T(8,128)(2,1)S(1)} %bitcast.16), channel_id=1, source_target_pairs={{0,1},{1,0},{2,3},{3,2},{4,5},{5,4},{6,7},{7,6},{8,9},{9,8},{10,11... | collective-permute-start | bytes 393224 | tf_op jit(solution)/shard_map/ppermute | solution.py:530
  103.3 2.8 %collective-permute-start.7 = (f32[64,128]{1,0:T(8,128)S(1)}, f32[64,128]{1,0:T(8,128)S(1)}, u32[]{:S(2)}, u32[]{:S(2)}) collective-permute-start(f32[64,128]{1,0:T(8,128)S(1)} %get-tuple-element.19), channel_id=1, source_target_pairs={{0,128},{8,136},{16,144},{24,152},{32,160},{40,168},{48,176},{56,1... | collective-permute-start | bytes 98312 | tf_op jit(solution)/shard_map/ppermute | solution.py:518
  106.5 4.3 %collective-permute-start.8 = (bf16[512,128]{1,0:T(8,128)(2,1)S(1)}, bf16[512,128]{1,0:T(8,128)(2,1)S(1)}, u32[]{:S(2)}, u32[]{:S(2)}) collective-permute-start(bf16[512,128]{1,0:T(8,128)(2,1)S(1)} %far_half.3), channel_id=1, source_target_pairs={{0,1},{1,0},{2,3},{3,2},{4,5},{5,4},{6,7},{7,6},{8,9},{9,8},{10,11... | collective-permute-start | bytes 393224 | tf_op jit(solution)/shard_map/ppermute | solution.py:523
